TPU v7x, 512 devices: a whole 4x4x16 slice. The times are simulated.
512 devices in a mesh: neuron: 16 (over z), tm: 32 (over y, x, core).
Axes of the slice: x: 4, y: 4, z: 16, core: 2. Of those that a mesh axis runs over, the one named last changes fastest.
Arguments:
- spikes: int32 [65536, 8192], P('neuron', 'tm'), may hold values from 0 to 7
- read_weight: bfloat16 [65536, 256], P('neuron')
- in_proj: bfloat16 [256, 2048], P(None, 'neuron'), may hold values from -0.375 to 0.375
- decay_rate: float32 [2048], P('neuron'), may hold values from 1.2207031e-05 to 0.0333333333
- gate: float32 [8192], P('tm'), may hold values from 0.65 to 1
- out_fwd: bfloat16 [2048, 256], P('neuron'), may hold values from -0.125 to 0.125
- out_bwd: bfloat16 [2048, 256], P('neuron'), may hold values from -0.125 to 0.125
Outputs:
- latent: bfloat16 [8192, 256], P('tm')
- nll: float32 [65536], P('neuron')
All inputs are finite; a program needn't handle non-finite values.
Results may differ from a plain program's by a relative error of at most 0.011.
Values may be sent and summed in bfloat16 or wider, within the bound.
No kernel may reach another device: no remote copies, remote signals or barrier semaphores. Data moves between devices by JAX's collectives and lax.ppermute only.
A program may use at most 64 MiB of HBM per device.

v0:
```python
import jax
import jax.numpy as jnp
from jax import lax
from jax.sharding import PartitionSpec as P


def prefix(part, axis, combine, identity, reverse):
    count = lax.axis_size(axis)
    place = lax.axis_index(axis)
    ahead = count - 1 - place if reverse else place
    gathered = jax.tree.map(lambda a: lax.all_gather(a, axis), part)
    state = jax.tree.map(lambda a, e: jnp.zeros_like(a) + jnp.asarray(e, a.dtype), part, identity)

    def one(turn, state):
        source = count - 1 - turn if reverse else turn
        return combine(
            state, jax.tree.map(lambda a: lax.dynamic_index_in_dim(a, source, 0, False), gathered)
        )

    return lax.fori_loop(0, ahead, one, state)


def combine(earlier, later):
    return (earlier[0] * later[0], later[0] * earlier[1] + later[1])


def rms_round(rows):
    power = jnp.mean(rows * rows, axis=-1, keepdims=True) + 1e-05
    return (rows * lax.rsqrt(power)).astype(jnp.bfloat16)


def body(spikes, read_weight, in_proj, decay_rate, gate, out_fwd, out_bwd):
    counts = spikes.astype(jnp.bfloat16)
    partial_sum = lax.dot_general(
        counts, read_weight, (((0,), (0,)), ((), ())), preferred_element_type=jnp.float32
    )
    readin = lax.psum(partial_sum, "neuron")
    normed = rms_round(readin)
    scale_in = jnp.sqrt(-jnp.expm1(-2.0 * decay_rate))
    drive = jnp.dot(normed, in_proj, preferred_element_type=jnp.float32) * scale_in[None, :]
    step = jnp.exp(-decay_rate)[None, :] * gate[:, None]
    cum_fwd, state_fwd = lax.associative_scan(combine, (step, drive), axis=0)
    flipped = lax.associative_scan(combine, (jnp.flip(step, 0), jnp.flip(drive, 0)), axis=0)
    cum_bwd = jnp.flip(flipped[0], 0)
    state_bwd = jnp.flip(flipped[1], 0)
    block_decay = cum_fwd[-1]
    ones = jnp.ones_like(block_decay)
    zeros = jnp.zeros_like(block_decay)
    enter_fwd = prefix((block_decay, state_fwd[-1]), "tm", combine, (ones, zeros), False)[1]
    enter_bwd = prefix((block_decay, state_bwd[0]), "tm", combine, (ones, zeros), True)[1]
    forward = state_fwd + cum_fwd * enter_fwd[None, :]
    backward = state_bwd + cum_bwd * enter_bwd[None, :]
    mixed_part = jnp.dot(forward.astype(jnp.bfloat16), out_fwd, preferred_element_type=jnp.float32)
    mixed_part = mixed_part + jnp.dot(
        backward.astype(jnp.bfloat16), out_bwd, preferred_element_type=jnp.float32
    )
    mixed = lax.psum(mixed_part, "neuron")
    latent = (normed.astype(jnp.float32) + mixed).astype(jnp.bfloat16)
    log_rate = lax.dot_general(
        read_weight, latent, (((1,), (1,)), ((), ())), preferred_element_type=jnp.float32
    )
    terms = jnp.exp(log_rate) - spikes.astype(jnp.float32) * log_rate
    total = lax.psum(jnp.sum(terms, axis=1), "tm")
    nll = total / (spikes.shape[1] * lax.axis_size("tm"))
    return (latent, nll)


def solution(mesh):
    return jax.shard_map(
        body,
        mesh=mesh,
        in_specs=(
            P("neuron", "tm"),
            P("neuron", None),
            P(None, "neuron"),
            P("neuron"),
            P("tm"),
            P("neuron", None),
            P("neuron", None),
        ),
        out_specs=(P("tm", None), P("neuron")),
        check_vma=False,
    )
```

profile of v0, /device:TPU:1, one launch (start us, length us, event | category | flops | bytes accessed | tf_op | source)
XLA Modules:
  0.0 485.0 jit_solution(6418655048388268585)
XLA Ops:
  7.2 0.0 copy-start
  7.2 0.0 copy-start.7
  7.2 0.0 all-reduce.67.cloned.1.call-start
  7.3 1.5 copy-done
  8.8 3.6 fusion
  12.4 0.0 all-reduce.67.cloned.1.call-update
  12.4 0.0 all-reduce.69.cloned.1.call-start
  12.5 0.1 broadcast_multiply_fusion
  12.8 131.3 %all-reduce.67.cloned.1.call-done = f32[256,256]{1,0:T(8,128)} async-done(((f32[256,256]{1,0:T(8,128)}), f32[256,256]{1,0:T(8,128)}) %all-reduce.67.cloned.1.call-update) | async-done | bytes 262160 | tf_op jit(solution)/shard_map/psum | solution.py:37
  144.1 1.1 multiply_reduce_fusion
  145.2 1.2 convolution_multiply_fusion
  148.8 0.0 copy-start.3
  148.9 0.0 copy-start.4
  150.0 31.2 %all-gather.1 = f32[32,1,128]{2,1,0:T(1,128)S(1)} all-gather(f32[1,1,128]{2,1,0:T(1,128)S(1)} %add_bitcast_fusion.1), channel_id=1, replica_groups=mesh['neuron'=16,'tm'=32] {'tm'}, dimensions={0}, use_global_device_ids=true | all-gather | bytes 16896 | tf_op jit(solution)/shard_map/all_gather | solution.py:11
  181.3 20.2 %all-gather = f32[32,1,128]{2,1,0:T(1,128)S(1)} all-gather(f32[1,1,128]{2,1,0:T(1,128)S(1)} %add_bitcast_fusion.2), channel_id=1, replica_groups=mesh['neuron'=16,'tm'=32] {'tm'}, dimensions={0}, use_global_device_ids=true | all-gather | bytes 16896 | tf_op jit(solution)/shard_map/all_gather | solution.py:11
  201.6 0.1 rev.10
  201.7 0.1 rev.9
  201.8 20.7 %all-gather.2 = f32[32,1,128]{2,1,0:T(1,128)S(1)} all-gather(f32[1,1,128]{2,1,0:T(1,128)S(1)} %add_bitcast_fusion), channel_id=1, replica_groups=mesh['neuron'=16,'tm'=32] {'tm'}, dimensions={0}, use_global_device_ids=true | all-gather | bytes 16896 | tf_op jit(solution)/shard_map/all_gather | solution.py:11
  222.5 1.2 while.27
  223.7 0.0 copy-done.3
  223.7 0.2 fusion.2
  223.9 0.9 convolution_add_fusion
  224.7 0.0 all-reduce.69.cloned.1.call-update
  224.8 5.7 %copy.10 = s32[4096,256]{0,1:T(8,128)} copy(s32[4096,256]{1,0:T(8,128)} %param.11) | data formatting | bytes 8388608 | tf_op args[0]
  230.4 114.6 %all-reduce.69.cloned.1.call-done = f32[256,256]{1,0:T(8,128)} async-done(((f32[256,256]{1,0:T(8,128)}), f32[256,256]{1,0:T(8,128)}) %all-reduce.69.cloned.1.call-update) | async-done | bytes 262160 | tf_op jit(solution)/shard_map/psum | solution.py:57
  345.0 0.0 copy-done.1
  345.0 1.0 add_convert_fusion
  346.1 0.0 copy-start.2
  346.1 3.4 subtract_reduce_fusion
  349.4 128.1 %psum.23 = f32[4096]{0:T(1024)S(1)} all-reduce(f32[4096]{0:T(1024)S(1)} %subtract_reduce_fusion), channel_id=1, replica_groups=mesh['neuron'=16,'tm'=32] {'tm'}, use_global_device_ids=true, to_apply=%region_8.9 | all-reduce | flops 4096 | bytes 32768 | tf_op jit(solution)/shard_map/psum | solution.py:63
  477.5 0.6 broadcast_multiply_fusion.1
  478.1 0.0 copy-done.2
  (292 shorter events, 3.2 us)
Async XLA Ops:
  7.2 1.6 copy-start
  7.2 5.3 %copy-start.7 = (f32[128]{0:T(128)S(1)}, f32[128]{0:T(128)}, u32[]{:S(2)}) copy-start(f32[128]{0:T(128)} %param.14) | copy-start | bytes 1540
  7.2 5.3 %copy-start.6 = (f32[256]{0:T(256)S(1)}, f32[256]{0:T(256)}, u32[]{:S(2)}) copy-start(f32[256]{0:T(256)} %param.15) | copy-start | bytes 3076
  7.2 138.0 %copy-start.5 = (bf16[256,128]{1,0:T(8,128)(2,1)S(1)}, bf16[256,128]{1,0:T(8,128)(2,1)}, u32[]{:S(2)}) copy-start(bf16[256,128]{1,0:T(8,128)(2,1)} %param.13) | copy-start | bytes 196612
  7.2 136.9 %all-reduce.67.cloned.1.call-start = ((), (), s32[]{:S(2)}) async-start(), calls=%async_computation | async-start | bytes 524288 | tf_op jit(solution)/shard_map/psum | solution.py:37
  12.4 332.6 %all-reduce.69.cloned.1.call-start = ((), (), s32[]{:S(2)}) async-start(), calls=%async_computation.1 | async-start | bytes 524288 | tf_op jit(solution)/shard_map/psum | solution.py:57
  148.8 74.9 %copy-start.3 = (bf16[128,256]{1,0:T(8,128)(2,1)S(1)}, bf16[128,256]{1,0:T(8,128)(2,1)}, u32[]{:S(2)}) copy-start(bf16[128,256]{1,0:T(8,128)(2,1)} %param.16) | copy-start | bytes 196612
  148.9 75.0 %copy-start.4 = (bf16[128,256]{1,0:T(8,128)(2,1)S(1)}, bf16[128,256]{1,0:T(8,128)(2,1)}, u32[]{:S(2)}) copy-start(bf16[128,256]{1,0:T(8,128)(2,1)} %param.17) | copy-start | bytes 196612
  224.8 120.3 %copy-start.1 = (f32[256,256]{1,0:T(8,128)S(1)}, f32[256,256]{1,0:T(8,128)}, u32[]{:S(2)}) copy-start(f32[256,256]{1,0:T(8,128)} %all-reduce.67.cloned.1.call-done) | copy-start | bytes 786436
  346.1 132.1 %copy-start.2 = (bf16[256,256]{1,0:T(8,128)(2,1)}, bf16[256,256]{1,0:T(8,128)(2,1)S(1)}, u32[]{:S(2)}) copy-start(bf16[256,256]{1,0:T(8,128)(2,1)S(1)} %add_convert_fusion) | copy-start | bytes 393220
Sparse Core Ops, SparseCore 0:
  12.5 131.5 all-reduce.66
  224.9 120.0 all-reduce.68
where the time goes:
time: 489 us; the launch traced here: 485 us
  waiting for transfers between devices  246 us (50%)
  blocking collectives  200 us (41%)
  between operations  15.5 us (3%)
  local copies, waits for them, and re-layouts  9.21 us (2%)
  matrix products  9.19 us (2%)
    psum x1, waiting for transfers between devices, body(): readin = lax.psum(partial_sum, 'neuron')  131 us
    psum x1, blocking collectives, body(): total = lax.psum(jnp.sum(terms, axis=1), 'tm')  128 us
    psum x1, waiting for transfers between devices, body(): mixed = lax.psum(mixed_part, 'neuron')  115 us
    all_gather x3, blocking collectives, prefix(): gathered = jax.tree.map(lambda a: lax.all_gather(a, axis), part)  72.1 us
  transfers between devices with their start and end apart: 2, of which 2 were waited for; matrix products, arithmetic and copies ran while one was open for 1% of the time, Pallas kernels for 0%

commit v1 on v0

v1 whole, which is shorter than its diff:
```python
import jax
import jax.numpy as jnp
from jax import lax
from jax.sharding import PartitionSpec as P

F32 = jnp.float32
BF16 = jnp.bfloat16
EXACT = lax.Precision.HIGHEST


def sum_rows(part, axis):
    count = lax.axis_size(axis)
    blocks = part.astype(BF16).reshape(count, part.shape[0] // count, part.shape[1])
    mine = lax.all_to_all(blocks, axis, 0, 0)
    return jnp.sum(mine.astype(F32), axis=0)


def body(spikes, read_weight, in_proj, decay_rate, gate, out_fwd, out_bwd):
    bins = spikes.shape[1]
    blocks = lax.axis_size("tm")
    place = lax.axis_index("tm")
    log_gate = jnp.log(gate)
    row = lax.broadcasted_iota(jnp.int32, (bins, bins), 0)
    col = lax.broadcasted_iota(jnp.int32, (bins, bins), 1)
    upto = jnp.sum(jnp.where(col <= row, log_gate[None, :], 0.0), axis=1)
    before = upto - log_gate
    upto_t = jnp.sum(jnp.where(row <= col, log_gate[:, None], 0.0), axis=0)
    before_t = upto_t - log_gate
    mix_fwd = jnp.where(col <= row, jnp.exp(jnp.minimum(upto[:, None] - upto_t[None, :], 0.0)), 0.0)
    mix_bwd = jnp.where(col >= row, jnp.exp(jnp.minimum(before_t[None, :] - before[:, None], 0.0)), 0.0)
    time = (lax.broadcasted_iota(jnp.int32, (bins, 1), 0) - bins // 2).astype(F32)
    grow = jnp.exp(time * decay_rate[None, :])
    shrink = jnp.exp(-time * decay_rate[None, :])
    first = jnp.arange(bins, dtype=jnp.int32).astype(F32)[:, None]
    cum_fwd = jnp.exp(upto[:, None] - (first + 1.0) * decay_rate[None, :])
    cum_bwd = jnp.exp((upto[-1] - before)[:, None] - (bins - first) * decay_rate[None, :])
    scale_in = jnp.sqrt(-jnp.expm1(-2.0 * decay_rate))

    counts = spikes.astype(BF16)
    partial_sum = lax.dot_general(
        counts, read_weight, (((0,), (0,)), ((), ())), preferred_element_type=F32
    )
    rows = sum_rows(partial_sum, "neuron")
    power = jnp.mean(rows * rows, axis=-1, keepdims=True) + 1e-05
    normed_rows = (rows * lax.rsqrt(power)).astype(BF16)
    normed = lax.all_gather(normed_rows, "neuron", tiled=True)

    drive = jnp.dot(normed, in_proj, preferred_element_type=F32) * scale_in[None, :]
    state_fwd = jnp.dot(mix_fwd, drive * grow, precision=EXACT) * shrink
    state_bwd = jnp.dot(mix_bwd, drive * shrink, precision=EXACT) * grow
    sent = jnp.stack([state_fwd[-1], state_bwd[0], jnp.broadcast_to(upto[-1], decay_rate.shape)])
    got = lax.all_gather(sent, "tm")
    loss = got[:, 2, :]
    order = jnp.arange(blocks, dtype=jnp.int32)[:, None]
    earlier = (order >= order.T).astype(F32)
    span = jnp.sum(earlier[:, :, None] * loss[None, :, :], axis=1)
    span_before = span - loss
    at_fwd = jnp.sum(jnp.where(order == place, span_before, 0.0), axis=0)
    at_bwd = jnp.sum(jnp.where(order == place, span, 0.0), axis=0)
    gap_fwd = ((place - 1 - order) * bins).astype(F32) * decay_rate[None, :]
    gap_bwd = ((order - 1 - place) * bins).astype(F32) * decay_rate[None, :]
    weight_fwd = jnp.where(order < place, jnp.exp(jnp.minimum(at_fwd[None, :] - span - gap_fwd, 0.0)), 0.0)
    weight_bwd = jnp.where(order > place, jnp.exp(jnp.minimum(span_before - at_bwd[None, :] - gap_bwd, 0.0)), 0.0)
    enter_fwd = jnp.sum(weight_fwd * got[:, 0, :], axis=0)
    enter_bwd = jnp.sum(weight_bwd * got[:, 1, :], axis=0)
    forward = state_fwd + cum_fwd * enter_fwd[None, :]
    backward = state_bwd + cum_bwd * enter_bwd[None, :]
    mixed_part = jnp.dot(forward.astype(BF16), out_fwd, preferred_element_type=F32)
    mixed_part = mixed_part + jnp.dot(backward.astype(BF16), out_bwd, preferred_element_type=F32)
    mixed_rows = sum_rows(mixed_part, "neuron")
    latent_rows = (normed_rows.astype(F32) + mixed_rows).astype(BF16)
    latent = lax.all_gather(latent_rows, "neuron", tiled=True)

    log_rate = lax.dot_general(
        read_weight, latent, (((1,), (1,)), ((), ())), preferred_element_type=F32
    )
    terms = jnp.exp(log_rate) - spikes.astype(F32) * log_rate
    part = jnp.sum(terms, axis=1).reshape(-1, 128)
    total = jnp.sum(lax.all_gather(part, "tm"), axis=0).reshape(-1)
    nll = total / (bins * blocks)
    return (latent, nll)


def solution(mesh):
    return jax.shard_map(
        body,
        mesh=mesh,
        in_specs=(
            P("neuron", "tm"),
            P("neuron", None),
            P(None, "neuron"),
            P("neuron"),
            P("tm"),
            P("neuron", None),
            P("neuron", None),
        ),
        out_specs=(P("tm", None), P("neuron")),
        check_vma=False,
    )
```

time: 489 us -> 172 us (0.35)
  waiting for transfers between devices: 246 us -> 16.2 us
  blocking collectives: 200 us -> 113 us
  starting transfers between devices: 0.08 us -> 19.8 us
  between operations: 15.5 us -> 0.86 us
    psum x2 -> x0, waiting for transfers between devices: 246 us -> none  [the longest x1 131 us: body(): readin = lax.psum(partial_sum, 'neuron')]
    psum x1 -> x0, blocking collectives: 128 us -> none  [body(): total = lax.psum(jnp.sum(terms, axis=1), 'tm')]
    all_gather x3 -> x4, blocking collectives: 72.1 us -> 113 us  [the longest x1 35.1 us: body(): got = lax.all_gather(sent, 'tm')]
    all_to_all x0 -> x2, starting transfers between devices: none -> 19.8 us  [sum_rows(): mine = lax.all_to_all(blocks, axis, 0, 0)]
    all_to_all x0 -> x2, waiting for transfers between devices: none -> 16.2 us  [sum_rows(): mine = lax.all_to_all(blocks, axis, 0, 0)]
  transfers between devices with their start and end apart: 2 -> 2, of which waited for: 2 -> 2; matrix products, arithmetic and copies ran while one was open for 1% -> 5% of each run, Pallas kernels for 0% -> 0%
where the time goes in v1:
time: 172 us; the launch traced here: 171 us
  blocking collectives  113 us (66%)
  starting transfers between devices  19.8 us (12%)
  waiting for transfers between devices  16.2 us (9%)
  matrix products  9.23 us (5%)
  local copies, waits for them, and re-layouts  9.19 us (5%)
  other arithmetic  2.44 us (1%)
    all_gather x1, blocking collectives, body(): got = lax.all_gather(sent, 'tm')  35.1 us
    all_gather x1, blocking collectives, body(): total = jnp.sum(lax.all_gather(part, 'tm'), axis=0).reshape(-1)  34.1 us
    all_gather x1, blocking collectives, body(): latent = lax.all_gather(latent_rows, 'neuron', tiled=True)  22.4 us
    all_gather x1, blocking collectives, body(): normed = lax.all_gather(normed_rows, 'neuron', tiled=True)  21.7 us
    all_to_all x2, starting transfers between devices, sum_rows(): mine = lax.all_to_all(blocks, axis, 0, 0)  19.8 us
    all_to_all x2, waiting for transfers between devices, sum_rows(): mine = lax.all_to_all(blocks, axis, 0, 0)  16.2 us
    unnamed x14, local copies, waits for them, and re-layouts  7.84 us
    dot_general x1, matrix products, body(): lax.dot_general(counts, read_weight, (((0,), (0,)), ((), ())), preferred_...  3.63 us
  transfers between devices with their start and end apart: 2, of which 2 were waited for; matrix products, arithmetic and copies ran while one was open for 5% of the time, Pallas kernels for 0%

profile of v1, /device:TPU:1, one launch (start us, length us, event | category | flops | bytes accessed | tf_op | source)
XLA Modules:
  0.0 171.1 jit_solution(11776192033542179723)
XLA Ops:
  0.6 0.0 copy-start
  0.7 1.5 copy-done
  2.2 3.6 %fusion.3 = bf16[256,256]{1,0:T(8,128)(2,1)} fusion(bf16[4096,256]{1,0:T(8,128)(2,1)S(1)} %copy-done, s32[4096,256]{1,0:T(8,128)} %param.7), kind=kOutput, calls=%fused_computation.6 | convolution fusion | flops 537985024 | bytes 6422528 | tf_op jit(solution)/shard_map/dot_general | solution.py:40
  5.9 15.7 %all-to-all-start = ((bf16[16,16,256]{2,1,0:T(8,128)(2,1)}), bf16[16,16,256]{2,1,0:T(8,128)(2,1)S(1)}, u32[]{:S(2)}, u32[]{:S(2)}) async-start(bf16[16,16,256]{2,1,0:T(8,128)(2,1)} %bitcast), calls=%async_computation | async-start | bytes 262144 | tf_op jit(solution)/shard_map/all_to_all | solution.py:14
  21.7 0.2 select_reduce_fusion.1
  21.9 0.6 slice.21
  22.5 0.7 pad.2.clone
  23.2 0.7 broadcast_subtract_fusion
  23.9 9.7 %all-to-all-done = bf16[16,16,256]{2,1,0:T(8,128)(2,1)S(1)} async-done(((bf16[16,16,256]{2,1,0:T(8,128)(2,1)}), bf16[16,16,256]{2,1,0:T(8,128)(2,1)S(1)}, u32[]{:S(2)}, u32[]{:S(2)}) %all-to-all-start) | async-done | bytes 131104 | tf_op jit(solution)/shard_map/all_to_all | solution.py:14
  33.6 0.1 multiply_reduce_fusion.3
  33.8 0.1 multiply_convert_fusion
  33.8 21.7 %all_gather.15 = bf16[256,256]{1,0:T(8,128)(2,1)S(1)} all-gather(bf16[16,256]{1,0:T(8,128)(2,1)S(1)} %multiply_convert_fusion), channel_id=1, replica_groups=mesh['neuron'=16,'tm'=32] {'neuron'}, dimensions={0}, use_global_device_ids=true | all-gather | bytes 139264 | tf_op jit(solution)/shard_map/all_gather | solution.py:46
  55.6 0.2 convolution_multiply_fusion.2
  55.8 0.5 convolution_multiply_fusion.1
  56.2 0.5 convolution_multiply_fusion
  56.7 0.1 maximum_bitcast_fusion
  56.8 35.1 %all-gather.1 = f32[32,3,128]{2,1,0:T(4,128)S(1)} all-gather(f32[1,3,128]{2,1,0:T(4,128)S(1)} %maximum_bitcast_fusion), channel_id=2, replica_groups=mesh['neuron'=16,'tm'=32] {'tm'}, dimensions={0}, use_global_device_ids=true | all-gather | bytes 50688 | tf_op jit(solution)/shard_map/all_gather | solution.py:52
  92.0 0.2 multiply_reduce_fusion
  92.2 0.1 select_reduce_fusion.2
  92.3 0.1 multiply_reduce_fusion.1
  92.4 0.1 multiply_reduce_fusion.2
  92.5 0.3 fusion.22
  92.8 0.9 fusion.2
  93.7 4.1 %all-to-all-start.1 = ((bf16[16,16,256]{2,1,0:T(8,128)(2,1)}), bf16[16,16,256]{2,1,0:T(8,128)(2,1)S(1)}, u32[]{:S(2)}, u32[]{:S(2)}) async-start(bf16[16,16,256]{2,1,0:T(8,128)(2,1)} %bitcast.6), calls=%async_computation.1 | async-start | bytes 262144 | tf_op jit(solution)/shard_map/all_to_all | solution.py:14
  97.8 5.6 %copy.18 = s32[4096,256]{0,1:T(8,128)} copy(s32[4096,256]{1,0:T(8,128)} %param.7) | data formatting | bytes 8388608 | tf_op args[0]
  103.4 6.5 %all-to-all-done.1 = bf16[16,16,256]{2,1,0:T(8,128)(2,1)S(1)} async-done(((bf16[16,16,256]{2,1,0:T(8,128)(2,1)}), bf16[16,16,256]{2,1,0:T(8,128)(2,1)S(1)}, u32[]{:S(2)}, u32[]{:S(2)}) %all-to-all-start.1) | async-done | bytes 131104 | tf_op jit(solution)/shard_map/all_to_all | solution.py:14
  110.0 0.1 add_convert_fusion.4
  110.0 22.4 %all_gather.18 = bf16[256,256]{1,0:T(8,128)(2,1)S(1)} all-gather(bf16[16,256]{1,0:T(8,128)(2,1)S(1)} %add_convert_fusion.4), channel_id=1, replica_groups=mesh['neuron'=16,'tm'=32] {'neuron'}, dimensions={0}, use_global_device_ids=true | all-gather | bytes 139264 | tf_op jit(solution)/shard_map/all_gather | solution.py:72
  132.4 3.3 %subtract_reduce_fusion = f32[4096]{0:T(1024)S(1)} fusion(s32[4096,256]{0,1:T(8,128)} %copy.18, bf16[256,256]{1,0:T(8,128)(2,1)S(1)} %all_gather.18, bf16[4096,256]{1,0:T(8,128)(2,1)S(1)} %copy-done), kind=kOutput, calls=%fused_computation.1 | convolution fusion | flops 541061120 | bytes 6438912 | tf_op jit(solution)/shard_map/dot_general | solution.py:74
  135.7 34.1 %all_gather.19 = f32[32,32,128]{2,1,0:T(8,128)S(1)} all-gather(f32[1,32,128]{2,1,0:T(8,128)S(1)} %bitcast.30), channel_id=1, replica_groups=mesh['neuron'=16,'tm'=32] {'tm'}, dimensions={0}, use_global_device_ids=true | all-gather | bytes 540672 | tf_op jit(solution)/shard_map/all_gather | solution.py:79
  169.8 0.6 multiply_bitcast_fusion
  170.5 0.7 copy.23
  (27 shorter events, 0.2 us)
Async XLA Ops:
  0.6 1.6 copy-start
  0.6 21.1 %copy-start.5 = (f32[256]{0:T(256)S(1)}, f32[256]{0:T(256)}, u32[]{:S(2)}) copy-start(f32[256]{0:T(256)} %param.11) | copy-start | bytes 3076
  0.7 22.6 %copy-start.4 = (f32[128]{0:T(128)S(1)}, f32[128]{0:T(128)}, u32[]{:S(2)}) copy-start(f32[128]{0:T(128)} %param.10) | copy-start | bytes 1540
  0.7 54.9 %copy-start.1 = (bf16[256,128]{1,0:T(8,128)(2,1)S(1)}, bf16[256,128]{1,0:T(8,128)(2,1)}, u32[]{:S(2)}) copy-start(bf16[256,128]{1,0:T(8,128)(2,1)} %param.9) | copy-start | bytes 196612
  0.7 91.8 %copy-start.2 = (bf16[128,256]{1,0:T(8,128)(2,1)S(1)}, bf16[128,256]{1,0:T(8,128)(2,1)}, u32[]{:S(2)}) copy-start(bf16[128,256]{1,0:T(8,128)(2,1)} %param.12) | copy-start | bytes 196612
  2.2 90.5 %copy-start.3 = (bf16[128,256]{1,0:T(8,128)(2,1)S(1)}, bf16[128,256]{1,0:T(8,128)(2,1)}, u32[]{:S(2)}) copy-start(bf16[128,256]{1,0:T(8,128)(2,1)} %param.13) | copy-start | bytes 196612
  5.9 27.7 %all-to-all-start = ((bf16[16,16,256]{2,1,0:T(8,128)(2,1)}), bf16[16,16,256]{2,1,0:T(8,128)(2,1)S(1)}, u32[]{:S(2)}, u32[]{:S(2)}) async-start(bf16[16,16,256]{2,1,0:T(8,128)(2,1)} %bitcast), calls=%async_computation | async-start | bytes 262144 | tf_op jit(solution)/shard_map/all_to_all | solution.py:14
  93.7 16.2 %all-to-all-start.1 = ((bf16[16,16,256]{2,1,0:T(8,128)(2,1)}), bf16[16,16,256]{2,1,0:T(8,128)(2,1)S(1)}, u32[]{:S(2)}, u32[]{:S(2)}) async-start(bf16[16,16,256]{2,1,0:T(8,128)(2,1)} %bitcast.6), calls=%async_computation.1 | async-start | bytes 262144 | tf_op jit(solution)/shard_map/all_to_all | solution.py:14

commit v2 on v1

--- a/solution.py
+++ b/solution.py
@@ -13,6 +13,12 @@
     blocks = part.astype(BF16).reshape(count, part.shape[0] // count, part.shape[1])
     mine = lax.all_to_all(blocks, axis, 0, 0)
     return jnp.sum(mine.astype(F32), axis=0)
+
+
+def spread(part, axis):
+    count = lax.axis_size(axis)
+    copies = jnp.broadcast_to(part[None], (count,) + part.shape)
+    return lax.all_to_all(copies, axis, 0, 0)
 
 
 def body(spikes, read_weight, in_proj, decay_rate, gate, out_fwd, out_bwd):
@@ -43,13 +49,13 @@
     rows = sum_rows(partial_sum, "neuron")
     power = jnp.mean(rows * rows, axis=-1, keepdims=True) + 1e-05
     normed_rows = (rows * lax.rsqrt(power)).astype(BF16)
-    normed = lax.all_gather(normed_rows, "neuron", tiled=True)
+    normed = spread(normed_rows, "neuron").reshape(bins, -1)
 
     drive = jnp.dot(normed, in_proj, preferred_element_type=F32) * scale_in[None, :]
     state_fwd = jnp.dot(mix_fwd, drive * grow, precision=EXACT) * shrink
     state_bwd = jnp.dot(mix_bwd, drive * shrink, precision=EXACT) * grow
     sent = jnp.stack([state_fwd[-1], state_bwd[0], jnp.broadcast_to(upto[-1], decay_rate.shape)])
-    got = lax.all_gather(sent, "tm")
+    got = spread(sent, "tm")
     loss = got[:, 2, :]
     order = jnp.arange(blocks, dtype=jnp.int32)[:, None]
     earlier = (order >= order.T).astype(F32)
@@ -69,14 +75,14 @@
     mixed_part = mixed_part + jnp.dot(backward.astype(BF16), out_bwd, preferred_element_type=F32)
     mixed_rows = sum_rows(mixed_part, "neuron")
     latent_rows = (normed_rows.astype(F32) + mixed_rows).astype(BF16)
-    latent = lax.all_gather(latent_rows, "neuron", tiled=True)
+    latent = spread(latent_rows, "neuron").reshape(bins, -1)
 
     log_rate = lax.dot_general(
         read_weight, latent, (((1,), (1,)), ((), ())), preferred_element_type=F32
     )
     terms = jnp.exp(log_rate) - spikes.astype(F32) * log_rate
     part = jnp.sum(terms, axis=1).reshape(-1, 128)
-    total = jnp.sum(lax.all_gather(part, "tm"), axis=0).reshape(-1)
+    total = jnp.sum(spread(part.astype(BF16), "tm").astype(F32), axis=0).reshape(-1)
     nll = total / (bins * blocks)
     return (latent, nll)
 

time: 172 us -> 129 us (0.75)
  blocking collectives: 113 us -> 31.2 us
  waiting for transfers between devices: 16.2 us -> 35.4 us
  starting transfers between devices: 19.8 us -> 38.8 us
  local copies, waits for them, and re-layouts: 9.19 us -> 11.2 us
    all_gather x4 -> x0, blocking collectives: 113 us -> none  [the longest x1 35.1 us: body(): got = lax.all_gather(sent, 'tm')]
    all_to_all x0 -> x2, blocking collectives: none -> 31.2 us  [the longest x1 15.7 us: spread(): return lax.all_to_all(copies, axis, 0, 0)]
    all_to_all x0 -> x3, waiting for transfers between devices: none -> 23.7 us  [spread(): return lax.all_to_all(copies, axis, 0, 0)]
    all_to_all x0 -> x3, starting transfers between devices: none -> 23.1 us  [spread(): return lax.all_to_all(copies, axis, 0, 0)]
    all_to_all x2 -> x1, waiting for transfers between devices: 16.2 us -> 11.7 us  [sum_rows(): mine = lax.all_to_all(blocks, axis, 0, 0)]
    all_to_all x2 -> x1, starting transfers between devices: 19.8 us -> 15.7 us  [sum_rows(): mine = lax.all_to_all(blocks, axis, 0, 0)]
    broadcast_in_dim x0 -> x4, local copies, waits for them, and re-layouts: none -> 2.02 us  [spread(): copies = jnp.broadcast_to(part[None], (count,) + part.shape)]
  transfers between devices with their start and end apart: 2 -> 4, of which waited for: 2 -> 4; matrix products, arithmetic and copies ran while one was open for 5% -> 6% of each run, Pallas kernels for 0% -> 0%
where the time goes in v2:
time: 129 us
  starting transfers between devices  38.8 us (30%)
  waiting for transfers between devices  35.4 us (27%)
  blocking collectives  31.2 us (24%)
  local copies, waits for them, and re-layouts  11.2 us (9%)
  matrix products  8.58 us (7%)
  other arithmetic  2.44 us (2%)
    all_to_all x3, waiting for transfers between devices, spread(): return lax.all_to_all(copies, axis, 0, 0)  23.7 us
    all_to_all x3, starting transfers between devices, spread(): return lax.all_to_all(copies, axis, 0, 0)  23.1 us
    all_to_all x1, starting transfers between devices, sum_rows(): mine = lax.all_to_all(blocks, axis, 0, 0)  15.7 us
    all_to_all x1, blocking collectives, spread(): return lax.all_to_all(copies, axis, 0, 0)  15.7 us
    all_to_all x1, blocking collectives, sum_rows(): mine = lax.all_to_all(blocks, axis, 0, 0)  15.6 us
    all_to_all x1, waiting for transfers between devices, sum_rows(): mine = lax.all_to_all(blocks, axis, 0, 0)  11.7 us
    unnamed x14, local copies, waits for them, and re-layouts  7.84 us
    dot_general x1, matrix products, body(): lax.dot_general(counts, read_weight, (((0,), (0,)), ((), ())), preferred_...  3.63 us
  transfers between devices with their start and end apart: 4, of which 4 were waited for; matrix products, arithmetic and copies ran while one was open for 6% of the time, Pallas kernels for 0%

profile of v2, /device:TPU:1, one launch (start us, length us, event | category | flops | bytes accessed | tf_op | source)
XLA Modules:
  0.0 128.5 jit_solution(11366003949801165308)
XLA Ops:
  0.7 1.5 %copy-done = bf16[4096,256]{1,0:T(8,128)(2,1)S(1)} copy-done((bf16[4096,256]{1,0:T(8,128)(2,1)S(1)}, bf16[4096,256]{1,0:T(8,128)(2,1)}, u32[]{:S(2)}) %copy-start) | copy-done | bytes 2097176
  2.2 3.6 %fusion.3 = bf16[256,256]{1,0:T(8,128)(2,1)} fusion(bf16[4096,256]{1,0:T(8,128)(2,1)S(1)} %copy-done, s32[4096,256]{1,0:T(8,128)} %param.7), kind=kOutput, calls=%fused_computation.6 | convolution fusion | flops 537985024 | bytes 6422528 | tf_op jit(solution)/shard_map/dot_general | solution.py:46
  5.9 15.7 %all-to-all-start = ((bf16[16,16,256]{2,1,0:T(8,128)(2,1)}), bf16[16,16,256]{2,1,0:T(8,128)(2,1)S(1)}, u32[]{:S(2)}, u32[]{:S(2)}) async-start(bf16[16,16,256]{2,1,0:T(8,128)(2,1)} %bitcast), calls=%async_computation | async-start | bytes 262144 | tf_op jit(solution)/shard_map/all_to_all | solution.py:14
  21.7 0.2 select_reduce_fusion.1
  21.9 11.7 %all-to-all-done = bf16[16,16,256]{2,1,0:T(8,128)(2,1)S(1)} async-done(((bf16[16,16,256]{2,1,0:T(8,128)(2,1)}), bf16[16,16,256]{2,1,0:T(8,128)(2,1)S(1)}, u32[]{:S(2)}, u32[]{:S(2)}) %all-to-all-start) | async-done | bytes 131104 | tf_op jit(solution)/shard_map/all_to_all | solution.py:14
  33.6 0.1 multiply_reduce_fusion.3
  33.8 0.7 broadcast_in_dim.64
  34.5 5.9 %all-to-all-start.1 = ((bf16[16,16,256]{2,1,0:T(8,128)(2,1)}), bf16[16,16,256]{2,1,0:T(8,128)(2,1)S(1)}, u32[]{:S(2)}, u32[]{:S(2)}) async-start(bf16[16,16,256]{2,1,0:T(8,128)(2,1)} %broadcast_in_dim.64), calls=%async_computation.1 | async-start | bytes 262144 | tf_op jit(solution)/shard_map/all_to_all | solution.py:21
  40.5 0.6 slice.21
  41.0 0.7 pad.2.clone
  41.8 0.7 broadcast_subtract_fusion
  42.4 10.0 %all-to-all-done.1 = bf16[16,16,256]{2,1,0:T(8,128)(2,1)S(1)} async-done(((bf16[16,16,256]{2,1,0:T(8,128)(2,1)}), bf16[16,16,256]{2,1,0:T(8,128)(2,1)S(1)}, u32[]{:S(2)}, u32[]{:S(2)}) %all-to-all-start.1) | async-done | bytes 131104 | tf_op jit(solution)/shard_map/all_to_all | solution.py:21
  52.4 0.2 convolution_multiply_fusion.2
  52.6 0.5 convolution_multiply_fusion.1
  53.1 0.5 convolution_multiply_fusion
  53.7 0.6 broadcast_in_dim.106
  54.3 10.7 %all-to-all-start.2 = ((f32[32,3,128]{2,1,0:T(4,128)}), f32[32,3,128]{2,1,0:T(4,128)S(1)}, u32[]{:S(2)}, u32[]{:S(2)}) async-start(f32[32,3,128]{2,1,0:T(4,128)} %broadcast_in_dim.106), calls=%async_computation.2 | async-start | bytes 131072 | tf_op jit(solution)/shard_map/all_to_all | solution.py:21
  65.0 7.3 %all-to-all-done.2 = f32[32,3,128]{2,1,0:T(4,128)S(1)} async-done(((f32[32,3,128]{2,1,0:T(4,128)}), f32[32,3,128]{2,1,0:T(4,128)S(1)}, u32[]{:S(2)}, u32[]{:S(2)}) %all-to-all-start.2) | async-done | bytes 49184 | tf_op jit(solution)/shard_map/all_to_all | solution.py:21
  72.3 0.2 multiply_reduce_fusion
  72.7 0.1 multiply_reduce_fusion.1
  72.8 0.1 multiply_reduce_fusion.2
  72.9 0.3 fusion.22
  73.1 0.3 fusion.2
  73.4 15.6 %all_to_all.30 = bf16[16,16,256]{2,1,0:T(8,128)(2,1)S(1)} all-to-all(bf16[16,16,256]{2,1,0:T(8,128)(2,1)S(1)} %bitcast.33), channel_id=1, replica_groups=mesh['neuron'=16,'tm'=32] {'neuron'}, dimensions={0} | all-to-all | bytes 262144 | tf_op jit(solution)/shard_map/all_to_all | solution.py:14
  89.1 0.7 broadcast_in_dim.109
  89.7 6.5 %all-to-all-start.4 = ((bf16[16,16,256]{2,1,0:T(8,128)(2,1)}), bf16[16,16,256]{2,1,0:T(8,128)(2,1)S(1)}, u32[]{:S(2)}, u32[]{:S(2)}) async-start(bf16[16,16,256]{2,1,0:T(8,128)(2,1)} %broadcast_in_dim.109), calls=%async_computation.4 | async-start | bytes 262144 | tf_op jit(solution)/shard_map/all_to_all | solution.py:21
  96.2 5.6 %copy.16 = s32[4096,256]{0,1:T(8,128)} copy(s32[4096,256]{1,0:T(8,128)} %param.7) | data formatting | bytes 8388608 | tf_op args[0]
  101.8 6.4 %all-to-all-done.4 = bf16[16,16,256]{2,1,0:T(8,128)(2,1)S(1)} async-done(((bf16[16,16,256]{2,1,0:T(8,128)(2,1)}), bf16[16,16,256]{2,1,0:T(8,128)(2,1)S(1)}, u32[]{:S(2)}, u32[]{:S(2)}) %all-to-all-start.4) | async-done | bytes 131104 | tf_op jit(solution)/shard_map/all_to_all | solution.py:21
  108.2 3.3 %subtract_reduce_fusion = bf16[4096]{0:T(1024)(128)(2,1)S(1)} fusion(s32[4096,256]{0,1:T(8,128)} %copy.16, bf16[256,256]{1,0:T(8,128)(2,1)S(1)} %bitcast.30, bf16[4096,256]{1,0:T(8,128)(2,1)S(1)} %copy-done), kind=kOutput, calls=%fused_computation.1 | convolution fusion | flops 541061120 | bytes 6430720 | tf_op jit(solution)/shard_map/dot_general | solution.py:80
  111.6 15.7 %all_to_all.31 = bf16[32,32,128]{2,1,0:T(8,128)(2,1)S(1)} all-to-all(bf16[32,32,128]{2,1,0:T(8,128)(2,1)S(1)} %broadcast_in_dim.110), channel_id=1, replica_groups=mesh['neuron'=16,'tm'=32] {'tm'}, dimensions={0} | all-to-all | bytes 524288 | tf_op jit(solution)/shard_map/all_to_all | solution.py:21
  127.3 0.6 multiply_bitcast_fusion
  127.9 0.7 copy.21
  (33 shorter events, 0.6 us)
Async XLA Ops:
  0.6 1.6 %copy-start = (bf16[4096,256]{1,0:T(8,128)(2,1)S(1)}, bf16[4096,256]{1,0:T(8,128)(2,1)}, u32[]{:S(2)}) copy-start(bf16[4096,256]{1,0:T(8,128)(2,1)} %param.8) | copy-start | bytes 6291460
  0.6 21.0 %copy-start.5 = (f32[256]{0:T(256)S(1)}, f32[256]{0:T(256)}, u32[]{:S(2)}) copy-start(f32[256]{0:T(256)} %param.11) | copy-start | bytes 3076
  0.7 41.1 %copy-start.4 = (f32[128]{0:T(128)S(1)}, f32[128]{0:T(128)}, u32[]{:S(2)}) copy-start(f32[128]{0:T(128)} %param.10) | copy-start | bytes 1540
  0.7 51.8 %copy-start.1 = (bf16[256,128]{1,0:T(8,128)(2,1)S(1)}, bf16[256,128]{1,0:T(8,128)(2,1)}, u32[]{:S(2)}) copy-start(bf16[256,128]{1,0:T(8,128)(2,1)} %param.9) | copy-start | bytes 196612
  0.7 72.2 %copy-start.2 = (bf16[128,256]{1,0:T(8,128)(2,1)S(1)}, bf16[128,256]{1,0:T(8,128)(2,1)}, u32[]{:S(2)}) copy-start(bf16[128,256]{1,0:T(8,128)(2,1)} %param.12) | copy-start | bytes 196612
  2.2 70.9 %copy-start.3 = (bf16[128,256]{1,0:T(8,128)(2,1)S(1)}, bf16[128,256]{1,0:T(8,128)(2,1)}, u32[]{:S(2)}) copy-start(bf16[128,256]{1,0:T(8,128)(2,1)} %param.13) | copy-start | bytes 196612
  5.9 27.7 %all-to-all-start = ((bf16[16,16,256]{2,1,0:T(8,128)(2,1)}), bf16[16,16,256]{2,1,0:T(8,128)(2,1)S(1)}, u32[]{:S(2)}, u32[]{:S(2)}) async-start(bf16[16,16,256]{2,1,0:T(8,128)(2,1)} %bitcast), calls=%async_computation | async-start | bytes 262144 | tf_op jit(solution)/shard_map/all_to_all | solution.py:14
  34.5 17.9 %all-to-all-start.1 = ((bf16[16,16,256]{2,1,0:T(8,128)(2,1)}), bf16[16,16,256]{2,1,0:T(8,128)(2,1)S(1)}, u32[]{:S(2)}, u32[]{:S(2)}) async-start(bf16[16,16,256]{2,1,0:T(8,128)(2,1)} %broadcast_in_dim.64), calls=%async_computation.1 | async-start | bytes 262144 | tf_op jit(solution)/shard_map/all_to_all | solution.py:21
  54.3 18.0 %all-to-all-start.2 = ((f32[32,3,128]{2,1,0:T(4,128)}), f32[32,3,128]{2,1,0:T(4,128)S(1)}, u32[]{:S(2)}, u32[]{:S(2)}) async-start(f32[32,3,128]{2,1,0:T(4,128)} %broadcast_in_dim.106), calls=%async_computation.2 | async-start | bytes 131072 | tf_op jit(solution)/shard_map/all_to_all | solution.py:21
  89.7 18.5 %all-to-all-start.4 = ((bf16[16,16,256]{2,1,0:T(8,128)(2,1)}), bf16[16,16,256]{2,1,0:T(8,128)(2,1)S(1)}, u32[]{:S(2)}, u32[]{:S(2)}) async-start(bf16[16,16,256]{2,1,0:T(8,128)(2,1)} %broadcast_in_dim.109), calls=%async_computation.4 | async-start | bytes 262144 | tf_op jit(solution)/shard_map/all_to_all | solution.py:21

commit v3 on v2

v3 whole, which is shorter than its diff:
```python
import jax
import jax.numpy as jnp
from jax import lax
from jax.experimental import pallas as pl
from jax.experimental.pallas import tpu as pltpu
from jax.sharding import PartitionSpec as P

F32 = jnp.float32
BF16 = jnp.bfloat16
ROWS = (((1,), (1,)), ((), ()))


def spread(part, axis):
    count = lax.axis_size(axis)
    copies = jnp.broadcast_to(part[None], (count,) + part.shape)
    return lax.all_to_all(copies, axis, 0, 0)


def powers(rate, bins, low, sign):
    fine = 16
    coarse = bins // fine
    a = lax.broadcasted_iota(jnp.int32, (coarse, 1), 0) * fine - low
    b = lax.broadcasted_iota(jnp.int32, (fine, 1), 0)
    big = jnp.exp(sign * (a.astype(F32) * rate))
    small = jnp.exp(sign * (b.astype(F32) * rate))
    return (big[:, None, :] * small[None, :, :]).reshape(bins, rate.shape[1])


def mix_kernel(normed, weights, enter, mix_fwd, mix_bwd, lead_fwd, lead_bwd, latent, total):
    turn = pl.program_id(0)
    bins = normed.shape[0]
    modes = weights.shape[1] // 3
    rows = normed[...]

    @pl.when(turn == 0)
    def _():
        total[...] = rows.astype(F32)

    acc = total[...]
    for pair in range(weights.shape[0] // 2):
        two = slice(2 * pair, 2 * pair + 2)

        def line(r):
            return jnp.concatenate([enter[2 * pair, r : r + 1, :], enter[2 * pair + 1, r : r + 1, :]], axis=1)

        rate = line(2)
        grow = powers(rate, bins, bins // 2, 1.0)
        shrink = powers(rate, bins, bins // 2, -1.0)
        proj = weights[two, :modes, :].reshape(2 * modes, -1)
        fwd_out = weights[two, modes : 2 * modes, :].reshape(2 * modes, -1)
        bwd_out = weights[two, 2 * modes :, :].reshape(2 * modes, -1)
        drive = lax.dot_general(rows, proj, ROWS, preferred_element_type=F32) * line(3)
        ahead = jnp.dot(mix_fwd[...], (drive * grow).astype(BF16), preferred_element_type=F32)
        behind = jnp.dot(mix_bwd[...], (drive * shrink).astype(BF16), preferred_element_type=F32)
        ahead = (ahead + lead_fwd[...] * line(0)) * shrink
        behind = (behind + lead_bwd[...] * line(1)) * grow
        acc = acc + jnp.dot(ahead.astype(BF16), fwd_out, preferred_element_type=F32)
        acc = acc + jnp.dot(behind.astype(BF16), bwd_out, preferred_element_type=F32)
    total[...] = acc

    @pl.when(turn == pl.num_programs(0) - 1)
    def _():
        latent[...] = acc.astype(BF16)


def mix_all(normed, weights, enter, mix_fwd, mix_bwd, lead_fwd, lead_bwd):
    bins, channels = normed.shape
    count = weights.shape[0]
    group = 4
    whole = lambda *shape: pl.BlockSpec(shape, lambda i: (0,) * len(shape))
    return pl.pallas_call(
        mix_kernel,
        grid=(count // group,),
        in_specs=[
            whole(bins, channels),
            pl.BlockSpec((group,) + weights.shape[1:], lambda i: (i, 0, 0)),
            pl.BlockSpec((group,) + enter.shape[1:], lambda i: (i, 0, 0)),
            whole(bins, bins),
            whole(bins, bins),
            whole(bins, 1),
            whole(bins, 1),
        ],
        out_specs=whole(bins, channels),
        out_shape=jax.ShapeDtypeStruct((bins, channels), BF16),
        scratch_shapes=[pltpu.VMEM((bins, channels), F32)],
        compiler_params=pltpu.CompilerParams(vmem_limit_bytes=32 * 1024 * 1024),
        name="mix_all",
    )(normed, weights, enter, mix_fwd, mix_bwd, lead_fwd, lead_bwd)


def body(spikes, read_weight, in_proj, decay_rate, gate, out_fwd, out_bwd):
    bins = spikes.shape[1]
    blocks = lax.axis_size("tm")
    place = lax.axis_index("tm")
    weights = lax.all_gather(jnp.concatenate([in_proj.T, out_fwd, out_bwd], axis=0), "neuron")
    log_gate = jnp.log(gate)
    row = lax.broadcasted_iota(jnp.int32, (bins, bins), 0)
    col = lax.broadcasted_iota(jnp.int32, (bins, bins), 1)
    upto = jnp.sum(jnp.where(col <= row, log_gate[None, :], 0.0), axis=1, keepdims=True)
    before = upto - log_gate[:, None]
    upto_t = jnp.sum(jnp.where(row <= col, log_gate[:, None], 0.0), axis=0, keepdims=True)
    before_t = upto_t - log_gate[None, :]
    mix_fwd = jnp.where(col <= row, jnp.exp(jnp.minimum(upto - upto_t, 0.0)), 0.0).astype(BF16)
    mix_bwd = jnp.where(col >= row, jnp.exp(jnp.minimum(before_t - before, 0.0)), 0.0).astype(BF16)
    whole = upto[bins - 1, 0]
    first = lax.broadcasted_iota(jnp.int32, (bins, 1), 0).astype(F32)
    rate = decay_rate[None, :]
    carry_fwd = jnp.exp((whole - upto) - (bins - 1 - first) * rate)
    carry_bwd = jnp.exp(before - first * rate)
    lead_fwd = jnp.exp(upto)
    lead_bwd = jnp.exp(whole - before)
    scale_in = jnp.sqrt(-jnp.expm1(-2.0 * decay_rate))

    counts = spikes.astype(BF16)
    partial_sum = lax.dot_general(
        counts, read_weight, (((0,), (0,)), ((), ())), preferred_element_type=F32
    )
    ring = lax.axis_size("neuron")
    parts = partial_sum.astype(BF16).reshape(ring, bins // ring, -1)
    rows = jnp.sum(lax.all_to_all(parts, "neuron", 0, 0).astype(F32), axis=0)
    power = jnp.mean(rows * rows, axis=-1, keepdims=True) + 1e-05
    normed_rows = (rows * lax.rsqrt(power)).astype(BF16)
    normed = spread(normed_rows, "neuron").reshape(bins, -1)

    drive = jnp.dot(normed, in_proj, preferred_element_type=F32)
    sent = jnp.stack(
        [
            jnp.sum(drive * carry_fwd, axis=0) * scale_in,
            jnp.sum(drive * carry_bwd, axis=0) * scale_in,
            jnp.broadcast_to(whole, decay_rate.shape),
        ]
    )
    got = spread(sent, "tm")
    loss = got[:, 2, :]
    order = jnp.arange(blocks, dtype=jnp.int32)[:, None]
    earlier = (order >= order.T).astype(F32)
    span = jnp.sum(earlier[:, :, None] * loss[None, :, :], axis=1)
    span_before = span - loss
    at_fwd = jnp.sum(jnp.where(order == place, span_before, 0.0), axis=0)
    at_bwd = jnp.sum(jnp.where(order == place, span, 0.0), axis=0)
    gap_fwd = ((place - 1 - order) * bins).astype(F32) * rate
    gap_bwd = ((order - 1 - place) * bins).astype(F32) * rate
    weight_fwd = jnp.where(order < place, jnp.exp(jnp.minimum(at_fwd[None, :] - span - gap_fwd, 0.0)), 0.0)
    weight_bwd = jnp.where(order > place, jnp.exp(jnp.minimum(span_before - at_bwd[None, :] - gap_bwd, 0.0)), 0.0)
    enter_fwd = jnp.sum(weight_fwd * got[:, 0, :], axis=0)
    enter_bwd = jnp.sum(weight_bwd * got[:, 1, :], axis=0)
    half = bins // 2
    enter = jnp.stack(
        [
            enter_fwd * jnp.exp(-(bins - half + 1.0) * decay_rate),
            enter_bwd * jnp.exp(-(bins - half) * decay_rate),
            decay_rate,
            scale_in,
        ]
    )
    latent = mix_all(normed, weights, spread(enter, "neuron"), mix_fwd, mix_bwd, lead_fwd, lead_bwd)

    log_rate = lax.dot_general(
        read_weight, latent, (((1,), (1,)), ((), ())), preferred_element_type=F32
    )
    terms = jnp.exp(log_rate) - spikes.astype(F32) * log_rate
    part = jnp.sum(terms, axis=1).reshape(-1, 128)
    total = jnp.sum(spread(part.astype(BF16), "tm").astype(F32), axis=0).reshape(-1)
    nll = total / (bins * blocks)
    return (latent, nll)


def solution(mesh):
    return jax.shard_map(
        body,
        mesh=mesh,
        in_specs=(
            P("neuron", "tm"),
            P("neuron", None),
            P(None, "neuron"),
            P("neuron"),
            P("tm"),
            P("neuron", None),
            P("neuron", None),
        ),
        out_specs=(P("tm", None), P("neuron")),
        check_vma=False,
    )
```

time: 129 us -> 134 us (1.039)
  between operations: 0.88 us -> 14.3 us
  blocking collectives: 31.2 us -> 18.2 us
  Pallas kernels: 0 us -> 4.59 us
  other arithmetic: 2.44 us -> 4.15 us
  matrix products: 8.58 us -> 7.23 us
    all_to_all x1 -> x0, blocking collectives: 15.6 us -> none  [sum_rows(): mine = lax.all_to_all(blocks, axis, 0, 0)]
    pallas_call x0 -> x1, Pallas kernels: none -> 4.59 us  [mix_all(): pl.pallas_call(mix_kernel, grid=(count // group,), in_specs=[whole(bins,...]
    all_to_all x1, blocking collectives: 15.7 us -> 18.2 us  [spread(): return lax.all_to_all(copies, axis, 0, 0)]
    concatenate x0 -> x1, other arithmetic: none -> 1.57 us  [body(): jnp.concatenate([in_proj.T, out_fwd, out_bwd], axis=0)]
    dot_general x5 -> x1, matrix products: 1.63 us -> 0.24 us  [body(): drive = jnp.dot(normed, in_proj, preferred_element_type=F32)]
    unnamed x14 -> x12, local copies, waits for them, and re-layouts: 7.84 us -> 8.62 us
  transfers between devices with their start and end apart: 4 -> 5, of which waited for: 4 -> 4; matrix products, arithmetic and copies ran while one was open for 6% -> 11% of each run, Pallas kernels for 0% -> 0%
where the time goes in v3:
time: 134 us
  starting transfers between devices  37.7 us (28%)
  waiting for transfers between devices  35.1 us (26%)
  blocking collectives  18.2 us (14%)
  between operations  14.3 us (11%)
  local copies, waits for them, and re-layouts  12.2 us (9%)
  matrix products  7.23 us (5%)
  Pallas kernels  4.59 us (3%)
  other arithmetic  4.15 us (3%)
    all_to_all x3, waiting for transfers between devices, spread(): return lax.all_to_all(copies, axis, 0, 0)  23.4 us
    all_to_all x3, starting transfers between devices, spread(): return lax.all_to_all(copies, axis, 0, 0)  22 us
    all_to_all x1, blocking collectives, spread(): return lax.all_to_all(copies, axis, 0, 0)  18.2 us
    all_to_all x1, starting transfers between devices, body(): rows = jnp.sum(lax.all_to_all(parts, 'neuron', 0, 0).astype(F32), axis=0)  15.7 us
    all_to_all x1, waiting for transfers between devices, body(): rows = jnp.sum(lax.all_to_all(parts, 'neuron', 0, 0).astype(F32), axis=0)  11.8 us
    unnamed x12, local copies, waits for them, and re-layouts  8.62 us
    pallas_call x1, Pallas kernels, mix_all(): pl.pallas_call(mix_kernel, grid=(count // group,), in_specs=[whole(bins,...  4.59 us
    dot_general x1, matrix products, body(): lax.dot_general(counts, read_weight, (((0,), (0,)), ((), ())), preferred_...  3.6 us
  transfers between devices with their start and end apart: 5, of which 4 were waited for; matrix products, arithmetic and copies ran while one was open for 11% of the time, Pallas kernels for 0%

profile of v3, /device:TPU:1, one launch (start us, length us, event | category | flops | bytes accessed | tf_op | source)
XLA Modules:
  0.0 133.5 jit_solution(13157375757388521964)
XLA Ops:
  7.3 1.1 copy.21
  8.3 1.6 %pad_maximum_fusion = bf16[384,256]{1,0:T(8,128)(2,1)} fusion(bf16[128,256]{1,0:T(8,128)(2,1)} %param.13, bf16[128,256]{1,0:T(8,128)(2,1)} %param.12, bf16[128,256]{1,0:T(8,128)(2,1)S(1)} %bitcast.44), kind=kLoop, calls=%fused_computation.15 | loop fusion | flops 589824 | bytes 393216 | tf_op jit(solution)/shard_map/concatenate | solution.py:95
  9.9 3.6 %fusion.2 = bf16[256,256]{1,0:T(8,128)(2,1)} fusion(bf16[4096,256]{1,0:T(8,128)(2,1)S(1)} %copy-done, s32[4096,256]{1,0:T(8,128)} %param.7), kind=kOutput, calls=%fused_computation.4 | convolution fusion | flops 537985024 | bytes 6422528 | tf_op jit(solution)/shard_map/dot_general | solution.py:115
  13.5 15.7 %all-to-all-start = ((bf16[16,16,256]{2,1,0:T(8,128)(2,1)}), bf16[16,16,256]{2,1,0:T(8,128)(2,1)S(1)}, u32[]{:S(2)}, u32[]{:S(2)}) async-start(bf16[16,16,256]{2,1,0:T(8,128)(2,1)} %bitcast), calls=%async_computation | async-start | bytes 262144 | tf_op jit(solution)/shard_map/all_to_all | solution.py:120
  29.4 0.2 select_reduce_fusion
  29.5 11.8 %all-to-all-done = bf16[16,16,256]{2,1,0:T(8,128)(2,1)S(1)} async-done(((bf16[16,16,256]{2,1,0:T(8,128)(2,1)}), bf16[16,16,256]{2,1,0:T(8,128)(2,1)S(1)}, u32[]{:S(2)}, u32[]{:S(2)}) %all-to-all-start) | async-done | bytes 131104 | tf_op jit(solution)/shard_map/all_to_all | solution.py:120
  41.3 0.1 multiply_reduce_fusion.5
  41.5 0.7 broadcast_in_dim.91
  42.2 6.4 %all-to-all-start.1 = ((bf16[16,16,256]{2,1,0:T(8,128)(2,1)}), bf16[16,16,256]{2,1,0:T(8,128)(2,1)S(1)}, u32[]{:S(2)}, u32[]{:S(2)}) async-start(bf16[16,16,256]{2,1,0:T(8,128)(2,1)} %broadcast_in_dim.91), calls=%async_computation.1 | async-start | bytes 262144 | tf_op jit(solution)/shard_map/all_to_all | solution.py:16
  48.6 0.6 slice.13
  49.2 0.7 pad.6.clone
  49.9 0.7 subtract_exponential_fusion
  50.6 0.1 select_convert_fusion.1.mix_fwd
  50.7 10.7 %all-to-all-done.1 = bf16[16,16,256]{2,1,0:T(8,128)(2,1)S(1)} async-done(((bf16[16,16,256]{2,1,0:T(8,128)(2,1)}), bf16[16,16,256]{2,1,0:T(8,128)(2,1)S(1)}, u32[]{:S(2)}, u32[]{:S(2)}) %all-to-all-start.1) | async-done | bytes 131104 | tf_op jit(solution)/shard_map/all_to_all | solution.py:16
  61.4 0.2 multiply_reduce_fusion.2
  61.7 0.7 broadcast_in_dim.96
  62.4 12.1 %all-to-all-start.2 = ((f32[32,3,128]{2,1,0:T(4,128)}), f32[32,3,128]{2,1,0:T(4,128)S(1)}, u32[]{:S(2)}, u32[]{:S(2)}) async-start(f32[32,3,128]{2,1,0:T(4,128)} %broadcast_in_dim.96), calls=%async_computation.2 | async-start | bytes 131072 | tf_op jit(solution)/shard_map/all_to_all | solution.py:16
  74.5 5.6 %copy.27 = s32[4096,256]{0,1:T(8,128)} copy(s32[4096,256]{1,0:T(8,128)} %param.7) | data formatting | bytes 8388608 | tf_op args[0]
  80.1 0.1 copy.25.lead_fwd
  80.3 0.1 copy.26.lead_bwd
  80.4 1.4 %all-to-all-done.2 = f32[32,3,128]{2,1,0:T(4,128)S(1)} async-done(((f32[32,3,128]{2,1,0:T(4,128)}), f32[32,3,128]{2,1,0:T(4,128)S(1)}, u32[]{:S(2)}, u32[]{:S(2)}) %all-to-all-start.2) | async-done | bytes 49184 | tf_op jit(solution)/shard_map/all_to_all | solution.py:16
  81.8 0.2 multiply_reduce_fusion
  82.1 0.1 select_reduce_fusion.3
  82.4 0.6 broadcast_in_dim.100
  83.0 3.5 %all-to-all-start.3 = ((f32[16,4,128]{2,1,0:T(4,128)}), f32[16,4,128]{2,1,0:T(4,128)S(1)}, u32[]{:S(2)}, u32[]{:S(2)}) async-start(f32[16,4,128]{2,1,0:T(4,128)} %broadcast_in_dim.100), calls=%async_computation.3 | async-start | bytes 65536 | tf_op jit(solution)/shard_map/all_to_all | solution.py:16
  86.5 0.1 select_convert_fusion.mix_bwd
  86.6 11.3 %all-to-all-done.3.enter = f32[16,4,128]{2,1,0:T(4,128)S(1)} async-done(((f32[16,4,128]{2,1,0:T(4,128)}), f32[16,4,128]{2,1,0:T(4,128)S(1)}, u32[]{:S(2)}, u32[]{:S(2)}) %all-to-all-start.3) | async-done | bytes 32800 | tf_op jit(solution)/shard_map/all_to_all | solution.py:16
  97.9 1.9 %copy-done.1 = bf16[6144,256]{1,0:T(8,128)(2,1)S(1)} copy-done((bf16[6144,256]{1,0:T(8,128)(2,1)S(1)}, bf16[6144,256]{1,0:T(8,128)(2,1)}, u32[]{:S(2)}) %copy-start.1) | copy-done | bytes 3145752
  99.8 4.6 %mix_all.1 = bf16[256,256]{1,0:T(8,128)(2,1)} custom-call(bf16[256,256]{1,0:T(8,128)(2,1)S(1)} %bitcast.43, bf16[16,384,256]{2,1,0:T(8,128)(2,1)S(1)} %bitcast.41, f32[16,4,128]{2,1,0:T(4,128)S(1)} %all-to-all-done.3.enter, bf16[256,256]{1,0:T(8,128)(2,1)S(1)} %select_convert_fusion.1.mix_fwd, bf16[256,256]{1,0:T(8,128)(2,1)S(1)} %select_convert_fusion.mix_bwd, ...), custom_call_target="tpu_custom_call" | custom-call | tf_op jit(solution)/shard_map/mix_all/pallas_call | solution.py:71
  104.4 3.4 %subtract_reduce_fusion = bf16[4096]{0:T(1024)(128)(2,1)S(1)} fusion(s32[4096,256]{0,1:T(8,128)} %copy.27, bf16[256,256]{1,0:T(8,128)(2,1)} %mix_all.1, bf16[4096,256]{1,0:T(8,128)(2,1)S(1)} %copy-done), kind=kOutput, calls=%fused_computation.1 | convolution fusion | flops 541061120 | bytes 6430720 | tf_op jit(solution)/shard_map/dot_general | solution.py:158
  107.8 18.2 %all_to_all.25 = bf16[32,32,128]{2,1,0:T(8,128)(2,1)S(1)} all-to-all(bf16[32,32,128]{2,1,0:T(8,128)(2,1)S(1)} %broadcast_in_dim.102), channel_id=1, replica_groups=mesh['neuron'=16,'tm'=32] {'tm'}, dimensions={0} | all-to-all | bytes 524288 | tf_op jit(solution)/shard_map/all_to_all | solution.py:16
  126.1 0.6 multiply_bitcast_fusion
  (31 shorter events, 0.7 us)
Async XLA Ops:
  7.2 2.8 %copy-start = (bf16[4096,256]{1,0:T(8,128)(2,1)S(1)}, bf16[4096,256]{1,0:T(8,128)(2,1)}, u32[]{:S(2)}) copy-start(bf16[4096,256]{1,0:T(8,128)(2,1)} %param.8) | copy-start | bytes 6291460
  7.2 54.2 %copy-start.2 = (bf16[256,128]{1,0:T(8,128)(2,1)S(1)}, bf16[256,128]{1,0:T(8,128)(2,1)}, u32[]{:S(2)}) copy-start(bf16[256,128]{1,0:T(8,128)(2,1)} %param.9) | copy-start | bytes 196612
  7.2 22.1 %copy-start.4 = (f32[256]{0:T(256)S(1)}, f32[256]{0:T(256)}, u32[]{:S(2)}) copy-start(f32[256]{0:T(256)} %param.11) | copy-start | bytes 3076
  7.2 54.2 %copy-start.3 = (f32[128]{0:T(128)S(1)}, f32[128]{0:T(128)}, u32[]{:S(2)}) copy-start(f32[128]{0:T(128)} %param.10) | copy-start | bytes 1540
  7.2 90.7 %all-gather.3.cloned.1.call-start = ((), (), s32[]{:S(2)}) async-start(), calls=%async_computation.5 | async-start | bytes 3342336 | tf_op jit(solution)/shard_map/all_gather | solution.py:95
  13.5 27.8 %all-to-all-start = ((bf16[16,16,256]{2,1,0:T(8,128)(2,1)}), bf16[16,16,256]{2,1,0:T(8,128)(2,1)S(1)}, u32[]{:S(2)}, u32[]{:S(2)}) async-start(bf16[16,16,256]{2,1,0:T(8,128)(2,1)} %bitcast), calls=%async_computation | async-start | bytes 262144 | tf_op jit(solution)/shard_map/all_to_all | solution.py:120
  42.2 19.2 %all-to-all-start.1 = ((bf16[16,16,256]{2,1,0:T(8,128)(2,1)}), bf16[16,16,256]{2,1,0:T(8,128)(2,1)S(1)}, u32[]{:S(2)}, u32[]{:S(2)}) async-start(bf16[16,16,256]{2,1,0:T(8,128)(2,1)} %broadcast_in_dim.91), calls=%async_computation.1 | async-start | bytes 262144 | tf_op jit(solution)/shard_map/all_to_all | solution.py:16
  62.4 19.4 %all-to-all-start.2 = ((f32[32,3,128]{2,1,0:T(4,128)}), f32[32,3,128]{2,1,0:T(4,128)S(1)}, u32[]{:S(2)}, u32[]{:S(2)}) async-start(f32[32,3,128]{2,1,0:T(4,128)} %broadcast_in_dim.96), calls=%async_computation.2 | async-start | bytes 131072 | tf_op jit(solution)/shard_map/all_to_all | solution.py:16
  83.0 14.9 %all-to-all-start.3 = ((f32[16,4,128]{2,1,0:T(4,128)}), f32[16,4,128]{2,1,0:T(4,128)S(1)}, u32[]{:S(2)}, u32[]{:S(2)}) async-start(f32[16,4,128]{2,1,0:T(4,128)} %broadcast_in_dim.100), calls=%async_computation.3 | async-start | bytes 65536 | tf_op jit(solution)/shard_map/all_to_all | solution.py:16
  97.9 1.9 %copy-start.1 = (bf16[6144,256]{1,0:T(8,128)(2,1)S(1)}, bf16[6144,256]{1,0:T(8,128)(2,1)}, u32[]{:S(2)}) copy-start(bf16[6144,256]{1,0:T(8,128)(2,1)} %all-gather.3.cloned.1.call-done) | copy-start | bytes 9437188
Sparse Core Ops, SparseCore 0:
  10.1 80.9 all-gather.2

commit v4 on v2

v4 whole, which is shorter than its diff:
```python
import jax
import jax.numpy as jnp
from jax import lax
from jax.experimental import pallas as pl
from jax.experimental.pallas import tpu as pltpu
from jax.sharding import PartitionSpec as P

F32 = jnp.float32
BF16 = jnp.bfloat16
ROWS = (((1,), (1,)), ((), ()))
LANES = 128
ROOM = 40 * 1024 * 1024
IN_VMEM = pl.BlockSpec(memory_space=pltpu.VMEM)
IN_HBM = pl.BlockSpec(memory_space=pltpu.HBM)


def far(array):
    return pltpu.with_memory_space_constraint(array, pltpu.HBM)


def near(array):
    return pltpu.with_memory_space_constraint(array, pltpu.VMEM)


def spread(part, axis):
    count = lax.axis_size(axis)
    copies = jnp.broadcast_to(part[None], (count,) + part.shape)
    return lax.all_to_all(copies, axis, 0, 0)


def read_kernel(counts_far, weights_far, part, turned, counts, weights, arrived):
    chunks, _, tall = turned.shape
    copies = []
    for k in range(chunks):
        here = pl.ds(k * tall, tall)
        for far, near, which in ((counts_far, counts, 0), (weights_far, weights, 1)):
            copies.append(pltpu.make_async_copy(far.at[here], near.at[here], arrived.at[which, k]))
            copies[-1].start()
    acc = None
    for k in range(chunks):
        here = slice(k * tall, (k + 1) * tall)
        copies[2 * k].wait()
        columns = counts[here, :].astype(F32).astype(BF16).T
        turned[k] = columns
        copies[2 * k + 1].wait()
        one = jnp.dot(columns, weights[here, :], preferred_element_type=F32)
        acc = one if acc is None else acc + one
    part[...] = acc.astype(BF16).reshape(part.shape)


def read_in(spikes, read_weight, ring):
    neurons, bins = spikes.shape
    channels = read_weight.shape[1]
    chunks = 8
    return pl.pallas_call(
        read_kernel,
        in_specs=[IN_HBM, IN_HBM],
        out_specs=[IN_VMEM, IN_VMEM],
        out_shape=[
            jax.ShapeDtypeStruct((ring, bins // ring, channels), BF16),
            jax.ShapeDtypeStruct((chunks, bins, neurons // chunks), BF16),
        ],
        scratch_shapes=[
            pltpu.VMEM((neurons, bins), spikes.dtype),
            pltpu.VMEM((neurons, channels), BF16),
            pltpu.SemaphoreType.DMA((2, chunks)),
        ],
        compiler_params=pltpu.CompilerParams(vmem_limit_bytes=ROOM),
        name="read_in",
    )(far(spikes), far(read_weight))


def likelihood_kernel(latent, weights, turned_far, copies, out_latent, sums, turned, arrived):
    chunks, _, wide = turned.shape
    pieces = wide // LANES
    coming = [pltpu.make_async_copy(turned_far.at[k], turned.at[k], arrived.at[k]) for k in range(chunks)]
    for one in coming:
        one.start()
    rows = latent[...]
    out_latent[...] = rows
    for k in range(chunks):
        log_rate = lax.dot_general(
            rows, weights[k * wide : (k + 1) * wide, :], ROWS, preferred_element_type=F32
        )
        coming[k].wait()
        terms = jnp.exp(log_rate) - turned[k].astype(F32) * log_rate
        one = jnp.sum(terms, axis=0, keepdims=True)
        for j in range(pieces):
            sums[pieces * k + j : pieces * k + j + 1, :] = one[:, j * LANES : (j + 1) * LANES]
    small = sums[...].astype(BF16)
    copies[...] = jnp.broadcast_to(small[None], copies.shape)


def likelihood(latent, read_weight, turned, blocks):
    neurons = read_weight.shape[0]
    return pl.pallas_call(
        likelihood_kernel,
        in_specs=[IN_VMEM, IN_VMEM, IN_HBM],
        out_specs=[IN_VMEM, IN_VMEM],
        out_shape=[
            jax.ShapeDtypeStruct((blocks, neurons // LANES, LANES), BF16),
            jax.ShapeDtypeStruct(latent.shape, BF16),
        ],
        scratch_shapes=[
            pltpu.VMEM((neurons // LANES, LANES), F32),
            pltpu.VMEM(turned.shape, BF16),
            pltpu.SemaphoreType.DMA((turned.shape[0],)),
        ],
        compiler_params=pltpu.CompilerParams(vmem_limit_bytes=ROOM),
        name="likelihood",
    )(latent, read_weight, far(turned))


def body(spikes, read_weight, in_proj, decay_rate, gate, out_fwd, out_bwd):
    bins = spikes.shape[1]
    ring = lax.axis_size("neuron")
    blocks = lax.axis_size("tm")
    place = lax.axis_index("tm")
    log_gate = jnp.log(gate)
    row = lax.broadcasted_iota(jnp.int32, (bins, bins), 0)
    col = lax.broadcasted_iota(jnp.int32, (bins, bins), 1)
    upto = jnp.sum(jnp.where(col <= row, log_gate[None, :], 0.0), axis=1, keepdims=True)
    before = upto - log_gate[:, None]
    upto_t = jnp.sum(jnp.where(row <= col, log_gate[:, None], 0.0), axis=0, keepdims=True)
    before_t = upto_t - log_gate[None, :]
    mix_fwd = jnp.where(col <= row, jnp.exp(jnp.minimum(upto - upto_t, 0.0)), 0.0).astype(BF16)
    mix_bwd = jnp.where(col >= row, jnp.exp(jnp.minimum(before_t - before, 0.0)), 0.0).astype(BF16)
    whole = upto[bins - 1, 0]
    first = lax.broadcasted_iota(jnp.int32, (bins, 1), 0).astype(F32)
    rate = decay_rate[None, :]
    scale_in = jnp.sqrt(-jnp.expm1(-2.0 * rate))
    carry_fwd = jnp.exp((whole - upto) - (bins - 1 - first) * rate) * scale_in
    carry_bwd = jnp.exp(before - first * rate) * scale_in
    cum_fwd = jnp.exp(upto - (first + 1.0) * rate)
    cum_bwd = jnp.exp((whole - before) - (bins - first) * rate)
    grow = jnp.exp((first - bins // 2) * rate)
    shrink = jnp.exp((bins // 2 - first) * rate)

    parts, turned = read_in(spikes, read_weight, ring)
    rows = jnp.sum(lax.all_to_all(parts, "neuron", 0, 0).astype(F32), axis=0)
    power = jnp.mean(rows * rows, axis=-1, keepdims=True) + 1e-05
    normed_rows = (rows * lax.rsqrt(power)).astype(BF16)
    normed = spread(normed_rows, "neuron").reshape(bins, -1)

    drive = jnp.dot(normed, in_proj, preferred_element_type=F32)
    sent = jnp.stack(
        [
            jnp.sum(drive * carry_fwd, axis=0),
            jnp.sum(drive * carry_bwd, axis=0),
            jnp.broadcast_to(whole, decay_rate.shape),
        ]
    )
    got = spread(sent, "tm")
    drive = drive * scale_in
    state_fwd = jnp.dot(mix_fwd, (drive * grow).astype(BF16), preferred_element_type=F32) * shrink
    state_bwd = jnp.dot(mix_bwd, (drive * shrink).astype(BF16), preferred_element_type=F32) * grow

    loss = got[:, 2, :]
    order = jnp.arange(blocks, dtype=jnp.int32)[:, None]
    earlier = (order >= order.T).astype(F32)
    span = jnp.sum(earlier[:, :, None] * loss[None, :, :], axis=1)
    span_before = span - loss
    at_fwd = jnp.sum(jnp.where(order == place, span_before, 0.0), axis=0)
    at_bwd = jnp.sum(jnp.where(order == place, span, 0.0), axis=0)
    gap_fwd = ((place - 1 - order) * bins).astype(F32) * rate
    gap_bwd = ((order - 1 - place) * bins).astype(F32) * rate
    weight_fwd = jnp.where(order < place, jnp.exp(jnp.minimum(at_fwd[None, :] - span - gap_fwd, 0.0)), 0.0)
    weight_bwd = jnp.where(order > place, jnp.exp(jnp.minimum(span_before - at_bwd[None, :] - gap_bwd, 0.0)), 0.0)
    enter_fwd = jnp.sum(weight_fwd * got[:, 0, :], axis=0)
    enter_bwd = jnp.sum(weight_bwd * got[:, 1, :], axis=0)
    forward = (state_fwd + cum_fwd * enter_fwd[None, :]).astype(BF16)
    backward = (state_bwd + cum_bwd * enter_bwd[None, :]).astype(BF16)
    mixed = jnp.dot(forward, out_fwd, preferred_element_type=F32)
    mixed = mixed + jnp.dot(backward, out_bwd, preferred_element_type=F32)
    parts = mixed.astype(BF16).reshape(ring, bins // ring, -1)
    mixed_rows = jnp.sum(lax.all_to_all(parts, "neuron", 0, 0).astype(F32), axis=0)
    latent_rows = (normed_rows.astype(F32) + mixed_rows).astype(BF16)
    latent = spread(latent_rows, "neuron").reshape(bins, -1)

    copies, latent = likelihood(latent, read_weight, turned, blocks)
    terms = lax.all_to_all(copies, "tm", 0, 0)
    nll = jnp.sum(terms.astype(F32), axis=0).reshape(-1) * (1.0 / (bins * blocks))
    return (latent, nll)


def solution(mesh):
    return jax.shard_map(
        body,
        mesh=mesh,
        in_specs=(
            P("neuron", "tm"),
            P("neuron", None),
            P(None, "neuron"),
            P("neuron"),
            P("tm"),
            P("neuron", None),
            P("neuron", None),
        ),
        out_specs=(P("tm", None), P("neuron")),
        check_vma=False,
    )
```

time: 129 us -> 129 us (level)
  blocking collectives: 31.2 us -> 49.5 us
  Pallas kernels: 0 us -> 8.66 us
  matrix products: 8.58 us -> 1.08 us
  local copies, waits for them, and re-layouts: 11.2 us -> 4.05 us
  waiting for transfers between devices: 35.4 us -> 29 us
  starting transfers between devices: 38.8 us -> 32.6 us
    all_to_all x1 -> x2, blocking collectives: 15.6 us -> 31.2 us  [the longest x1 15.7 us: body(): terms = lax.all_to_all(copies, 'tm', 0, 0)]
    pallas_call x0 -> x2, Pallas kernels: none -> 8.66 us  [the longest x1 4.56 us: read_in(): pl.pallas_call(read_kernel, in_specs=[IN_HBM, IN_HBM], out_specs=[IN_VMEM...]
    dot_general x7 -> x3, matrix products: 8.58 us -> 1.08 us  [the longest x1 0.42 us: body(): mixed = mixed + jnp.dot(backward, out_bwd, preferred_element_type=F32)]
    unnamed x14, local copies, waits for them, and re-layouts: 7.84 us -> 1.37 us
    all_to_all x3 -> x2, waiting for transfers between devices: 23.7 us -> 17.3 us  [spread(): return lax.all_to_all(copies, axis, 0, 0)]
    all_to_all x3 -> x2, starting transfers between devices: 23.1 us -> 16.7 us  [spread(): return lax.all_to_all(copies, axis, 0, 0)]
    all_to_all x1, blocking collectives: 15.7 us -> 18.3 us  [spread(): return lax.all_to_all(copies, axis, 0, 0)]
  transfers between devices with their start and end apart: 4 -> 3, of which waited for: 4 -> 3; matrix products, arithmetic and copies ran while one was open for 6% -> 2% of each run, Pallas kernels for 0% -> 0%
where the time goes in v4:
time: 129 us; the launch traced here: 128 us
  blocking collectives  49.5 us (38%)
  starting transfers between devices  32.6 us (25%)
  waiting for transfers between devices  29 us (22%)
  Pallas kernels  8.66 us (7%)
  local copies, waits for them, and re-layouts  4.05 us (3%)
  other arithmetic  2.44 us (2%)
    all_to_all x1, blocking collectives, spread(): return lax.all_to_all(copies, axis, 0, 0)  18.3 us
    all_to_all x2, waiting for transfers between devices, spread(): return lax.all_to_all(copies, axis, 0, 0)  17.3 us
    all_to_all x2, starting transfers between devices, spread(): return lax.all_to_all(copies, axis, 0, 0)  16.7 us
    all_to_all x1, starting transfers between devices, body(): rows = jnp.sum(lax.all_to_all(parts, 'neuron', 0, 0).astype(F32), axis=0)  15.9 us
    all_to_all x1, blocking collectives, body(): terms = lax.all_to_all(copies, 'tm', 0, 0)  15.7 us
    all_to_all x1, blocking collectives, body(): lax.all_to_all(parts, 'neuron', 0, 0).astype(F32)  15.6 us
    all_to_all x1, waiting for transfers between devices, body(): rows = jnp.sum(lax.all_to_all(parts, 'neuron', 0, 0).astype(F32), axis=0)  11.7 us
    pallas_call x1, Pallas kernels, read_in(): pl.pallas_call(read_kernel, in_specs=[IN_HBM, IN_HBM], out_specs=[IN_VMEM...  4.56 us
  transfers between devices with their start and end apart: 3, of which 3 were waited for; matrix products, arithmetic and copies ran while one was open for 2% of the time, Pallas kernels for 0%

profile of v4, /device:TPU:1, one launch (start us, length us, event | category | flops | bytes accessed | tf_op | source)
XLA Modules:
  0.0 128.2 jit_solution(14718098738652536098)
XLA Ops:
  0.6 0.0 copy-start
  0.7 4.6 %read_in.1 = (bf16[16,16,256]{2,1,0:T(8,128)(2,1)}, bf16[8,256,512]{2,1,0:T(8,128)(2,1)S(1)}) custom-call(s32[4096,256]{1,0:T(8,128)} %counts_far.1, bf16[4096,256]{1,0:T(8,128)(2,1)} %weights.1), custom_call_target="tpu_custom_call" | custom-call | tf_op jit(solution)/shard_map/read_in/pallas_call | solution.py:55
  5.3 1.3 %copy-done.2 = bf16[8,256,512]{2,1,0:T(8,128)(2,1)} copy-done((bf16[8,256,512]{2,1,0:T(8,128)(2,1)}, bf16[8,256,512]{2,1,0:T(8,128)(2,1)S(1)}, u32[]{:S(2)}) %copy-start.2) | copy-done | bytes 2097176
  6.6 15.9 %all-to-all-start = ((bf16[16,16,256]{2,1,0:T(8,128)(2,1)}), bf16[16,16,256]{2,1,0:T(8,128)(2,1)S(1)}, u32[]{:S(2)}, u32[]{:S(2)}) async-start(bf16[16,16,256]{2,1,0:T(8,128)(2,1)} %get-tuple-element.6), calls=%async_computation | async-start | bytes 262144 | tf_op jit(solution)/shard_map/all_to_all | solution.py:140
  22.6 0.2 select_reduce_fusion.1
  22.8 11.7 %all-to-all-done = bf16[16,16,256]{2,1,0:T(8,128)(2,1)S(1)} async-done(((bf16[16,16,256]{2,1,0:T(8,128)(2,1)}), bf16[16,16,256]{2,1,0:T(8,128)(2,1)S(1)}, u32[]{:S(2)}, u32[]{:S(2)}) %all-to-all-start) | async-done | bytes 131104 | tf_op jit(solution)/shard_map/all_to_all | solution.py:140
  34.5 0.1 multiply_reduce_fusion.5
  34.6 0.1 multiply_convert_fusion.6
  34.7 0.7 broadcast_in_dim.88
  35.4 6.1 %all-to-all-start.1 = ((bf16[16,16,256]{2,1,0:T(8,128)(2,1)}), bf16[16,16,256]{2,1,0:T(8,128)(2,1)S(1)}, u32[]{:S(2)}, u32[]{:S(2)}) async-start(bf16[16,16,256]{2,1,0:T(8,128)(2,1)} %broadcast_in_dim.88), calls=%async_computation.1 | async-start | bytes 262144 | tf_op jit(solution)/shard_map/all_to_all | solution.py:28
  41.5 0.6 slice.13
  42.0 0.7 pad.2.clone
  42.8 0.7 broadcast_subtract_fusion
  43.4 10.0 %all-to-all-done.1 = bf16[16,16,256]{2,1,0:T(8,128)(2,1)S(1)} async-done(((bf16[16,16,256]{2,1,0:T(8,128)(2,1)}), bf16[16,16,256]{2,1,0:T(8,128)(2,1)S(1)}, u32[]{:S(2)}, u32[]{:S(2)}) %all-to-all-start.1) | async-done | bytes 131104 | tf_op jit(solution)/shard_map/all_to_all | solution.py:28
  53.4 0.2 multiply_reduce_fusion.2
  53.7 0.1 maximum_maximum_fusion
  53.8 0.6 broadcast_in_dim.91
  54.4 10.7 %all-to-all-start.2 = ((f32[32,3,128]{2,1,0:T(4,128)}), f32[32,3,128]{2,1,0:T(4,128)S(1)}, u32[]{:S(2)}, u32[]{:S(2)}) async-start(f32[32,3,128]{2,1,0:T(4,128)} %broadcast_in_dim.91), calls=%async_computation.2 | async-start | bytes 131072 | tf_op jit(solution)/shard_map/all_to_all | solution.py:28
  65.1 7.3 %all-to-all-done.2 = f32[32,3,128]{2,1,0:T(4,128)S(1)} async-done(((f32[32,3,128]{2,1,0:T(4,128)}), f32[32,3,128]{2,1,0:T(4,128)S(1)}, u32[]{:S(2)}, u32[]{:S(2)}) %all-to-all-start.2) | async-done | bytes 49184 | tf_op jit(solution)/shard_map/all_to_all | solution.py:28
  72.5 0.2 multiply_reduce_fusion
  72.7 0.1 select_reduce_fusion.2
  72.8 0.1 multiply_reduce_fusion.3
  72.9 0.1 multiply_reduce_fusion.4
  73.0 0.4 fusion.5
  73.4 0.0 copy-done.6
  73.4 0.4 fusion
  73.8 15.6 %all_to_all.30 = bf16[16,16,256]{2,1,0:T(8,128)(2,1)S(1)} all-to-all(bf16[16,16,256]{2,1,0:T(8,128)(2,1)S(1)} %bitcast.25), channel_id=1, replica_groups=mesh['neuron'=16,'tm'=32] {'neuron'}, dimensions={0} | all-to-all | bytes 262144 | tf_op jit(solution)/shard_map/all_to_all | solution.py:176
  89.4 0.1 add_convert_fusion
  89.5 18.3 %all_to_all.31 = bf16[16,16,256]{2,1,0:T(8,128)(2,1)S(1)} all-to-all(bf16[16,16,256]{2,1,0:T(8,128)(2,1)S(1)} %broadcast_in_dim.94), channel_id=1, replica_groups=mesh['neuron'=16,'tm'=32] {'neuron'}, dimensions={0} | all-to-all | bytes 262144 | tf_op jit(solution)/shard_map/all_to_all | solution.py:28
  107.8 4.1 %likelihood.1 = (bf16[32,32,128]{2,1,0:T(8,128)(2,1)S(1)}, bf16[256,256]{1,0:T(8,128)(2,1)}) custom-call(bf16[256,256]{1,0:T(8,128)(2,1)S(1)} %bitcast.21, bf16[4096,256]{1,0:T(8,128)(2,1)S(1)} %copy-done.1, bf16[8,256,512]{2,1,0:T(8,128)(2,1)} %copy-done.2), custom_call_target="tpu_custom_call" | custom-call | tf_op jit(solution)/shard_map/likelihood/pallas_call | solution.py:96
  111.9 15.7 %all_to_all.32 = bf16[32,32,128]{2,1,0:T(8,128)(2,1)S(1)} all-to-all(bf16[32,32,128]{2,1,0:T(8,128)(2,1)S(1)} %get-tuple-element.9), channel_id=1, replica_groups=mesh['neuron'=16,'tm'=32] {'tm'}, dimensions={0} | all-to-all | bytes 524288 | tf_op jit(solution)/shard_map/all_to_all | solution.py:181
  127.6 0.6 multiply_bitcast_fusion
  (28 shorter events, 0.2 us)
Async XLA Ops:
  0.6 72.3 %copy-start = (bf16[128,256]{1,0:T(8,128)(2,1)S(1)}, bf16[128,256]{1,0:T(8,128)(2,1)}, u32[]{:S(2)}) copy-start(bf16[128,256]{1,0:T(8,128)(2,1)} %param.12) | copy-start | bytes 196612
  0.6 21.9 %copy-start.3 = (f32[256]{0:T(256)S(1)}, f32[256]{0:T(256)}, u32[]{:S(2)}) copy-start(f32[256]{0:T(256)} %param.11) | copy-start | bytes 3076
  0.7 42.1 %copy-start.4 = (f32[128]{0:T(128)S(1)}, f32[128]{0:T(128)}, u32[]{:S(2)}) copy-start(f32[128]{0:T(128)} %param.10) | copy-start | bytes 1540
  0.7 52.8 %copy-start.5 = (bf16[256,128]{1,0:T(8,128)(2,1)S(1)}, bf16[256,128]{1,0:T(8,128)(2,1)}, u32[]{:S(2)}) copy-start(bf16[256,128]{1,0:T(8,128)(2,1)} %param.9) | copy-start | bytes 196612
  5.2 1.4 %copy-start.2 = (bf16[8,256,512]{2,1,0:T(8,128)(2,1)}, bf16[8,256,512]{2,1,0:T(8,128)(2,1)S(1)}, u32[]{:S(2)}) copy-start(bf16[8,256,512]{2,1,0:T(8,128)(2,1)S(1)} %get-tuple-element.7.turned_far) | copy-start | bytes 6291460
  6.6 66.8 %copy-start.6 = (bf16[128,256]{1,0:T(8,128)(2,1)S(1)}, bf16[128,256]{1,0:T(8,128)(2,1)}, u32[]{:S(2)}) copy-start(bf16[128,256]{1,0:T(8,128)(2,1)} %param.13) | copy-start | bytes 196612
  6.6 27.9 %all-to-all-start = ((bf16[16,16,256]{2,1,0:T(8,128)(2,1)}), bf16[16,16,256]{2,1,0:T(8,128)(2,1)S(1)}, u32[]{:S(2)}, u32[]{:S(2)}) async-start(bf16[16,16,256]{2,1,0:T(8,128)(2,1)} %get-tuple-element.6), calls=%async_computation | async-start | bytes 262144 | tf_op jit(solution)/shard_map/all_to_all | solution.py:140
  35.4 72.4 %copy-start.1 = (bf16[4096,256]{1,0:T(8,128)(2,1)S(1)}, bf16[4096,256]{1,0:T(8,128)(2,1)}, u32[]{:S(2)}) copy-start(bf16[4096,256]{1,0:T(8,128)(2,1)} %weights.1) | copy-start | bytes 6291460
  35.4 18.1 %all-to-all-start.1 = ((bf16[16,16,256]{2,1,0:T(8,128)(2,1)}), bf16[16,16,256]{2,1,0:T(8,128)(2,1)S(1)}, u32[]{:S(2)}, u32[]{:S(2)}) async-start(bf16[16,16,256]{2,1,0:T(8,128)(2,1)} %broadcast_in_dim.88), calls=%async_computation.1 | async-start | bytes 262144 | tf_op jit(solution)/shard_map/all_to_all | solution.py:28
  54.4 18.0 %all-to-all-start.2 = ((f32[32,3,128]{2,1,0:T(4,128)}), f32[32,3,128]{2,1,0:T(4,128)S(1)}, u32[]{:S(2)}, u32[]{:S(2)}) async-start(f32[32,3,128]{2,1,0:T(4,128)} %broadcast_in_dim.91), calls=%async_computation.2 | async-start | bytes 131072 | tf_op jit(solution)/shard_map/all_to_all | solution.py:28

commit v5 on v4

--- a/solution.py
+++ b/solution.py
@@ -8,8 +8,9 @@
 F32 = jnp.float32
 BF16 = jnp.bfloat16
 ROWS = (((1,), (1,)), ((), ()))
+COLUMNS = (((0,), (0,)), ((), ()))
 LANES = 128
-ROOM = 40 * 1024 * 1024
+ROOM = 14 * 1024 * 1024
 IN_VMEM = pl.BlockSpec(memory_space=pltpu.VMEM)
 IN_HBM = pl.BlockSpec(memory_space=pltpu.HBM)
 
@@ -28,22 +29,22 @@
     return lax.all_to_all(copies, axis, 0, 0)
 
 
-def read_kernel(counts_far, weights_far, part, turned, counts, weights, arrived):
-    chunks, _, tall = turned.shape
+def read_kernel(counts_far, weights_far, part, counts, weights, arrived):
+    chunks = arrived.shape[1]
+    tall = counts.shape[0] // chunks
     copies = []
     for k in range(chunks):
         here = pl.ds(k * tall, tall)
-        for far, near, which in ((counts_far, counts, 0), (weights_far, weights, 1)):
-            copies.append(pltpu.make_async_copy(far.at[here], near.at[here], arrived.at[which, k]))
+        for away, here_ref, which in ((counts_far, counts, 0), (weights_far, weights, 1)):
+            copies.append(pltpu.make_async_copy(away.at[here], here_ref.at[here], arrived.at[which, k]))
             copies[-1].start()
     acc = None
     for k in range(chunks):
         here = slice(k * tall, (k + 1) * tall)
         copies[2 * k].wait()
-        columns = counts[here, :].astype(F32).astype(BF16).T
-        turned[k] = columns
         copies[2 * k + 1].wait()
-        one = jnp.dot(columns, weights[here, :], preferred_element_type=F32)
+        rows = counts[here, :].astype(F32).astype(BF16)
+        one = lax.dot_general(rows, weights[here, :], COLUMNS, preferred_element_type=F32)
         acc = one if acc is None else acc + one
     part[...] = acc.astype(BF16).reshape(part.shape)
 
@@ -51,38 +52,60 @@
 def read_in(spikes, read_weight, ring):
     neurons, bins = spikes.shape
     channels = read_weight.shape[1]
-    chunks = 8
     return pl.pallas_call(
         read_kernel,
         in_specs=[IN_HBM, IN_HBM],
-        out_specs=[IN_VMEM, IN_VMEM],
-        out_shape=[
-            jax.ShapeDtypeStruct((ring, bins // ring, channels), BF16),
-            jax.ShapeDtypeStruct((chunks, bins, neurons // chunks), BF16),
-        ],
+        out_specs=IN_VMEM,
+        out_shape=jax.ShapeDtypeStruct((ring, bins // ring, channels), BF16),
         scratch_shapes=[
             pltpu.VMEM((neurons, bins), spikes.dtype),
             pltpu.VMEM((neurons, channels), BF16),
-            pltpu.SemaphoreType.DMA((2, chunks)),
+            pltpu.SemaphoreType.DMA((2, 8)),
         ],
         compiler_params=pltpu.CompilerParams(vmem_limit_bytes=ROOM),
         name="read_in",
     )(far(spikes), far(read_weight))
 
 
-def likelihood_kernel(latent, weights, turned_far, copies, out_latent, sums, turned, arrived):
+def turn_kernel(counts_far, after, turned, counts, arrived):
+    chunks, _, tall = turned.shape
+    coming = []
+    for k in range(chunks):
+        here = pl.ds(k * tall, tall)
+        coming.append(pltpu.make_async_copy(counts_far.at[here], counts.at[here], arrived.at[k]))
+        coming[-1].start()
+    for k in range(chunks):
+        coming[k].wait()
+        turned[k] = counts[k * tall : (k + 1) * tall, :].astype(F32).astype(BF16).T
+
+
+def turn(spikes, after):
+    neurons, bins = spikes.shape
+    chunks = 8
+    turned = (chunks, bins, neurons // chunks)
+    return pl.pallas_call(
+        turn_kernel,
+        in_specs=[IN_HBM, pl.BlockSpec(memory_space=pl.ANY)],
+        out_specs=IN_VMEM,
+        out_shape=pltpu.VMEM(turned, BF16),
+        scratch_shapes=[
+            pltpu.VMEM((neurons, bins), spikes.dtype),
+            pltpu.SemaphoreType.DMA((chunks,)),
+        ],
+        compiler_params=pltpu.CompilerParams(vmem_limit_bytes=ROOM),
+        name="turn",
+    )(far(spikes), after)
+
+
+def likelihood_kernel(latent, weights, turned, copies, out_latent, sums):
     chunks, _, wide = turned.shape
     pieces = wide // LANES
-    coming = [pltpu.make_async_copy(turned_far.at[k], turned.at[k], arrived.at[k]) for k in range(chunks)]
-    for one in coming:
-        one.start()
     rows = latent[...]
     out_latent[...] = rows
     for k in range(chunks):
         log_rate = lax.dot_general(
             rows, weights[k * wide : (k + 1) * wide, :], ROWS, preferred_element_type=F32
         )
-        coming[k].wait()
         terms = jnp.exp(log_rate) - turned[k].astype(F32) * log_rate
         one = jnp.sum(terms, axis=0, keepdims=True)
         for j in range(pieces):
@@ -95,7 +118,7 @@
     neurons = read_weight.shape[0]
     return pl.pallas_call(
         likelihood_kernel,
-        in_specs=[IN_VMEM, IN_VMEM, IN_HBM],
+        in_specs=[IN_VMEM, IN_VMEM, IN_VMEM],
         out_specs=[IN_VMEM, IN_VMEM],
         out_shape=[
             jax.ShapeDtypeStruct((blocks, neurons // LANES, LANES), BF16),
@@ -103,12 +126,10 @@
         ],
         scratch_shapes=[
             pltpu.VMEM((neurons // LANES, LANES), F32),
-            pltpu.VMEM(turned.shape, BF16),
-            pltpu.SemaphoreType.DMA((turned.shape[0],)),
         ],
         compiler_params=pltpu.CompilerParams(vmem_limit_bytes=ROOM),
         name="likelihood",
-    )(latent, read_weight, far(turned))
+    )(near(latent), near(read_weight), near(turned))
 
 
 def body(spikes, read_weight, in_proj, decay_rate, gate, out_fwd, out_bwd):
@@ -136,11 +157,12 @@
     grow = jnp.exp((first - bins // 2) * rate)
     shrink = jnp.exp((bins // 2 - first) * rate)
 
-    parts, turned = read_in(spikes, read_weight, ring)
+    parts = read_in(spikes, read_weight, ring)
     rows = jnp.sum(lax.all_to_all(parts, "neuron", 0, 0).astype(F32), axis=0)
     power = jnp.mean(rows * rows, axis=-1, keepdims=True) + 1e-05
     normed_rows = (rows * lax.rsqrt(power)).astype(BF16)
     normed = spread(normed_rows, "neuron").reshape(bins, -1)
+    turned = turn(spikes, normed_rows)
 
     drive = jnp.dot(normed, in_proj, preferred_element_type=F32)
     sent = jnp.stack(

time: 129 us -> 126 us (0.977)
  blocking collectives: 49.5 us -> 31.2 us
  waiting for transfers between devices: 29 us -> 37.2 us
  starting transfers between devices: 32.6 us -> 38.9 us
  local copies, waits for them, and re-layouts: 4.05 us -> 6.3 us
    all_to_all x1 -> x0, blocking collectives: 18.3 us -> none  [spread(): return lax.all_to_all(copies, axis, 0, 0)]
    all_to_all x2 -> x3, waiting for transfers between devices: 17.3 us -> 25.4 us  [spread(): return lax.all_to_all(copies, axis, 0, 0)]
    all_to_all x2 -> x3, starting transfers between devices: 16.7 us -> 23.1 us  [spread(): return lax.all_to_all(copies, axis, 0, 0)]
    unnamed x14 -> x16, local copies, waits for them, and re-layouts: 1.37 us -> 2.97 us
    pallas_call x2 -> x3, Pallas kernels: 8.66 us -> 7.82 us  [the longest x1 3.93 us: read_in(): pl.pallas_call(read_kernel, in_specs=[IN_HBM, IN_HBM], out_specs=IN_VMEM,...]
  transfers between devices with their start and end apart: 3 -> 4, of which waited for: 3 -> 4; matrix products, arithmetic and copies ran while one was open for 2% -> 2% of each run, Pallas kernels for 0% -> 2%
where the time goes in v5:
time: 126 us
  starting transfers between devices  38.9 us (31%)
  waiting for transfers between devices  37.2 us (30%)
  blocking collectives  31.2 us (25%)
  Pallas kernels  7.82 us (6%)
  local copies, waits for them, and re-layouts  6.3 us (5%)
  other arithmetic  2.44 us (2%)
    all_to_all x3, waiting for transfers between devices, spread(): return lax.all_to_all(copies, axis, 0, 0)  25.4 us
    all_to_all x3, starting transfers between devices, spread(): return lax.all_to_all(copies, axis, 0, 0)  23.1 us
    all_to_all x1, starting transfers between devices, body(): rows = jnp.sum(lax.all_to_all(parts, 'neuron', 0, 0).astype(F32), axis=0)  15.9 us
    all_to_all x1, blocking collectives, body(): terms = lax.all_to_all(copies, 'tm', 0, 0)  15.6 us
    all_to_all x1, blocking collectives, body(): lax.all_to_all(parts, 'neuron', 0, 0).astype(F32)  15.6 us
    all_to_all x1, waiting for transfers between devices, body(): rows = jnp.sum(lax.all_to_all(parts, 'neuron', 0, 0).astype(F32), axis=0)  11.7 us
    pallas_call x1, Pallas kernels, read_in(): pl.pallas_call(read_kernel, in_specs=[IN_HBM, IN_HBM], out_specs=IN_VMEM,...  3.93 us
    unnamed x16, local copies, waits for them, and re-layouts  2.97 us
  transfers between devices with their start and end apart: 4, of which 4 were waited for; matrix products, arithmetic and copies ran while one was open for 2% of the time, Pallas kernels for 2%

profile of v5, /device:TPU:1, one launch (start us, length us, event | category | flops | bytes accessed | tf_op | source)
XLA Modules:
  0.0 125.8 jit_solution(7205026232297470489)
XLA Ops:
  0.7 3.9 %read_in.1 = bf16[16,16,256]{2,1,0:T(8,128)(2,1)} custom-call(s32[4096,256]{1,0:T(8,128)} %counts_far.3, bf16[4096,256]{1,0:T(8,128)(2,1)} %weights.1), custom_call_target="tpu_custom_call" | custom-call | tf_op jit(solution)/shard_map/read_in/pallas_call | solution.py:55
  4.6 15.9 %all-to-all-start = ((bf16[16,16,256]{2,1,0:T(8,128)(2,1)}), bf16[16,16,256]{2,1,0:T(8,128)(2,1)S(1)}, u32[]{:S(2)}, u32[]{:S(2)}) async-start(bf16[16,16,256]{2,1,0:T(8,128)(2,1)} %read_in.1), calls=%async_computation | async-start | bytes 262144 | tf_op jit(solution)/shard_map/all_to_all | solution.py:161
  20.6 0.2 select_reduce_fusion.1
  20.8 11.7 %all-to-all-done = bf16[16,16,256]{2,1,0:T(8,128)(2,1)S(1)} async-done(((bf16[16,16,256]{2,1,0:T(8,128)(2,1)}), bf16[16,16,256]{2,1,0:T(8,128)(2,1)S(1)}, u32[]{:S(2)}, u32[]{:S(2)}) %all-to-all-start) | async-done | bytes 131104 | tf_op jit(solution)/shard_map/all_to_all | solution.py:161
  32.5 0.1 multiply_reduce_fusion.5
  32.7 0.1 multiply_convert_fusion.6.after
  32.7 0.7 broadcast_in_dim.88
  33.4 5.9 %all-to-all-start.1 = ((bf16[16,16,256]{2,1,0:T(8,128)(2,1)}), bf16[16,16,256]{2,1,0:T(8,128)(2,1)S(1)}, u32[]{:S(2)}, u32[]{:S(2)}) async-start(bf16[16,16,256]{2,1,0:T(8,128)(2,1)} %broadcast_in_dim.88), calls=%async_computation.1 | async-start | bytes 262144 | tf_op jit(solution)/shard_map/all_to_all | solution.py:29
  39.4 0.6 slice.13
  40.0 0.7 pad.2.clone
  40.7 0.7 broadcast_subtract_fusion
  41.4 10.0 %all-to-all-done.1 = bf16[16,16,256]{2,1,0:T(8,128)(2,1)S(1)} async-done(((bf16[16,16,256]{2,1,0:T(8,128)(2,1)}), bf16[16,16,256]{2,1,0:T(8,128)(2,1)S(1)}, u32[]{:S(2)}, u32[]{:S(2)}) %all-to-all-start.1) | async-done | bytes 131104 | tf_op jit(solution)/shard_map/all_to_all | solution.py:29
  51.4 0.2 multiply_reduce_fusion.2
  51.7 0.6 broadcast_in_dim.91
  52.3 10.7 %all-to-all-start.2 = ((f32[32,3,128]{2,1,0:T(4,128)}), f32[32,3,128]{2,1,0:T(4,128)S(1)}, u32[]{:S(2)}, u32[]{:S(2)}) async-start(f32[32,3,128]{2,1,0:T(4,128)} %broadcast_in_dim.91), calls=%async_computation.2 | async-start | bytes 131072 | tf_op jit(solution)/shard_map/all_to_all | solution.py:29
  63.0 7.3 %all-to-all-done.2 = f32[32,3,128]{2,1,0:T(4,128)S(1)} async-done(((f32[32,3,128]{2,1,0:T(4,128)}), f32[32,3,128]{2,1,0:T(4,128)S(1)}, u32[]{:S(2)}, u32[]{:S(2)}) %all-to-all-start.2) | async-done | bytes 49184 | tf_op jit(solution)/shard_map/all_to_all | solution.py:29
  70.4 0.2 multiply_reduce_fusion
  70.6 0.1 select_reduce_fusion.2
  70.7 0.1 multiply_reduce_fusion.3
  70.8 0.1 multiply_reduce_fusion.4
  70.9 0.4 fusion.5
  71.3 0.4 fusion
  71.7 15.6 %all_to_all.30 = bf16[16,16,256]{2,1,0:T(8,128)(2,1)S(1)} all-to-all(bf16[16,16,256]{2,1,0:T(8,128)(2,1)S(1)} %bitcast.25), channel_id=1, replica_groups=mesh['neuron'=16,'tm'=32] {'neuron'}, dimensions={0} | all-to-all | bytes 262144 | tf_op jit(solution)/shard_map/all_to_all | solution.py:198
  87.4 0.7 broadcast_in_dim.94
  88.1 6.5 %all-to-all-start.4 = ((bf16[16,16,256]{2,1,0:T(8,128)(2,1)}), bf16[16,16,256]{2,1,0:T(8,128)(2,1)S(1)}, u32[]{:S(2)}, u32[]{:S(2)}) async-start(bf16[16,16,256]{2,1,0:T(8,128)(2,1)} %broadcast_in_dim.94), calls=%async_computation.4 | async-start | bytes 262144 | tf_op jit(solution)/shard_map/all_to_all | solution.py:29
  94.5 2.5 %turn.1.turned = bf16[8,256,512]{2,1,0:T(8,128)(2,1)S(1)} custom-call(s32[4096,256]{1,0:T(8,128)} %counts_far.3, bf16[16,256]{1,0:T(8,128)(2,1)S(1)} %multiply_convert_fusion.6.after), custom_call_target="tpu_custom_call" | custom-call | tf_op jit(solution)/shard_map/turn/pallas_call | solution.py:86
  97.1 1.3 %copy-done.2 = bf16[8,256,512]{2,1,0:T(8,128)(2,1)} copy-done((bf16[8,256,512]{2,1,0:T(8,128)(2,1)}, bf16[8,256,512]{2,1,0:T(8,128)(2,1)S(1)}, u32[]{:S(2)}) %copy-start.2) | copy-done | bytes 2097176
  98.4 8.1 %all-to-all-done.4 = bf16[16,16,256]{2,1,0:T(8,128)(2,1)S(1)} async-done(((bf16[16,16,256]{2,1,0:T(8,128)(2,1)}), bf16[16,16,256]{2,1,0:T(8,128)(2,1)S(1)}, u32[]{:S(2)}, u32[]{:S(2)}) %all-to-all-start.4) | async-done | bytes 131104 | tf_op jit(solution)/shard_map/all_to_all | solution.py:29
  106.5 1.6 %copy-done.3 = bf16[8,256,512]{2,1,0:T(8,128)(2,1)S(1)} copy-done((bf16[8,256,512]{2,1,0:T(8,128)(2,1)S(1)}, bf16[8,256,512]{2,1,0:T(8,128)(2,1)}, u32[]{:S(2)}) %copy-start.3) | copy-done | bytes 2097176
  108.1 1.4 %likelihood.1 = (bf16[32,32,128]{2,1,0:T(8,128)(2,1)S(1)}, bf16[256,256]{1,0:T(8,128)(2,1)}) custom-call(bf16[256,256]{1,0:T(8,128)(2,1)S(1)} %bitcast.21, bf16[4096,256]{1,0:T(8,128)(2,1)S(1)} %copy-done.1, bf16[8,256,512]{2,1,0:T(8,128)(2,1)S(1)} %copy-done.3), custom_call_target="tpu_custom_call" | custom-call | tf_op jit(solution)/shard_map/likelihood/pallas_call | solution.py:119
  109.5 15.6 %all_to_all.31 = bf16[32,32,128]{2,1,0:T(8,128)(2,1)S(1)} all-to-all(bf16[32,32,128]{2,1,0:T(8,128)(2,1)S(1)} %get-tuple-element.5), channel_id=1, replica_groups=mesh['neuron'=16,'tm'=32] {'tm'}, dimensions={0} | all-to-all | bytes 524288 | tf_op jit(solution)/shard_map/all_to_all | solution.py:203
  125.2 0.6 multiply_bitcast_fusion
  (32 shorter events, 0.4 us)
Async XLA Ops:
  0.6 70.2 %copy-start = (bf16[128,256]{1,0:T(8,128)(2,1)S(1)}, bf16[128,256]{1,0:T(8,128)(2,1)}, u32[]{:S(2)}) copy-start(bf16[128,256]{1,0:T(8,128)(2,1)} %param.12) | copy-start | bytes 196612
  0.6 19.9 %copy-start.4 = (f32[256]{0:T(256)S(1)}, f32[256]{0:T(256)}, u32[]{:S(2)}) copy-start(f32[256]{0:T(256)} %param.11) | copy-start | bytes 3076
  0.7 40.0 %copy-start.5 = (f32[128]{0:T(128)S(1)}, f32[128]{0:T(128)}, u32[]{:S(2)}) copy-start(f32[128]{0:T(128)} %param.10) | copy-start | bytes 1540
  0.7 50.7 %copy-start.6 = (bf16[256,128]{1,0:T(8,128)(2,1)S(1)}, bf16[256,128]{1,0:T(8,128)(2,1)}, u32[]{:S(2)}) copy-start(bf16[256,128]{1,0:T(8,128)(2,1)} %param.9) | copy-start | bytes 196612
  4.6 66.7 %copy-start.7 = (bf16[128,256]{1,0:T(8,128)(2,1)S(1)}, bf16[128,256]{1,0:T(8,128)(2,1)}, u32[]{:S(2)}) copy-start(bf16[128,256]{1,0:T(8,128)(2,1)} %param.13) | copy-start | bytes 196612
  4.6 27.9 %all-to-all-start = ((bf16[16,16,256]{2,1,0:T(8,128)(2,1)}), bf16[16,16,256]{2,1,0:T(8,128)(2,1)S(1)}, u32[]{:S(2)}, u32[]{:S(2)}) async-start(bf16[16,16,256]{2,1,0:T(8,128)(2,1)} %read_in.1), calls=%async_computation | async-start | bytes 262144 | tf_op jit(solution)/shard_map/all_to_all | solution.py:161
  33.4 17.9 %all-to-all-start.1 = ((bf16[16,16,256]{2,1,0:T(8,128)(2,1)}), bf16[16,16,256]{2,1,0:T(8,128)(2,1)S(1)}, u32[]{:S(2)}, u32[]{:S(2)}) async-start(bf16[16,16,256]{2,1,0:T(8,128)(2,1)} %broadcast_in_dim.88), calls=%async_computation.1 | async-start | bytes 262144 | tf_op jit(solution)/shard_map/all_to_all | solution.py:29
  52.3 18.0 %all-to-all-start.2 = ((f32[32,3,128]{2,1,0:T(4,128)}), f32[32,3,128]{2,1,0:T(4,128)S(1)}, u32[]{:S(2)}, u32[]{:S(2)}) async-start(f32[32,3,128]{2,1,0:T(4,128)} %broadcast_in_dim.91), calls=%async_computation.2 | async-start | bytes 131072 | tf_op jit(solution)/shard_map/all_to_all | solution.py:29
  88.1 18.5 %all-to-all-start.4 = ((bf16[16,16,256]{2,1,0:T(8,128)(2,1)}), bf16[16,16,256]{2,1,0:T(8,128)(2,1)S(1)}, u32[]{:S(2)}, u32[]{:S(2)}) async-start(bf16[16,16,256]{2,1,0:T(8,128)(2,1)} %broadcast_in_dim.94), calls=%async_computation.4 | async-start | bytes 262144 | tf_op jit(solution)/shard_map/all_to_all | solution.py:29
  94.5 12.0 %copy-start.1 = (bf16[4096,256]{1,0:T(8,128)(2,1)S(1)}, bf16[4096,256]{1,0:T(8,128)(2,1)}, u32[]{:S(2)}) copy-start(bf16[4096,256]{1,0:T(8,128)(2,1)} %weights.1) | copy-start | bytes 6291460
  97.0 1.4 %copy-start.2 = (bf16[8,256,512]{2,1,0:T(8,128)(2,1)}, bf16[8,256,512]{2,1,0:T(8,128)(2,1)S(1)}, u32[]{:S(2)}) copy-start(bf16[8,256,512]{2,1,0:T(8,128)(2,1)S(1)} %turn.1.turned) | copy-start | bytes 6291460
  106.5 1.6 %copy-start.3 = (bf16[8,256,512]{2,1,0:T(8,128)(2,1)S(1)}, bf16[8,256,512]{2,1,0:T(8,128)(2,1)}, u32[]{:S(2)}) copy-start(bf16[8,256,512]{2,1,0:T(8,128)(2,1)} %copy-done.2) | copy-start | bytes 6291460

commit v6 on v5

--- a/solution.py
+++ b/solution.py
@@ -3,6 +3,7 @@
 from jax import lax
 from jax.experimental import pallas as pl
 from jax.experimental.pallas import tpu as pltpu
+from jax.sharding import Mesh
 from jax.sharding import PartitionSpec as P
 
 F32 = jnp.float32
@@ -27,6 +28,11 @@
     count = lax.axis_size(axis)
     copies = jnp.broadcast_to(part[None], (count,) + part.shape)
     return lax.all_to_all(copies, axis, 0, 0)
+
+
+def reduce_rows(parts):
+    quarter = jnp.sum(lax.all_to_all(parts, "near", 0, 0).astype(F32), axis=0)
+    return jnp.sum(spread(quarter.astype(BF16), "far").astype(F32), axis=0)
 
 
 def read_kernel(counts_far, weights_far, part, counts, weights, arrived):
@@ -67,16 +73,20 @@
     )(far(spikes), far(read_weight))
 
 
-def turn_kernel(counts_far, after, turned, counts, arrived):
+def turn_kernel(counts_far, after, turned_far, counts, turned, arrived, left):
     chunks, _, tall = turned.shape
-    coming = []
+    coming, leaving = [], []
     for k in range(chunks):
         here = pl.ds(k * tall, tall)
         coming.append(pltpu.make_async_copy(counts_far.at[here], counts.at[here], arrived.at[k]))
+        leaving.append(pltpu.make_async_copy(turned.at[k], turned_far.at[k], left.at[k]))
         coming[-1].start()
     for k in range(chunks):
         coming[k].wait()
         turned[k] = counts[k * tall : (k + 1) * tall, :].astype(F32).astype(BF16).T
+        leaving[k].start()
+    for one in leaving:
+        one.wait()
 
 
 def turn(spikes, after):
@@ -86,10 +96,12 @@
     return pl.pallas_call(
         turn_kernel,
         in_specs=[IN_HBM, pl.BlockSpec(memory_space=pl.ANY)],
-        out_specs=IN_VMEM,
-        out_shape=pltpu.VMEM(turned, BF16),
+        out_specs=IN_HBM,
+        out_shape=pltpu.HBM(turned, BF16),
         scratch_shapes=[
             pltpu.VMEM((neurons, bins), spikes.dtype),
+            pltpu.VMEM(turned, BF16),
+            pltpu.SemaphoreType.DMA((chunks,)),
             pltpu.SemaphoreType.DMA((chunks,)),
         ],
         compiler_params=pltpu.CompilerParams(vmem_limit_bytes=ROOM),
@@ -97,15 +109,19 @@
     )(far(spikes), after)
 
 
-def likelihood_kernel(latent, weights, turned, copies, out_latent, sums):
+def likelihood_kernel(latent, weights, turned_far, copies, out_latent, sums, turned, arrived):
     chunks, _, wide = turned.shape
     pieces = wide // LANES
+    coming = [pltpu.make_async_copy(turned_far.at[k], turned.at[k], arrived.at[k]) for k in range(chunks)]
+    for one in coming:
+        one.start()
     rows = latent[...]
     out_latent[...] = rows
     for k in range(chunks):
         log_rate = lax.dot_general(
             rows, weights[k * wide : (k + 1) * wide, :], ROWS, preferred_element_type=F32
         )
+        coming[k].wait()
         terms = jnp.exp(log_rate) - turned[k].astype(F32) * log_rate
         one = jnp.sum(terms, axis=0, keepdims=True)
         for j in range(pieces):
@@ -118,7 +134,7 @@
     neurons = read_weight.shape[0]
     return pl.pallas_call(
         likelihood_kernel,
-        in_specs=[IN_VMEM, IN_VMEM, IN_VMEM],
+        in_specs=[IN_VMEM, IN_VMEM, IN_HBM],
         out_specs=[IN_VMEM, IN_VMEM],
         out_shape=[
             jax.ShapeDtypeStruct((blocks, neurons // LANES, LANES), BF16),
@@ -126,15 +142,17 @@
         ],
         scratch_shapes=[
             pltpu.VMEM((neurons // LANES, LANES), F32),
+            pltpu.VMEM(turned.shape, BF16),
+            pltpu.SemaphoreType.DMA((turned.shape[0],)),
         ],
         compiler_params=pltpu.CompilerParams(vmem_limit_bytes=ROOM),
         name="likelihood",
-    )(near(latent), near(read_weight), near(turned))
+    )(near(latent), near(read_weight), far(turned))
 
 
 def body(spikes, read_weight, in_proj, decay_rate, gate, out_fwd, out_bwd):
     bins = spikes.shape[1]
-    ring = lax.axis_size("neuron")
+    quad = lax.axis_size("near")
     blocks = lax.axis_size("tm")
     place = lax.axis_index("tm")
     log_gate = jnp.log(gate)
@@ -157,11 +175,10 @@
     grow = jnp.exp((first - bins // 2) * rate)
     shrink = jnp.exp((bins // 2 - first) * rate)
 
-    parts = read_in(spikes, read_weight, ring)
-    rows = jnp.sum(lax.all_to_all(parts, "neuron", 0, 0).astype(F32), axis=0)
+    rows = reduce_rows(read_in(spikes, read_weight, quad))
     power = jnp.mean(rows * rows, axis=-1, keepdims=True) + 1e-05
     normed_rows = (rows * lax.rsqrt(power)).astype(BF16)
-    normed = spread(normed_rows, "neuron").reshape(bins, -1)
+    normed = spread(normed_rows, "near").reshape(bins, -1)
     turned = turn(spikes, normed_rows)
 
     drive = jnp.dot(normed, in_proj, preferred_element_type=F32)
@@ -194,10 +211,9 @@
     backward = (state_bwd + cum_bwd * enter_bwd[None, :]).astype(BF16)
     mixed = jnp.dot(forward, out_fwd, preferred_element_type=F32)
     mixed = mixed + jnp.dot(backward, out_bwd, preferred_element_type=F32)
-    parts = mixed.astype(BF16).reshape(ring, bins // ring, -1)
-    mixed_rows = jnp.sum(lax.all_to_all(parts, "neuron", 0, 0).astype(F32), axis=0)
+    mixed_rows = reduce_rows(mixed.astype(BF16).reshape(quad, bins // quad, -1))
     latent_rows = (normed_rows.astype(F32) + mixed_rows).astype(BF16)
-    latent = spread(latent_rows, "neuron").reshape(bins, -1)
+    latent = spread(latent_rows, "near").reshape(bins, -1)
 
     copies, latent = likelihood(latent, read_weight, turned, blocks)
     terms = lax.all_to_all(copies, "tm", 0, 0)
@@ -206,18 +222,21 @@
 
 
 def solution(mesh):
+    ring = mesh.shape["neuron"]
+    quads = Mesh(mesh.devices.reshape(ring // 4, 4, -1), ("far", "near", "tm"))
+    neuron = ("far", "near")
     return jax.shard_map(
         body,
-        mesh=mesh,
+        mesh=quads,
         in_specs=(
-            P("neuron", "tm"),
-            P("neuron", None),
-            P(None, "neuron"),
-            P("neuron"),
+            P(neuron, "tm"),
+            P(neuron, None),
+            P(None, neuron),
+            P(neuron),
             P("tm"),
-            P("neuron", None),
-            P("neuron", None),
+            P(neuron, None),
+            P(neuron, None),
         ),
-        out_specs=(P("tm", None), P("neuron")),
+        out_specs=(P("tm", None), P(neuron)),
         check_vma=False,
     )

time: 126 us -> 127 us (level)
  waiting for transfers between devices: 37.2 us -> 28.1 us
  blocking collectives: 31.2 us -> 39.2 us
  Pallas kernels: 7.82 us -> 11.4 us
  local copies, waits for them, and re-layouts: 6.3 us -> 4.03 us
    all_to_all x1, starting transfers between devices: 15.9 us -> 6.59 us  [reduce_rows(): quarter = jnp.sum(lax.all_to_all(parts, 'near', 0, 0).astype(F32), axis=0)]
    all_to_all x3 -> x4, starting transfers between devices: 23.1 us -> 32.1 us  [spread(): return lax.all_to_all(copies, axis, 0, 0)]
    all_to_all x1, waiting for transfers between devices: 11.7 us -> 3.25 us  [reduce_rows(): quarter = jnp.sum(lax.all_to_all(parts, 'near', 0, 0).astype(F32), axis=0)]
    all_to_all x1 -> x2, blocking collectives: 15.6 us -> 21.7 us  [the longest x1 14.5 us: spread(): return lax.all_to_all(copies, axis, 0, 0)]
    unnamed x16 -> x12, local copies, waits for them, and re-layouts: 2.97 us -> 0.03 us
    pallas_call x1, Pallas kernels: 1.4 us -> 4.1 us  [likelihood(): pl.pallas_call(likelihood_kernel, in_specs=[IN_VMEM, IN_VMEM, IN_HBM], ou...]
    all_to_all x1, blocking collectives: 15.6 us -> 17.4 us  [body(): terms = lax.all_to_all(copies, 'tm', 0, 0)]
    broadcast_in_dim x3 -> x5, local copies, waits for them, and re-layouts: 1.99 us -> 2.65 us  [spread(): copies = jnp.broadcast_to(part[None], (count,) + part.shape)]
  transfers between devices with their start and end apart: 4 -> 5, of which waited for: 4 -> 5; matrix products, arithmetic and copies ran while one was open for 2% -> 2% of each run, Pallas kernels for 2% -> 3%
where the time goes in v6:
time: 127 us; the launch traced here: 126 us
  blocking collectives  39.2 us (31%)
  starting transfers between devices  38.6 us (30%)
  waiting for transfers between devices  28.1 us (22%)
  Pallas kernels  11.4 us (9%)
  local copies, waits for them, and re-layouts  4.03 us (3%)
  other arithmetic  2.47 us (2%)
    all_to_all x4, starting transfers between devices, spread(): return lax.all_to_all(copies, axis, 0, 0)  32.1 us
    all_to_all x4, waiting for transfers between devices, spread(): return lax.all_to_all(copies, axis, 0, 0)  24.9 us
    all_to_all x1, blocking collectives, body(): terms = lax.all_to_all(copies, 'tm', 0, 0)  17.4 us
    all_to_all x1, blocking collectives, spread(): return lax.all_to_all(copies, axis, 0, 0)  14.5 us
    all_to_all x1, blocking collectives, reduce_rows(): quarter = jnp.sum(lax.all_to_all(parts, 'near', 0, 0).astype(F32), axis=0)  7.19 us
    all_to_all x1, starting transfers between devices, reduce_rows(): quarter = jnp.sum(lax.all_to_all(parts, 'near', 0, 0).astype(F32), axis=0)  6.59 us
    pallas_call x1, Pallas kernels, likelihood(): pl.pallas_call(likelihood_kernel, in_specs=[IN_VMEM, IN_VMEM, IN_HBM], ou...  4.1 us
    pallas_call x1, Pallas kernels, read_in(): pl.pallas_call(read_kernel, in_specs=[IN_HBM, IN_HBM], out_specs=IN_VMEM,...  3.93 us
  transfers between devices with their start and end apart: 5, of which 5 were waited for; matrix products, arithmetic and copies ran while one was open for 2% of the time, Pallas kernels for 3%

profile of v6, /device:TPU:1, one launch (start us, length us, event | category | flops | bytes accessed | tf_op | source)
XLA Modules:
  0.0 125.8 jit_solution(9656155202129796397)
XLA Ops:
  0.7 3.9 %read_in.1 = bf16[4,64,256]{2,1,0:T(8,128)(2,1)} custom-call(s32[4096,256]{1,0:T(8,128)} %counts_far.3, bf16[4096,256]{1,0:T(8,128)(2,1)} %weights.1), custom_call_target="tpu_custom_call" | custom-call | tf_op jit(solution)/shard_map/read_in/pallas_call | solution.py:61
  4.6 6.6 %all-to-all-start = ((bf16[4,64,256]{2,1,0:T(8,128)(2,1)}), bf16[4,64,256]{2,1,0:T(8,128)(2,1)S(1)}, u32[]{:S(2)}, u32[]{:S(2)}) async-start(bf16[4,64,256]{2,1,0:T(8,128)(2,1)} %read_in.1), calls=%async_computation | async-start | bytes 262144 | tf_op jit(solution)/shard_map/all_to_all | solution.py:34
  11.2 0.2 select_reduce_fusion.1
  11.4 0.6 slice.13
  12.0 0.7 pad.2.clone
  12.7 3.2 %all-to-all-done = bf16[4,64,256]{2,1,0:T(8,128)(2,1)S(1)} async-done(((bf16[4,64,256]{2,1,0:T(8,128)(2,1)}), bf16[4,64,256]{2,1,0:T(8,128)(2,1)S(1)}, u32[]{:S(2)}, u32[]{:S(2)}) %all-to-all-start) | async-done | bytes 131104 | tf_op jit(solution)/shard_map/all_to_all | solution.py:34
  16.0 0.7 broadcast_in_dim.97
  16.7 12.5 %all-to-all-start.1 = ((bf16[4,64,256]{2,1,0:T(8,128)(2,1)}), bf16[4,64,256]{2,1,0:T(8,128)(2,1)S(1)}, u32[]{:S(2)}, u32[]{:S(2)}) async-start(bf16[4,64,256]{2,1,0:T(8,128)(2,1)} %broadcast_in_dim.97), calls=%async_computation.1 | async-start | bytes 262144 | tf_op jit(solution)/shard_map/all_to_all | solution.py:30
  29.2 12.1 %all-to-all-done.1 = bf16[4,64,256]{2,1,0:T(8,128)(2,1)S(1)} async-done(((bf16[4,64,256]{2,1,0:T(8,128)(2,1)}), bf16[4,64,256]{2,1,0:T(8,128)(2,1)S(1)}, u32[]{:S(2)}, u32[]{:S(2)}) %all-to-all-start.1) | async-done | bytes 131104 | tf_op jit(solution)/shard_map/all_to_all | solution.py:30
  41.4 0.1 multiply_reduce_fusion.3
  41.6 0.7 broadcast_in_dim.101
  42.3 3.5 %all-to-all-start.2 = ((bf16[4,64,256]{2,1,0:T(8,128)(2,1)}), bf16[4,64,256]{2,1,0:T(8,128)(2,1)S(1)}, u32[]{:S(2)}, u32[]{:S(2)}) async-start(bf16[4,64,256]{2,1,0:T(8,128)(2,1)} %broadcast_in_dim.101), calls=%async_computation.2 | async-start | bytes 262144 | tf_op jit(solution)/shard_map/all_to_all | solution.py:30
  45.7 0.7 broadcast_subtract_fusion
  46.4 4.1 %all-to-all-done.2 = bf16[4,64,256]{2,1,0:T(8,128)(2,1)S(1)} async-done(((bf16[4,64,256]{2,1,0:T(8,128)(2,1)}), bf16[4,64,256]{2,1,0:T(8,128)(2,1)S(1)}, u32[]{:S(2)}, u32[]{:S(2)}) %all-to-all-start.2) | async-done | bytes 131104 | tf_op jit(solution)/shard_map/all_to_all | solution.py:30
  50.5 0.2 multiply_reduce_fusion.2
  50.8 0.6 broadcast_in_dim.104
  51.4 12.6 %all-to-all-start.3 = ((f32[32,3,128]{2,1,0:T(4,128)}), f32[32,3,128]{2,1,0:T(4,128)S(1)}, u32[]{:S(2)}, u32[]{:S(2)}) async-start(f32[32,3,128]{2,1,0:T(4,128)} %broadcast_in_dim.104), calls=%async_computation.3 | async-start | bytes 131072 | tf_op jit(solution)/shard_map/all_to_all | solution.py:30
  64.1 7.3 %all-to-all-done.3 = f32[32,3,128]{2,1,0:T(4,128)S(1)} async-done(((f32[32,3,128]{2,1,0:T(4,128)}), f32[32,3,128]{2,1,0:T(4,128)S(1)}, u32[]{:S(2)}, u32[]{:S(2)}) %all-to-all-start.3) | async-done | bytes 49184 | tf_op jit(solution)/shard_map/all_to_all | solution.py:30
  71.4 0.2 multiply_reduce_fusion
  71.7 0.1 multiply_reduce_fusion.4
  71.8 0.1 multiply_reduce_fusion.5
  71.9 0.4 fusion.5
  72.4 0.4 fusion
  72.8 7.2 %all_to_all.40 = bf16[4,64,256]{2,1,0:T(8,128)(2,1)S(1)} all-to-all(bf16[4,64,256]{2,1,0:T(8,128)(2,1)S(1)} %bitcast.25), channel_id=1, replica_groups=mesh['far'=4,'near'=4,'tm'=32] {'near'}, dimensions={0} | all-to-all | bytes 262144 | tf_op jit(solution)/shard_map/all_to_all | solution.py:34
  80.0 14.5 %all_to_all.41 = bf16[4,64,256]{2,1,0:T(8,128)(2,1)S(1)} all-to-all(bf16[4,64,256]{2,1,0:T(8,128)(2,1)S(1)} %broadcast_in_dim.107), channel_id=1, replica_groups=mesh['far'=4,'near'=4,'tm'=32] {'far'}, dimensions={0} | all-to-all | bytes 262144 | tf_op jit(solution)/shard_map/all_to_all | solution.py:30
  94.7 0.7 broadcast_in_dim.108
  95.3 3.5 %all-to-all-start.6 = ((bf16[4,64,256]{2,1,0:T(8,128)(2,1)}), bf16[4,64,256]{2,1,0:T(8,128)(2,1)S(1)}, u32[]{:S(2)}, u32[]{:S(2)}) async-start(bf16[4,64,256]{2,1,0:T(8,128)(2,1)} %broadcast_in_dim.108), calls=%async_computation.6 | async-start | bytes 262144 | tf_op jit(solution)/shard_map/all_to_all | solution.py:30
  98.8 3.4 %turn.1.turned_far = bf16[8,256,512]{2,1,0:T(8,128)(2,1)} custom-call(s32[4096,256]{1,0:T(8,128)} %counts_far.3, bf16[64,256]{1,0:T(8,128)(2,1)S(1)} %multiply_convert_fusion.6.after), custom_call_target="tpu_custom_call" | custom-call | tf_op jit(solution)/shard_map/turn/pallas_call | solution.py:96
  102.2 1.4 %all-to-all-done.6 = bf16[4,64,256]{2,1,0:T(8,128)(2,1)S(1)} async-done(((bf16[4,64,256]{2,1,0:T(8,128)(2,1)}), bf16[4,64,256]{2,1,0:T(8,128)(2,1)S(1)}, u32[]{:S(2)}, u32[]{:S(2)}) %all-to-all-start.6) | async-done | bytes 131104 | tf_op jit(solution)/shard_map/all_to_all | solution.py:30
  103.6 4.1 %likelihood.1 = (bf16[32,32,128]{2,1,0:T(8,128)(2,1)S(1)}, bf16[256,256]{1,0:T(8,128)(2,1)}) custom-call(bf16[256,256]{1,0:T(8,128)(2,1)S(1)} %bitcast.21, bf16[4096,256]{1,0:T(8,128)(2,1)S(1)} %copy-done.1, bf16[8,256,512]{2,1,0:T(8,128)(2,1)} %turn.1.turned_far), custom_call_target="tpu_custom_call" | custom-call | tf_op jit(solution)/shard_map/likelihood/pallas_call | solution.py:135
  107.7 17.4 %all_to_all.42 = bf16[32,32,128]{2,1,0:T(8,128)(2,1)S(1)} all-to-all(bf16[32,32,128]{2,1,0:T(8,128)(2,1)S(1)} %get-tuple-element.5), channel_id=1, replica_groups=mesh['far'=4,'near'=4,'tm'=32] {'tm'}, dimensions={0} | all-to-all | bytes 524288 | tf_op jit(solution)/shard_map/all_to_all | solution.py:219
  125.2 0.6 multiply_bitcast_fusion
  (35 shorter events, 0.6 us)
Async XLA Ops:
  0.6 71.3 %copy-start = (bf16[128,256]{1,0:T(8,128)(2,1)S(1)}, bf16[128,256]{1,0:T(8,128)(2,1)}, u32[]{:S(2)}) copy-start(bf16[128,256]{1,0:T(8,128)(2,1)} %param.12) | copy-start | bytes 196612
  0.6 10.6 %copy-start.2 = (f32[256]{0:T(256)S(1)}, f32[256]{0:T(256)}, u32[]{:S(2)}) copy-start(f32[256]{0:T(256)} %param.11) | copy-start | bytes 3076
  0.7 45.1 %copy-start.3 = (f32[128]{0:T(128)S(1)}, f32[128]{0:T(128)}, u32[]{:S(2)}) copy-start(f32[128]{0:T(128)} %param.10) | copy-start | bytes 1540
  0.7 49.8 %copy-start.4 = (bf16[256,128]{1,0:T(8,128)(2,1)S(1)}, bf16[256,128]{1,0:T(8,128)(2,1)}, u32[]{:S(2)}) copy-start(bf16[256,128]{1,0:T(8,128)(2,1)} %param.9) | copy-start | bytes 196612
  4.6 67.7 %copy-start.5 = (bf16[128,256]{1,0:T(8,128)(2,1)S(1)}, bf16[128,256]{1,0:T(8,128)(2,1)}, u32[]{:S(2)}) copy-start(bf16[128,256]{1,0:T(8,128)(2,1)} %param.13) | copy-start | bytes 196612
  4.6 11.4 %all-to-all-start = ((bf16[4,64,256]{2,1,0:T(8,128)(2,1)}), bf16[4,64,256]{2,1,0:T(8,128)(2,1)S(1)}, u32[]{:S(2)}, u32[]{:S(2)}) async-start(bf16[4,64,256]{2,1,0:T(8,128)(2,1)} %read_in.1), calls=%async_computation | async-start | bytes 262144 | tf_op jit(solution)/shard_map/all_to_all | solution.py:34
  16.7 24.7 %all-to-all-start.1 = ((bf16[4,64,256]{2,1,0:T(8,128)(2,1)}), bf16[4,64,256]{2,1,0:T(8,128)(2,1)S(1)}, u32[]{:S(2)}, u32[]{:S(2)}) async-start(bf16[4,64,256]{2,1,0:T(8,128)(2,1)} %broadcast_in_dim.97), calls=%async_computation.1 | async-start | bytes 262144 | tf_op jit(solution)/shard_map/all_to_all | solution.py:30
  42.3 8.2 %all-to-all-start.2 = ((bf16[4,64,256]{2,1,0:T(8,128)(2,1)}), bf16[4,64,256]{2,1,0:T(8,128)(2,1)S(1)}, u32[]{:S(2)}, u32[]{:S(2)}) async-start(bf16[4,64,256]{2,1,0:T(8,128)(2,1)} %broadcast_in_dim.101), calls=%async_computation.2 | async-start | bytes 262144 | tf_op jit(solution)/shard_map/all_to_all | solution.py:30
  51.4 19.9 %all-to-all-start.3 = ((f32[32,3,128]{2,1,0:T(4,128)}), f32[32,3,128]{2,1,0:T(4,128)S(1)}, u32[]{:S(2)}, u32[]{:S(2)}) async-start(f32[32,3,128]{2,1,0:T(4,128)} %broadcast_in_dim.104), calls=%async_computation.3 | async-start | bytes 131072 | tf_op jit(solution)/shard_map/all_to_all | solution.py:30
  95.3 8.3 %all-to-all-start.6 = ((bf16[4,64,256]{2,1,0:T(8,128)(2,1)}), bf16[4,64,256]{2,1,0:T(8,128)(2,1)S(1)}, u32[]{:S(2)}, u32[]{:S(2)}) async-start(bf16[4,64,256]{2,1,0:T(8,128)(2,1)} %broadcast_in_dim.108), calls=%async_computation.6 | async-start | bytes 262144 | tf_op jit(solution)/shard_map/all_to_all | solution.py:30
  98.8 4.8 %copy-start.1 = (bf16[4096,256]{1,0:T(8,128)(2,1)S(1)}, bf16[4096,256]{1,0:T(8,128)(2,1)}, u32[]{:S(2)}) copy-start(bf16[4096,256]{1,0:T(8,128)(2,1)} %weights.1) | copy-start | bytes 6291460

commit v7 on v6

--- a/solution.py
+++ b/solution.py
@@ -14,6 +14,7 @@
 ROOM = 14 * 1024 * 1024
 IN_VMEM = pl.BlockSpec(memory_space=pltpu.VMEM)
 IN_HBM = pl.BlockSpec(memory_space=pltpu.HBM)
+ANYWHERE = pl.BlockSpec(memory_space=pl.ANY)
 
 
 def far(array):
@@ -73,81 +74,65 @@
     )(far(spikes), far(read_weight))
 
 
-def turn_kernel(counts_far, after, turned_far, counts, turned, arrived, left):
-    chunks, _, tall = turned.shape
-    coming, leaving = [], []
+def narrow_kernel(counts_far, after, narrow, counts, arrived):
+    chunks = arrived.shape[0]
+    tall = counts.shape[0] // chunks
+    coming = []
     for k in range(chunks):
         here = pl.ds(k * tall, tall)
         coming.append(pltpu.make_async_copy(counts_far.at[here], counts.at[here], arrived.at[k]))
-        leaving.append(pltpu.make_async_copy(turned.at[k], turned_far.at[k], left.at[k]))
         coming[-1].start()
     for k in range(chunks):
         coming[k].wait()
-        turned[k] = counts[k * tall : (k + 1) * tall, :].astype(F32).astype(BF16).T
-        leaving[k].start()
-    for one in leaving:
-        one.wait()
-
-
-def turn(spikes, after):
-    neurons, bins = spikes.shape
-    chunks = 8
-    turned = (chunks, bins, neurons // chunks)
+        here = slice(k * tall, (k + 1) * tall)
+        narrow[here, :] = counts[here, :].astype(jnp.int8)
+
+
+def narrowed(spikes, after):
     return pl.pallas_call(
-        turn_kernel,
-        in_specs=[IN_HBM, pl.BlockSpec(memory_space=pl.ANY)],
-        out_specs=IN_HBM,
-        out_shape=pltpu.HBM(turned, BF16),
+        narrow_kernel,
+        in_specs=[IN_HBM, ANYWHERE],
+        out_specs=IN_VMEM,
+        out_shape=pltpu.VMEM(spikes.shape, jnp.int8),
         scratch_shapes=[
-            pltpu.VMEM((neurons, bins), spikes.dtype),
-            pltpu.VMEM(turned, BF16),
-            pltpu.SemaphoreType.DMA((chunks,)),
-            pltpu.SemaphoreType.DMA((chunks,)),
+            pltpu.VMEM(spikes.shape, spikes.dtype),
+            pltpu.SemaphoreType.DMA((8,)),
         ],
         compiler_params=pltpu.CompilerParams(vmem_limit_bytes=ROOM),
-        name="turn",
+        name="narrow",
     )(far(spikes), after)
 
 
-def likelihood_kernel(latent, weights, turned_far, copies, out_latent, sums, turned, arrived):
-    chunks, _, wide = turned.shape
-    pieces = wide // LANES
-    coming = [pltpu.make_async_copy(turned_far.at[k], turned.at[k], arrived.at[k]) for k in range(chunks)]
-    for one in coming:
-        one.start()
+def likelihood_kernel(latent, weights, counts, copies, out_latent, sums):
+    wide = 4 * LANES
     rows = latent[...]
     out_latent[...] = rows
-    for k in range(chunks):
-        log_rate = lax.dot_general(
-            rows, weights[k * wide : (k + 1) * wide, :], ROWS, preferred_element_type=F32
-        )
-        coming[k].wait()
-        terms = jnp.exp(log_rate) - turned[k].astype(F32) * log_rate
-        one = jnp.sum(terms, axis=0, keepdims=True)
-        for j in range(pieces):
-            sums[pieces * k + j : pieces * k + j + 1, :] = one[:, j * LANES : (j + 1) * LANES]
+    for k in range(weights.shape[0] // wide):
+        here = slice(k * wide, (k + 1) * wide)
+        log_rate = lax.dot_general(weights[here, :], rows, ROWS, preferred_element_type=F32)
+        terms = jnp.exp(log_rate) - counts[here, :].astype(F32) * log_rate
+        folded = sum(terms[:, j : j + LANES] for j in range(0, rows.shape[0], LANES))
+        for j in range(4):
+            turned = folded[j * LANES : (j + 1) * LANES, :].T
+            sums[4 * k + j : 4 * k + j + 1, :] = jnp.sum(turned, axis=0, keepdims=True)
     small = sums[...].astype(BF16)
     copies[...] = jnp.broadcast_to(small[None], copies.shape)
 
 
-def likelihood(latent, read_weight, turned, blocks):
+def likelihood(latent, read_weight, spikes, blocks):
     neurons = read_weight.shape[0]
     return pl.pallas_call(
         likelihood_kernel,
-        in_specs=[IN_VMEM, IN_VMEM, IN_HBM],
+        in_specs=[IN_VMEM, IN_VMEM, IN_VMEM],
         out_specs=[IN_VMEM, IN_VMEM],
         out_shape=[
             jax.ShapeDtypeStruct((blocks, neurons // LANES, LANES), BF16),
             jax.ShapeDtypeStruct(latent.shape, BF16),
         ],
-        scratch_shapes=[
-            pltpu.VMEM((neurons // LANES, LANES), F32),
-            pltpu.VMEM(turned.shape, BF16),
-            pltpu.SemaphoreType.DMA((turned.shape[0],)),
-        ],
+        scratch_shapes=[pltpu.VMEM((neurons // LANES, LANES), F32)],
         compiler_params=pltpu.CompilerParams(vmem_limit_bytes=ROOM),
         name="likelihood",
-    )(near(latent), near(read_weight), far(turned))
+    )(near(latent), near(read_weight), near(spikes))
 
 
 def body(spikes, read_weight, in_proj, decay_rate, gate, out_fwd, out_bwd):
@@ -179,7 +164,6 @@
     power = jnp.mean(rows * rows, axis=-1, keepdims=True) + 1e-05
     normed_rows = (rows * lax.rsqrt(power)).astype(BF16)
     normed = spread(normed_rows, "near").reshape(bins, -1)
-    turned = turn(spikes, normed_rows)
 
     drive = jnp.dot(normed, in_proj, preferred_element_type=F32)
     sent = jnp.stack(
@@ -211,11 +195,13 @@
     backward = (state_bwd + cum_bwd * enter_bwd[None, :]).astype(BF16)
     mixed = jnp.dot(forward, out_fwd, preferred_element_type=F32)
     mixed = mixed + jnp.dot(backward, out_bwd, preferred_element_type=F32)
+    counts = narrowed(spikes, sent)
+    mixed, counts = lax.optimization_barrier((mixed, counts))
     mixed_rows = reduce_rows(mixed.astype(BF16).reshape(quad, bins // quad, -1))
     latent_rows = (normed_rows.astype(F32) + mixed_rows).astype(BF16)
     latent = spread(latent_rows, "near").reshape(bins, -1)
 
-    copies, latent = likelihood(latent, read_weight, turned, blocks)
+    copies, latent = likelihood(latent, read_weight, counts, blocks)
     terms = lax.all_to_all(copies, "tm", 0, 0)
     nll = jnp.sum(terms.astype(F32), axis=0).reshape(-1) * (1.0 / (bins * blocks))
     return (latent, nll)

time: 127 us -> 126 us (level)
  blocking collectives: 39.2 us -> 46.9 us
  waiting for transfers between devices: 28.1 us -> 24.3 us
  starting transfers between devices: 38.6 us -> 35 us
  Pallas kernels: 11.4 us -> 8.11 us
  matrix products: 1.08 us -> 4.33 us
    all_to_all x1 -> x2, blocking collectives: 14.5 us -> 22.6 us  [spread(): return lax.all_to_all(copies, axis, 0, 0)]
    all_to_all x4 -> x3, waiting for transfers between devices: 24.9 us -> 21.1 us  [spread(): return lax.all_to_all(copies, axis, 0, 0)]
    all_to_all x4 -> x3, starting transfers between devices: 32.1 us -> 28.6 us  [spread(): return lax.all_to_all(copies, axis, 0, 0)]
    pallas_call x2, Pallas kernels: 7.5 us -> 4.18 us  [the longest x1 2.39 us: narrowed(): pl.pallas_call(narrow_kernel, in_specs=[IN_HBM, ANYWHERE], out_specs=IN_V...]
    dot_general x1, matrix products: 0.42 us -> 2.02 us  [body(): mixed = jnp.dot(forward, out_fwd, preferred_element_type=F32)]
  transfers between devices with their start and end apart: 5 -> 4, of which waited for: 5 -> 4; matrix products, arithmetic and copies ran while one was open for 2% -> 2% of each run, Pallas kernels for 3% -> 2%
where the time goes in v7:
time: 126 us; the launch traced here: 125 us
  blocking collectives  46.9 us (37%)
  starting transfers between devices  35 us (28%)
  waiting for transfers between devices  24.3 us (19%)
  Pallas kernels  8.11 us (6%)
  matrix products  4.33 us (3%)
  local copies, waits for them, and re-layouts  3.37 us (3%)
  other arithmetic  2.47 us (2%)
    all_to_all x3, starting transfers between devices, spread(): return lax.all_to_all(copies, axis, 0, 0)  28.6 us
    all_to_all x2, blocking collectives, spread(): return lax.all_to_all(copies, axis, 0, 0)  22.6 us
    all_to_all x3, waiting for transfers between devices, spread(): return lax.all_to_all(copies, axis, 0, 0)  21.1 us
    all_to_all x1, blocking collectives, body(): terms = lax.all_to_all(copies, 'tm', 0, 0)  17.1 us
    all_to_all x1, blocking collectives, reduce_rows(): quarter = jnp.sum(lax.all_to_all(parts, 'near', 0, 0).astype(F32), axis=0)  7.19 us
    all_to_all x1, starting transfers between devices, reduce_rows(): quarter = jnp.sum(lax.all_to_all(parts, 'near', 0, 0).astype(F32), axis=0)  6.45 us
    pallas_call x1, Pallas kernels, read_in(): pl.pallas_call(read_kernel, in_specs=[IN_HBM, IN_HBM], out_specs=IN_VMEM,...  3.93 us
    all_to_all x1, waiting for transfers between devices, reduce_rows(): quarter = jnp.sum(lax.all_to_all(parts, 'near', 0, 0).astype(F32), axis=0)  3.25 us
  transfers between devices with their start and end apart: 4, of which 4 were waited for; matrix products, arithmetic and copies ran while one was open for 2% of the time, Pallas kernels for 2%

profile of v7, /device:TPU:1, one launch (start us, length us, event | category | flops | bytes accessed | tf_op | source)
XLA Modules:
  0.0 125.4 jit_solution(2394987665686119686)
XLA Ops:
  0.7 3.9 %read_in.1 = bf16[4,64,256]{2,1,0:T(8,128)(2,1)} custom-call(s32[4096,256]{1,0:T(8,128)} %counts_far.3, bf16[4096,256]{1,0:T(8,128)(2,1)} %weights.1), custom_call_target="tpu_custom_call" | custom-call | tf_op jit(solution)/shard_map/read_in/pallas_call | solution.py:62
  4.6 6.5 %all-to-all-start = ((bf16[4,64,256]{2,1,0:T(8,128)(2,1)}), bf16[4,64,256]{2,1,0:T(8,128)(2,1)S(1)}, u32[]{:S(2)}, u32[]{:S(2)}) async-start(bf16[4,64,256]{2,1,0:T(8,128)(2,1)} %read_in.1), calls=%async_computation | async-start | bytes 262144 | tf_op jit(solution)/shard_map/all_to_all | solution.py:35
  11.1 0.2 select_reduce_fusion.1
  11.2 0.6 slice.13
  11.8 0.7 pad.2.clone
  12.6 3.2 %all-to-all-done = bf16[4,64,256]{2,1,0:T(8,128)(2,1)S(1)} async-done(((bf16[4,64,256]{2,1,0:T(8,128)(2,1)}), bf16[4,64,256]{2,1,0:T(8,128)(2,1)S(1)}, u32[]{:S(2)}, u32[]{:S(2)}) %all-to-all-start) | async-done | bytes 131104 | tf_op jit(solution)/shard_map/all_to_all | solution.py:35
  15.9 0.7 broadcast_in_dim.97
  16.5 12.5 %all-to-all-start.1 = ((bf16[4,64,256]{2,1,0:T(8,128)(2,1)}), bf16[4,64,256]{2,1,0:T(8,128)(2,1)S(1)}, u32[]{:S(2)}, u32[]{:S(2)}) async-start(bf16[4,64,256]{2,1,0:T(8,128)(2,1)} %broadcast_in_dim.97), calls=%async_computation.1 | async-start | bytes 262144 | tf_op jit(solution)/shard_map/all_to_all | solution.py:31
  29.1 12.1 %all-to-all-done.1 = bf16[4,64,256]{2,1,0:T(8,128)(2,1)S(1)} async-done(((bf16[4,64,256]{2,1,0:T(8,128)(2,1)}), bf16[4,64,256]{2,1,0:T(8,128)(2,1)S(1)}, u32[]{:S(2)}, u32[]{:S(2)}) %all-to-all-start.1) | async-done | bytes 131104 | tf_op jit(solution)/shard_map/all_to_all | solution.py:31
  41.2 0.1 multiply_reduce_fusion.3
  41.4 0.7 broadcast_in_dim.101
  42.1 3.5 %all-to-all-start.2 = ((bf16[4,64,256]{2,1,0:T(8,128)(2,1)}), bf16[4,64,256]{2,1,0:T(8,128)(2,1)S(1)}, u32[]{:S(2)}, u32[]{:S(2)}) async-start(bf16[4,64,256]{2,1,0:T(8,128)(2,1)} %broadcast_in_dim.101), calls=%async_computation.2 | async-start | bytes 262144 | tf_op jit(solution)/shard_map/all_to_all | solution.py:31
  45.6 0.7 broadcast_subtract_fusion
  46.3 4.1 %all-to-all-done.2 = bf16[4,64,256]{2,1,0:T(8,128)(2,1)S(1)} async-done(((bf16[4,64,256]{2,1,0:T(8,128)(2,1)}), bf16[4,64,256]{2,1,0:T(8,128)(2,1)S(1)}, u32[]{:S(2)}, u32[]{:S(2)}) %all-to-all-start.2) | async-done | bytes 131104 | tf_op jit(solution)/shard_map/all_to_all | solution.py:31
  50.3 0.8 multiply_reduce_fusion.2
  51.3 0.6 broadcast_in_dim.104
  51.9 12.6 %all-to-all-start.3 = ((f32[32,3,128]{2,1,0:T(4,128)}), f32[32,3,128]{2,1,0:T(4,128)S(1)}, u32[]{:S(2)}, u32[]{:S(2)}) async-start(f32[32,3,128]{2,1,0:T(4,128)} %broadcast_in_dim.104), calls=%async_computation.3 | async-start | bytes 131072 | tf_op jit(solution)/shard_map/all_to_all | solution.py:31
  64.5 2.4 %narrow.1.counts = s8[4096,256]{1,0:T(32,128)(4,1)S(1)} custom-call(s32[4096,256]{1,0:T(8,128)} %counts_far.3, f32[3,128]{1,0:T(4,128)S(1)} %maximum_maximum_fusion.after), custom_call_target="tpu_custom_call" | custom-call | tf_op jit(solution)/shard_map/narrow/pallas_call | solution.py:92
  66.9 4.9 %all-to-all-done.3 = f32[32,3,128]{2,1,0:T(4,128)S(1)} async-done(((f32[32,3,128]{2,1,0:T(4,128)}), f32[32,3,128]{2,1,0:T(4,128)S(1)}, u32[]{:S(2)}, u32[]{:S(2)}) %all-to-all-start.3) | async-done | bytes 49184 | tf_op jit(solution)/shard_map/all_to_all | solution.py:31
  71.9 0.2 multiply_reduce_fusion
  72.1 0.1 select_reduce_fusion.2
  72.2 0.1 multiply_reduce_fusion.4
  72.3 0.1 multiply_reduce_fusion.5
  72.4 2.0 %fusion.4 = f32[256,256]{1,0:T(8,128)} fusion(bf16[128,256]{1,0:T(8,128)(2,1)S(1)} %copy-done, f32[256]{0:T(256)S(1)} %get-tuple-element.15, f32[256]{0:T(256)S(1)} %get-tuple-element.14, f32[256,128]{1,0:T(8,128)} %get-tuple-element.23, f32[128]{0:T(128)S(1)} %multiply_reduce_fusion.5, f32[256]{0:T(256)S(1)} %get-tuple-element.27, ...), kind=kOutput, calls=%fused_computation.7 | convolution fusion | flops 34242560 | bytes 465408 | tf_op jit(solution)/shard_map/dot_general | solution.py:196
  74.4 1.5 %convolution_add_fusion = bf16[256,256]{1,0:T(8,128)(2,1)S(1)} fusion(f32[256,256]{1,0:T(8,128)} %fusion.4, bf16[128,256]{1,0:T(8,128)(2,1)} %param.13, f32[256]{0:T(256)S(1)} %get-tuple-element.17, f32[256]{0:T(256)S(1)} %get-tuple-element.21, f32[256,128]{1,0:T(8,128)} %get-tuple-element.23, f32[128]{0:T(128)S(1)} %get-tuple-element.12, f32[256]{0:T(256)S(1)} %fusion.46, ...), kind=kOutput, calls=%fused_computation | convolution fusion | flops 34373632 | bytes 597504 | tf_op jit(solution)/shard_map/dot_general | solution.py:197
  75.9 7.2 %all_to_all.40 = bf16[4,64,256]{2,1,0:T(8,128)(2,1)S(1)} all-to-all(bf16[4,64,256]{2,1,0:T(8,128)(2,1)S(1)} %bitcast.25), channel_id=1, replica_groups=mesh['far'=4,'near'=4,'tm'=32] {'near'}, dimensions={0} | all-to-all | bytes 262144 | tf_op jit(solution)/shard_map/all_to_all | solution.py:35
  83.1 14.5 %all_to_all.41 = bf16[4,64,256]{2,1,0:T(8,128)(2,1)S(1)} all-to-all(bf16[4,64,256]{2,1,0:T(8,128)(2,1)S(1)} %broadcast_in_dim.107), channel_id=1, replica_groups=mesh['far'=4,'near'=4,'tm'=32] {'far'}, dimensions={0} | all-to-all | bytes 262144 | tf_op jit(solution)/shard_map/all_to_all | solution.py:31
  97.7 0.1 add_convert_fusion
  97.8 8.1 %all_to_all.42 = bf16[4,64,256]{2,1,0:T(8,128)(2,1)S(1)} all-to-all(bf16[4,64,256]{2,1,0:T(8,128)(2,1)S(1)} %broadcast_in_dim.108), channel_id=1, replica_groups=mesh['far'=4,'near'=4,'tm'=32] {'near'}, dimensions={0} | all-to-all | bytes 262144 | tf_op jit(solution)/shard_map/all_to_all | solution.py:31
  105.8 1.8 %likelihood.1 = (bf16[32,32,128]{2,1,0:T(8,128)(2,1)S(1)}, bf16[256,256]{1,0:T(8,128)(2,1)}) custom-call(bf16[256,256]{1,0:T(8,128)(2,1)S(1)} %bitcast.21, bf16[4096,256]{1,0:T(8,128)(2,1)S(1)} %copy-done.1, s8[4096,256]{1,0:T(32,128)(4,1)S(1)} %narrow.1.counts), custom_call_target="tpu_custom_call" | custom-call | tf_op jit(solution)/shard_map/likelihood/pallas_call | solution.py:124
  107.6 17.1 %all_to_all.43 = bf16[32,32,128]{2,1,0:T(8,128)(2,1)S(1)} all-to-all(bf16[32,32,128]{2,1,0:T(8,128)(2,1)S(1)} %get-tuple-element.9), channel_id=1, replica_groups=mesh['far'=4,'near'=4,'tm'=32] {'tm'}, dimensions={0} | all-to-all | bytes 524288 | tf_op jit(solution)/shard_map/all_to_all | solution.py:205
  124.8 0.6 multiply_bitcast_fusion
  (34 shorter events, 0.4 us)
Async XLA Ops:
  0.6 71.7 %copy-start = (bf16[128,256]{1,0:T(8,128)(2,1)S(1)}, bf16[128,256]{1,0:T(8,128)(2,1)}, u32[]{:S(2)}) copy-start(bf16[128,256]{1,0:T(8,128)(2,1)} %param.12) | copy-start | bytes 196612
  0.6 10.4 %copy-start.2 = (f32[256]{0:T(256)S(1)}, f32[256]{0:T(256)}, u32[]{:S(2)}) copy-start(f32[256]{0:T(256)} %param.11) | copy-start | bytes 3076
  0.7 44.9 %copy-start.3 = (f32[128]{0:T(128)S(1)}, f32[128]{0:T(128)}, u32[]{:S(2)}) copy-start(f32[128]{0:T(128)} %param.10) | copy-start | bytes 1540
  0.7 49.7 %copy-start.4 = (bf16[256,128]{1,0:T(8,128)(2,1)S(1)}, bf16[256,128]{1,0:T(8,128)(2,1)}, u32[]{:S(2)}) copy-start(bf16[256,128]{1,0:T(8,128)(2,1)} %param.9) | copy-start | bytes 196612
  4.6 11.2 %all-to-all-start = ((bf16[4,64,256]{2,1,0:T(8,128)(2,1)}), bf16[4,64,256]{2,1,0:T(8,128)(2,1)S(1)}, u32[]{:S(2)}, u32[]{:S(2)}) async-start(bf16[4,64,256]{2,1,0:T(8,128)(2,1)} %read_in.1), calls=%async_computation | async-start | bytes 262144 | tf_op jit(solution)/shard_map/all_to_all | solution.py:35
  16.5 24.7 %all-to-all-start.1 = ((bf16[4,64,256]{2,1,0:T(8,128)(2,1)}), bf16[4,64,256]{2,1,0:T(8,128)(2,1)S(1)}, u32[]{:S(2)}, u32[]{:S(2)}) async-start(bf16[4,64,256]{2,1,0:T(8,128)(2,1)} %broadcast_in_dim.97), calls=%async_computation.1 | async-start | bytes 262144 | tf_op jit(solution)/shard_map/all_to_all | solution.py:31
  42.1 8.2 %all-to-all-start.2 = ((bf16[4,64,256]{2,1,0:T(8,128)(2,1)}), bf16[4,64,256]{2,1,0:T(8,128)(2,1)S(1)}, u32[]{:S(2)}, u32[]{:S(2)}) async-start(bf16[4,64,256]{2,1,0:T(8,128)(2,1)} %broadcast_in_dim.101), calls=%async_computation.2 | async-start | bytes 262144 | tf_op jit(solution)/shard_map/all_to_all | solution.py:31
  45.6 28.8 %copy-start.5 = (f32[128]{0:T(128)}, f32[128]{0:T(128)S(1)}, u32[]{:S(2)}) copy-start(f32[128]{0:T(128)S(1)} %negate_sqrt_fusion) | copy-start | bytes 1540
  51.9 19.9 %all-to-all-start.3 = ((f32[32,3,128]{2,1,0:T(4,128)}), f32[32,3,128]{2,1,0:T(4,128)S(1)}, u32[]{:S(2)}, u32[]{:S(2)}) async-start(f32[32,3,128]{2,1,0:T(4,128)} %broadcast_in_dim.104), calls=%async_computation.3 | async-start | bytes 131072 | tf_op jit(solution)/shard_map/all_to_all | solution.py:31
  64.5 41.3 %copy-start.1 = (bf16[4096,256]{1,0:T(8,128)(2,1)S(1)}, bf16[4096,256]{1,0:T(8,128)(2,1)}, u32[]{:S(2)}) copy-start(bf16[4096,256]{1,0:T(8,128)(2,1)} %weights.1) | copy-start | bytes 6291460

commit v8 on v7

--- a/solution.py
+++ b/solution.py
@@ -195,12 +195,11 @@
     backward = (state_bwd + cum_bwd * enter_bwd[None, :]).astype(BF16)
     mixed = jnp.dot(forward, out_fwd, preferred_element_type=F32)
     mixed = mixed + jnp.dot(backward, out_bwd, preferred_element_type=F32)
-    counts = narrowed(spikes, sent)
-    mixed, counts = lax.optimization_barrier((mixed, counts))
     mixed_rows = reduce_rows(mixed.astype(BF16).reshape(quad, bins // quad, -1))
     latent_rows = (normed_rows.astype(F32) + mixed_rows).astype(BF16)
     latent = spread(latent_rows, "near").reshape(bins, -1)
 
+    counts = narrowed(spikes, normed_rows)
     copies, latent = likelihood(latent, read_weight, counts, blocks)
     terms = lax.all_to_all(copies, "tm", 0, 0)
     nll = jnp.sum(terms.astype(F32), axis=0).reshape(-1) * (1.0 / (bins * blocks))

time: 126 us -> 124 us (0.984)
  blocking collectives: 46.9 us -> 39.3 us
  waiting for transfers between devices: 24.3 us -> 29.3 us
  starting transfers between devices: 35 us -> 38.5 us
  matrix products: 4.33 us -> 1.08 us
    all_to_all x2 -> x1, blocking collectives: 22.6 us -> 14.5 us  [spread(): return lax.all_to_all(copies, axis, 0, 0)]
    all_to_all x3 -> x4, waiting for transfers between devices: 21.1 us -> 26 us  [spread(): return lax.all_to_all(copies, axis, 0, 0)]
    all_to_all x3 -> x4, starting transfers between devices: 28.6 us -> 32.1 us  [spread(): return lax.all_to_all(copies, axis, 0, 0)]
    dot_general x1, matrix products: 2.02 us -> 0.42 us  [body(): mixed = jnp.dot(forward, out_fwd, preferred_element_type=F32)]
  transfers between devices with their start and end apart: 4 -> 5, of which waited for: 4 -> 5; matrix products, arithmetic and copies ran while one was open for 2% -> 2% of each run, Pallas kernels for 2% -> 2%
where the time goes in v8:
time: 124 us; the launch traced here: 123 us
  blocking collectives  39.3 us (32%)
  starting transfers between devices  38.5 us (31%)
  waiting for transfers between devices  29.3 us (24%)
  Pallas kernels  7.95 us (6%)
  local copies, waits for them, and re-layouts  4.03 us (3%)
  other arithmetic  2.47 us (2%)
    all_to_all x4, starting transfers between devices, spread(): return lax.all_to_all(copies, axis, 0, 0)  32.1 us
    all_to_all x4, waiting for transfers between devices, spread(): return lax.all_to_all(copies, axis, 0, 0)  26 us
    all_to_all x1, blocking collectives, body(): terms = lax.all_to_all(copies, 'tm', 0, 0)  17.4 us
    all_to_all x1, blocking collectives, spread(): return lax.all_to_all(copies, axis, 0, 0)  14.5 us
    all_to_all x1, blocking collectives, reduce_rows(): quarter = jnp.sum(lax.all_to_all(parts, 'near', 0, 0).astype(F32), axis=0)  7.32 us
    all_to_all x1, starting transfers between devices, reduce_rows(): quarter = jnp.sum(lax.all_to_all(parts, 'near', 0, 0).astype(F32), axis=0)  6.46 us
    pallas_call x1, Pallas kernels, read_in(): pl.pallas_call(read_kernel, in_specs=[IN_HBM, IN_HBM], out_specs=IN_VMEM,...  3.92 us
    all_to_all x1, waiting for transfers between devices, reduce_rows(): quarter = jnp.sum(lax.all_to_all(parts, 'near', 0, 0).astype(F32), axis=0)  3.25 us
  transfers between devices with their start and end apart: 5, of which 5 were waited for; matrix products, arithmetic and copies ran while one was open for 2% of the time, Pallas kernels for 2%

profile of v8, /device:TPU:1, one launch (start us, length us, event | category | flops | bytes accessed | tf_op | source)
XLA Modules:
  0.0 123.5 jit_solution(6621009635854108255)
XLA Ops:
  0.7 3.9 %read_in.1 = bf16[4,64,256]{2,1,0:T(8,128)(2,1)} custom-call(s32[4096,256]{1,0:T(8,128)} %counts_far.3, bf16[4096,256]{1,0:T(8,128)(2,1)} %weights.1), custom_call_target="tpu_custom_call" | custom-call | tf_op jit(solution)/shard_map/read_in/pallas_call | solution.py:62
  4.6 6.5 %all-to-all-start = ((bf16[4,64,256]{2,1,0:T(8,128)(2,1)}), bf16[4,64,256]{2,1,0:T(8,128)(2,1)S(1)}, u32[]{:S(2)}, u32[]{:S(2)}) async-start(bf16[4,64,256]{2,1,0:T(8,128)(2,1)} %read_in.1), calls=%async_computation | async-start | bytes 262144 | tf_op jit(solution)/shard_map/all_to_all | solution.py:35
  11.1 0.2 select_reduce_fusion.1
  11.2 0.6 slice.13
  11.8 0.7 pad.2.clone
  12.6 3.2 %all-to-all-done = bf16[4,64,256]{2,1,0:T(8,128)(2,1)S(1)} async-done(((bf16[4,64,256]{2,1,0:T(8,128)(2,1)}), bf16[4,64,256]{2,1,0:T(8,128)(2,1)S(1)}, u32[]{:S(2)}, u32[]{:S(2)}) %all-to-all-start) | async-done | bytes 131104 | tf_op jit(solution)/shard_map/all_to_all | solution.py:35
  15.9 0.7 broadcast_in_dim.97
  16.5 12.5 %all-to-all-start.1 = ((bf16[4,64,256]{2,1,0:T(8,128)(2,1)}), bf16[4,64,256]{2,1,0:T(8,128)(2,1)S(1)}, u32[]{:S(2)}, u32[]{:S(2)}) async-start(bf16[4,64,256]{2,1,0:T(8,128)(2,1)} %broadcast_in_dim.97), calls=%async_computation.1 | async-start | bytes 262144 | tf_op jit(solution)/shard_map/all_to_all | solution.py:31
  29.1 12.1 %all-to-all-done.1 = bf16[4,64,256]{2,1,0:T(8,128)(2,1)S(1)} async-done(((bf16[4,64,256]{2,1,0:T(8,128)(2,1)}), bf16[4,64,256]{2,1,0:T(8,128)(2,1)S(1)}, u32[]{:S(2)}, u32[]{:S(2)}) %all-to-all-start.1) | async-done | bytes 131104 | tf_op jit(solution)/shard_map/all_to_all | solution.py:31
  41.2 0.1 multiply_reduce_fusion.3
  41.4 0.7 broadcast_in_dim.101
  42.1 3.5 %all-to-all-start.2 = ((bf16[4,64,256]{2,1,0:T(8,128)(2,1)}), bf16[4,64,256]{2,1,0:T(8,128)(2,1)S(1)}, u32[]{:S(2)}, u32[]{:S(2)}) async-start(bf16[4,64,256]{2,1,0:T(8,128)(2,1)} %broadcast_in_dim.101), calls=%async_computation.2 | async-start | bytes 262144 | tf_op jit(solution)/shard_map/all_to_all | solution.py:31
  45.6 0.7 broadcast_subtract_fusion
  46.3 4.1 %all-to-all-done.2 = bf16[4,64,256]{2,1,0:T(8,128)(2,1)S(1)} async-done(((bf16[4,64,256]{2,1,0:T(8,128)(2,1)}), bf16[4,64,256]{2,1,0:T(8,128)(2,1)S(1)}, u32[]{:S(2)}, u32[]{:S(2)}) %all-to-all-start.2) | async-done | bytes 131104 | tf_op jit(solution)/shard_map/all_to_all | solution.py:31
  50.3 0.2 multiply_reduce_fusion.2
  50.7 0.6 broadcast_in_dim.104
  51.3 12.6 %all-to-all-start.3 = ((f32[32,3,128]{2,1,0:T(4,128)}), f32[32,3,128]{2,1,0:T(4,128)S(1)}, u32[]{:S(2)}, u32[]{:S(2)}) async-start(f32[32,3,128]{2,1,0:T(4,128)} %broadcast_in_dim.104), calls=%async_computation.3 | async-start | bytes 131072 | tf_op jit(solution)/shard_map/all_to_all | solution.py:31
  63.9 7.3 %all-to-all-done.3 = f32[32,3,128]{2,1,0:T(4,128)S(1)} async-done(((f32[32,3,128]{2,1,0:T(4,128)}), f32[32,3,128]{2,1,0:T(4,128)S(1)}, u32[]{:S(2)}, u32[]{:S(2)}) %all-to-all-start.3) | async-done | bytes 49184 | tf_op jit(solution)/shard_map/all_to_all | solution.py:31
  71.3 0.2 multiply_reduce_fusion
  71.6 0.1 multiply_reduce_fusion.4
  71.7 0.1 multiply_reduce_fusion.5
  71.8 0.4 fusion.5
  72.2 0.4 fusion
  72.7 7.3 %all_to_all.40 = bf16[4,64,256]{2,1,0:T(8,128)(2,1)S(1)} all-to-all(bf16[4,64,256]{2,1,0:T(8,128)(2,1)S(1)} %bitcast.25), channel_id=1, replica_groups=mesh['far'=4,'near'=4,'tm'=32] {'near'}, dimensions={0} | all-to-all | bytes 262144 | tf_op jit(solution)/shard_map/all_to_all | solution.py:35
  80.0 14.5 %all_to_all.41 = bf16[4,64,256]{2,1,0:T(8,128)(2,1)S(1)} all-to-all(bf16[4,64,256]{2,1,0:T(8,128)(2,1)S(1)} %broadcast_in_dim.107), channel_id=1, replica_groups=mesh['far'=4,'near'=4,'tm'=32] {'far'}, dimensions={0} | all-to-all | bytes 262144 | tf_op jit(solution)/shard_map/all_to_all | solution.py:31
  94.7 0.7 broadcast_in_dim.108
  95.3 3.5 %all-to-all-start.6 = ((bf16[4,64,256]{2,1,0:T(8,128)(2,1)}), bf16[4,64,256]{2,1,0:T(8,128)(2,1)S(1)}, u32[]{:S(2)}, u32[]{:S(2)}) async-start(bf16[4,64,256]{2,1,0:T(8,128)(2,1)} %broadcast_in_dim.108), calls=%async_computation.6 | async-start | bytes 262144 | tf_op jit(solution)/shard_map/all_to_all | solution.py:31
  98.8 2.2 %narrow.1.counts = s8[4096,256]{1,0:T(32,128)(4,1)S(1)} custom-call(s32[4096,256]{1,0:T(8,128)} %counts_far.3, bf16[64,256]{1,0:T(8,128)(2,1)S(1)} %multiply_convert_fusion.6.after), custom_call_target="tpu_custom_call" | custom-call | tf_op jit(solution)/shard_map/narrow/pallas_call | solution.py:92
  101.1 2.5 %all-to-all-done.6 = bf16[4,64,256]{2,1,0:T(8,128)(2,1)S(1)} async-done(((bf16[4,64,256]{2,1,0:T(8,128)(2,1)}), bf16[4,64,256]{2,1,0:T(8,128)(2,1)S(1)}, u32[]{:S(2)}, u32[]{:S(2)}) %all-to-all-start.6) | async-done | bytes 131104 | tf_op jit(solution)/shard_map/all_to_all | solution.py:31
  103.6 1.8 %likelihood.1 = (bf16[32,32,128]{2,1,0:T(8,128)(2,1)S(1)}, bf16[256,256]{1,0:T(8,128)(2,1)}) custom-call(bf16[256,256]{1,0:T(8,128)(2,1)S(1)} %bitcast.21, bf16[4096,256]{1,0:T(8,128)(2,1)S(1)} %copy-done.1, s8[4096,256]{1,0:T(32,128)(4,1)S(1)} %narrow.1.counts), custom_call_target="tpu_custom_call" | custom-call | tf_op jit(solution)/shard_map/likelihood/pallas_call | solution.py:124
  105.4 17.4 %all_to_all.42 = bf16[32,32,128]{2,1,0:T(8,128)(2,1)S(1)} all-to-all(bf16[32,32,128]{2,1,0:T(8,128)(2,1)S(1)} %get-tuple-element.5), channel_id=1, replica_groups=mesh['far'=4,'near'=4,'tm'=32] {'tm'}, dimensions={0} | all-to-all | bytes 524288 | tf_op jit(solution)/shard_map/all_to_all | solution.py:204
  122.9 0.6 multiply_bitcast_fusion
  (35 shorter events, 0.6 us)
Async XLA Ops:
  0.6 71.2 %copy-start = (bf16[128,256]{1,0:T(8,128)(2,1)S(1)}, bf16[128,256]{1,0:T(8,128)(2,1)}, u32[]{:S(2)}) copy-start(bf16[128,256]{1,0:T(8,128)(2,1)} %param.12) | copy-start | bytes 196612
  0.6 10.4 %copy-start.2 = (f32[256]{0:T(256)S(1)}, f32[256]{0:T(256)}, u32[]{:S(2)}) copy-start(f32[256]{0:T(256)} %param.11) | copy-start | bytes 3076
  0.7 44.9 %copy-start.3 = (f32[128]{0:T(128)S(1)}, f32[128]{0:T(128)}, u32[]{:S(2)}) copy-start(f32[128]{0:T(128)} %param.10) | copy-start | bytes 1540
  0.7 49.7 %copy-start.4 = (bf16[256,128]{1,0:T(8,128)(2,1)S(1)}, bf16[256,128]{1,0:T(8,128)(2,1)}, u32[]{:S(2)}) copy-start(bf16[256,128]{1,0:T(8,128)(2,1)} %param.9) | copy-start | bytes 196612
  0.7 71.5 %copy-start.5 = (bf16[128,256]{1,0:T(8,128)(2,1)S(1)}, bf16[128,256]{1,0:T(8,128)(2,1)}, u32[]{:S(2)}) copy-start(bf16[128,256]{1,0:T(8,128)(2,1)} %param.13) | copy-start | bytes 196612
  4.6 11.2 %all-to-all-start = ((bf16[4,64,256]{2,1,0:T(8,128)(2,1)}), bf16[4,64,256]{2,1,0:T(8,128)(2,1)S(1)}, u32[]{:S(2)}, u32[]{:S(2)}) async-start(bf16[4,64,256]{2,1,0:T(8,128)(2,1)} %read_in.1), calls=%async_computation | async-start | bytes 262144 | tf_op jit(solution)/shard_map/all_to_all | solution.py:35
  16.5 24.7 %all-to-all-start.1 = ((bf16[4,64,256]{2,1,0:T(8,128)(2,1)}), bf16[4,64,256]{2,1,0:T(8,128)(2,1)S(1)}, u32[]{:S(2)}, u32[]{:S(2)}) async-start(bf16[4,64,256]{2,1,0:T(8,128)(2,1)} %broadcast_in_dim.97), calls=%async_computation.1 | async-start | bytes 262144 | tf_op jit(solution)/shard_map/all_to_all | solution.py:31
  42.1 8.2 %all-to-all-start.2 = ((bf16[4,64,256]{2,1,0:T(8,128)(2,1)}), bf16[4,64,256]{2,1,0:T(8,128)(2,1)S(1)}, u32[]{:S(2)}, u32[]{:S(2)}) async-start(bf16[4,64,256]{2,1,0:T(8,128)(2,1)} %broadcast_in_dim.101), calls=%async_computation.2 | async-start | bytes 262144 | tf_op jit(solution)/shard_map/all_to_all | solution.py:31
  51.3 19.9 %all-to-all-start.3 = ((f32[32,3,128]{2,1,0:T(4,128)}), f32[32,3,128]{2,1,0:T(4,128)S(1)}, u32[]{:S(2)}, u32[]{:S(2)}) async-start(f32[32,3,128]{2,1,0:T(4,128)} %broadcast_in_dim.104), calls=%async_computation.3 | async-start | bytes 131072 | tf_op jit(solution)/shard_map/all_to_all | solution.py:31
  72.2 31.4 %copy-start.1 = (bf16[4096,256]{1,0:T(8,128)(2,1)S(1)}, bf16[4096,256]{1,0:T(8,128)(2,1)}, u32[]{:S(2)}) copy-start(bf16[4096,256]{1,0:T(8,128)(2,1)} %weights.1) | copy-start | bytes 6291460
  95.3 8.3 %all-to-all-start.6 = ((bf16[4,64,256]{2,1,0:T(8,128)(2,1)}), bf16[4,64,256]{2,1,0:T(8,128)(2,1)S(1)}, u32[]{:S(2)}, u32[]{:S(2)}) async-start(bf16[4,64,256]{2,1,0:T(8,128)(2,1)} %broadcast_in_dim.108), calls=%async_computation.6 | async-start | bytes 262144 | tf_op jit(solution)/shard_map/all_to_all | solution.py:31

commit v9 on v8

--- a/solution.py
+++ b/solution.py
@@ -31,9 +31,12 @@
     return lax.all_to_all(copies, axis, 0, 0)
 
 
+def reduce_near(parts):
+    return jnp.sum(lax.all_to_all(parts, "near", 0, 0).astype(F32), axis=0).astype(BF16)
+
+
 def reduce_rows(parts):
-    quarter = jnp.sum(lax.all_to_all(parts, "near", 0, 0).astype(F32), axis=0)
-    return jnp.sum(spread(quarter.astype(BF16), "far").astype(F32), axis=0)
+    return jnp.sum(spread(reduce_near(parts), "far").astype(F32), axis=0)
 
 
 def read_kernel(counts_far, weights_far, part, counts, weights, arrived):
@@ -135,60 +138,94 @@
     )(near(latent), near(read_weight), near(spikes))
 
 
+def tables_of(gate, decay_rate, bin_down, bin_across, order, place):
+    bins = gate.shape[0]
+    across = jnp.log(gate)[None, :]
+    down = jnp.log(gate)[:, None]
+    upto = jnp.sum(jnp.where(bin_across <= bin_down, across, 0.0), axis=1, keepdims=True)
+    upto_t = jnp.sum(jnp.where(bin_down <= bin_across, down, 0.0), axis=0, keepdims=True)
+    whole = jnp.sum(across, axis=1, keepdims=True)
+    before = upto - down
+    rate = decay_rate[None, :]
+    return dict(
+        upto=upto,
+        upto_t=upto_t,
+        before=before,
+        before_t=upto_t - across,
+        after_upto=whole - upto,
+        after_before=whole - before,
+        whole=jnp.broadcast_to(whole, rate.shape),
+        rate=rate,
+        scale=jnp.sqrt(-jnp.expm1(-2.0 * rate)),
+        bin_down=bin_down,
+        bin_across=bin_across,
+        to_last=bins - 1 - bin_down,
+        from_start=bin_down + 1.0,
+        to_end=bins - bin_down,
+        from_half=bin_down - bins // 2,
+        to_half=bins // 2 - bin_down,
+        earlier=(order >= order.T).astype(F32),
+        is_before=(order < place).astype(F32),
+        is_here=(order == place).astype(F32),
+        is_after=(order > place).astype(F32),
+        gap_fwd=(place - 1.0 - order) * bins,
+        gap_bwd=(order - 1.0 - place) * bins,
+    )
+
+
 def body(spikes, read_weight, in_proj, decay_rate, gate, out_fwd, out_bwd):
     bins = spikes.shape[1]
     quad = lax.axis_size("near")
     blocks = lax.axis_size("tm")
-    place = lax.axis_index("tm")
-    log_gate = jnp.log(gate)
-    row = lax.broadcasted_iota(jnp.int32, (bins, bins), 0)
-    col = lax.broadcasted_iota(jnp.int32, (bins, bins), 1)
-    upto = jnp.sum(jnp.where(col <= row, log_gate[None, :], 0.0), axis=1, keepdims=True)
-    before = upto - log_gate[:, None]
-    upto_t = jnp.sum(jnp.where(row <= col, log_gate[:, None], 0.0), axis=0, keepdims=True)
-    before_t = upto_t - log_gate[None, :]
-    mix_fwd = jnp.where(col <= row, jnp.exp(jnp.minimum(upto - upto_t, 0.0)), 0.0).astype(BF16)
-    mix_bwd = jnp.where(col >= row, jnp.exp(jnp.minimum(before_t - before, 0.0)), 0.0).astype(BF16)
-    whole = upto[bins - 1, 0]
-    first = lax.broadcasted_iota(jnp.int32, (bins, 1), 0).astype(F32)
-    rate = decay_rate[None, :]
-    scale_in = jnp.sqrt(-jnp.expm1(-2.0 * rate))
-    carry_fwd = jnp.exp((whole - upto) - (bins - 1 - first) * rate) * scale_in
-    carry_bwd = jnp.exp(before - first * rate) * scale_in
-    cum_fwd = jnp.exp(upto - (first + 1.0) * rate)
-    cum_bwd = jnp.exp((whole - before) - (bins - first) * rate)
-    grow = jnp.exp((first - bins // 2) * rate)
-    shrink = jnp.exp((bins // 2 - first) * rate)
-
-    rows = reduce_rows(read_in(spikes, read_weight, quad))
+    bin_down = jnp.arange(bins, dtype=jnp.int32).astype(F32)[:, None]
+    bin_across = jnp.arange(bins, dtype=jnp.int32).astype(F32)[None, :]
+    order = jnp.arange(blocks, dtype=jnp.int32).astype(F32)[:, None]
+    place = lax.axis_index("tm").astype(F32)
+
+    quarter = reduce_near(read_in(spikes, read_weight, quad))
+    got, tables = lax.optimization_barrier(
+        (spread(quarter, "far"), tables_of(gate, decay_rate, bin_down, bin_across, order, place))
+    )
+    rows = jnp.sum(got.astype(F32), axis=0)
     power = jnp.mean(rows * rows, axis=-1, keepdims=True) + 1e-05
     normed_rows = (rows * lax.rsqrt(power)).astype(BF16)
     normed = spread(normed_rows, "near").reshape(bins, -1)
 
+    rate, scale = tables["rate"], tables["scale"]
+    bin_down, bin_across = tables["bin_down"], tables["bin_across"]
+    carry_fwd = jnp.exp(tables["after_upto"] - tables["to_last"] * rate) * scale
+    carry_bwd = jnp.exp(tables["before"] - bin_down * rate) * scale
     drive = jnp.dot(normed, in_proj, preferred_element_type=F32)
     sent = jnp.stack(
         [
             jnp.sum(drive * carry_fwd, axis=0),
             jnp.sum(drive * carry_bwd, axis=0),
-            jnp.broadcast_to(whole, decay_rate.shape),
+            tables["whole"][0],
         ]
     )
     got = spread(sent, "tm")
-    drive = drive * scale_in
+
+    cum_fwd = jnp.exp(tables["upto"] - tables["from_start"] * rate)
+    cum_bwd = jnp.exp(tables["after_before"] - tables["to_end"] * rate)
+    grow = jnp.exp(tables["from_half"] * rate)
+    shrink = jnp.exp(tables["to_half"] * rate)
+    mix_fwd = jnp.where(
+        bin_across <= bin_down, jnp.exp(jnp.minimum(tables["upto"] - tables["upto_t"], 0.0)), 0.0
+    ).astype(BF16)
+    mix_bwd = jnp.where(
+        bin_across >= bin_down, jnp.exp(jnp.minimum(tables["before_t"] - tables["before"], 0.0)), 0.0
+    ).astype(BF16)
+    drive = drive * scale
     state_fwd = jnp.dot(mix_fwd, (drive * grow).astype(BF16), preferred_element_type=F32) * shrink
     state_bwd = jnp.dot(mix_bwd, (drive * shrink).astype(BF16), preferred_element_type=F32) * grow
 
     loss = got[:, 2, :]
-    order = jnp.arange(blocks, dtype=jnp.int32)[:, None]
-    earlier = (order >= order.T).astype(F32)
-    span = jnp.sum(earlier[:, :, None] * loss[None, :, :], axis=1)
+    span = jnp.sum(tables["earlier"][:, :, None] * loss[None, :, :], axis=1)
     span_before = span - loss
-    at_fwd = jnp.sum(jnp.where(order == place, span_before, 0.0), axis=0)
-    at_bwd = jnp.sum(jnp.where(order == place, span, 0.0), axis=0)
-    gap_fwd = ((place - 1 - order) * bins).astype(F32) * rate
-    gap_bwd = ((order - 1 - place) * bins).astype(F32) * rate
-    weight_fwd = jnp.where(order < place, jnp.exp(jnp.minimum(at_fwd[None, :] - span - gap_fwd, 0.0)), 0.0)
-    weight_bwd = jnp.where(order > place, jnp.exp(jnp.minimum(span_before - at_bwd[None, :] - gap_bwd, 0.0)), 0.0)
+    at_fwd = jnp.sum(tables["is_here"] * span_before, axis=0, keepdims=True)
+    at_bwd = jnp.sum(tables["is_here"] * span, axis=0, keepdims=True)
+    weight_fwd = tables["is_before"] * jnp.exp(jnp.minimum(at_fwd - span - tables["gap_fwd"] * rate, 0.0))
+    weight_bwd = tables["is_after"] * jnp.exp(jnp.minimum(span_before - at_bwd - tables["gap_bwd"] * rate, 0.0))
     enter_fwd = jnp.sum(weight_fwd * got[:, 0, :], axis=0)
     enter_bwd = jnp.sum(weight_bwd * got[:, 1, :], axis=0)
     forward = (state_fwd + cum_fwd * enter_fwd[None, :]).astype(BF16)

time: 124 us -> 123 us (level)
  blocking collectives: 39.3 us -> 67.1 us
  starting transfers between devices: 38.5 us -> 22.4 us
  waiting for transfers between devices: 29.3 us -> 17.1 us
  local copies, waits for them, and re-layouts: 4.03 us -> 2.08 us
  other arithmetic: 2.47 us -> 3.77 us
    all_to_all x1 -> x3, blocking collectives: 14.5 us -> 42.3 us  [spread(): return lax.all_to_all(copies, axis, 0, 0)]
    all_to_all x4 -> x2, starting transfers between devices: 32.1 us -> 16 us  [spread(): return lax.all_to_all(copies, axis, 0, 0)]
    all_to_all x4 -> x2, waiting for transfers between devices: 26 us -> 14.6 us  [spread(): return lax.all_to_all(copies, axis, 0, 0)]
    broadcast_in_dim x5, local copies, waits for them, and re-layouts: 2.65 us -> 1.36 us  [spread(): copies = jnp.broadcast_to(part[None], (count,) + part.shape)]
    sub x3 -> x5, other arithmetic: 0.67 us -> 1.93 us  [the longest x1 0.65 us: tables_of(): whole - before]
  transfers between devices with their start and end apart: 5 -> 3, of which waited for: 5 -> 3; matrix products, arithmetic and copies ran while one was open for 2% -> 2% of each run, Pallas kernels for 2% -> 2%
where the time goes in v9:
time: 123 us; the launch traced here: 122 us
  blocking collectives  67.1 us (55%)
  starting transfers between devices  22.4 us (18%)
  waiting for transfers between devices  17.1 us (14%)
  Pallas kernels  7.94 us (6%)
  other arithmetic  3.77 us (3%)
  local copies, waits for them, and re-layouts  2.08 us (2%)
    all_to_all x3, blocking collectives, spread(): return lax.all_to_all(copies, axis, 0, 0)  42.3 us
    all_to_all x1, blocking collectives, body(): terms = lax.all_to_all(copies, 'tm', 0, 0)  17.5 us
    all_to_all x2, starting transfers between devices, spread(): return lax.all_to_all(copies, axis, 0, 0)  16 us
    all_to_all x2, waiting for transfers between devices, spread(): return lax.all_to_all(copies, axis, 0, 0)  14.6 us
    all_to_all x1, blocking collectives, reduce_near(): lax.all_to_all(parts, 'near', 0, 0).astype(F32)  7.32 us
    all_to_all x1, starting transfers between devices, reduce_near(): lax.all_to_all(parts, 'near', 0, 0).astype(F32)  6.46 us
    pallas_call x1, Pallas kernels, read_in(): pl.pallas_call(read_kernel, in_specs=[IN_HBM, IN_HBM], out_specs=IN_VMEM,...  3.92 us
    all_to_all x1, waiting for transfers between devices, reduce_near(): lax.all_to_all(parts, 'near', 0, 0).astype(F32)  2.53 us
  transfers between devices with their start and end apart: 3, of which 3 were waited for; matrix products, arithmetic and copies ran while one was open for 2% of the time, Pallas kernels for 2%

profile of v9, /device:TPU:1, one launch (start us, length us, event | category | flops | bytes accessed | tf_op | source)
XLA Modules:
  0.0 122.4 jit_solution(10305764930456695128)
XLA Ops:
  0.7 3.9 %read_in.1 = bf16[4,64,256]{2,1,0:T(8,128)(2,1)} custom-call(s32[4096,256]{1,0:T(8,128)} %counts_far.3, bf16[4096,256]{1,0:T(8,128)(2,1)} %weights.1), custom_call_target="tpu_custom_call" | custom-call | tf_op jit(solution)/shard_map/read_in/pallas_call | solution.py:65
  4.6 6.5 %all-to-all-start = ((bf16[4,64,256]{2,1,0:T(8,128)(2,1)}), bf16[4,64,256]{2,1,0:T(8,128)(2,1)S(1)}, u32[]{:S(2)}, u32[]{:S(2)}) async-start(bf16[4,64,256]{2,1,0:T(8,128)(2,1)} %read_in.1), calls=%async_computation | async-start | bytes 262144 | tf_op jit(solution)/shard_map/all_to_all | solution.py:35
  11.2 0.2 select_reduce_fusion
  11.4 0.6 log_subtract_fusion
  12.0 0.7 broadcast_add_fusion.1
  12.7 0.7 broadcast_subtract_fusion.4
  13.3 2.5 %all-to-all-done = bf16[4,64,256]{2,1,0:T(8,128)(2,1)S(1)} async-done(((bf16[4,64,256]{2,1,0:T(8,128)(2,1)}), bf16[4,64,256]{2,1,0:T(8,128)(2,1)S(1)}, u32[]{:S(2)}, u32[]{:S(2)}) %all-to-all-start) | async-done | bytes 131104 | tf_op jit(solution)/shard_map/all_to_all | solution.py:35
  15.9 0.7 broadcast_in_dim.40
  16.5 12.5 %all-to-all-start.1 = ((bf16[4,64,256]{2,1,0:T(8,128)(2,1)}), bf16[4,64,256]{2,1,0:T(8,128)(2,1)S(1)}, u32[]{:S(2)}, u32[]{:S(2)}) async-start(bf16[4,64,256]{2,1,0:T(8,128)(2,1)} %broadcast_in_dim.40), calls=%async_computation.1 | async-start | bytes 262144 | tf_op jit(solution)/shard_map/all_to_all | solution.py:31
  29.1 12.1 %all-to-all-done.1 = bf16[4,64,256]{2,1,0:T(8,128)(2,1)S(1)} async-done(((bf16[4,64,256]{2,1,0:T(8,128)(2,1)}), bf16[4,64,256]{2,1,0:T(8,128)(2,1)S(1)}, u32[]{:S(2)}, u32[]{:S(2)}) %all-to-all-start.1) | async-done | bytes 131104 | tf_op jit(solution)/shard_map/all_to_all | solution.py:31
  41.2 0.6 broadcast_in_dim.47
  41.9 0.1 multiply_reduce_fusion.3
  42.0 0.1 multiply_convert_fusion.6.after
  42.1 8.0 %all_to_all.40 = bf16[4,64,256]{2,1,0:T(8,128)(2,1)S(1)} all-to-all(bf16[4,64,256]{2,1,0:T(8,128)(2,1)S(1)} %broadcast_in_dim.48), channel_id=1, replica_groups=mesh['far'=4,'near'=4,'tm'=32] {'near'}, dimensions={0} | all-to-all | bytes 262144 | tf_op jit(solution)/shard_map/all_to_all | solution.py:31
  50.1 0.2 multiply_reduce_fusion.2
  50.4 19.3 %all_to_all.41 = f32[32,3,128]{2,1,0:T(4,128)S(1)} all-to-all(f32[32,3,128]{2,1,0:T(4,128)S(1)} %broadcast_in_dim.49), channel_id=1, replica_groups=mesh['far'=4,'near'=4,'tm'=32] {'tm'}, dimensions={0} | all-to-all | bytes 98304 | tf_op jit(solution)/shard_map/all_to_all | solution.py:31
  69.7 0.2 multiply_reduce_fusion
  70.0 0.1 multiply_reduce_fusion.5
  70.1 0.1 multiply_reduce_fusion.4
  70.2 0.1 multiply_reduce_fusion.6
  70.3 0.4 fusion.5
  70.7 0.4 fusion
  71.1 7.3 %all_to_all.42 = bf16[4,64,256]{2,1,0:T(8,128)(2,1)S(1)} all-to-all(bf16[4,64,256]{2,1,0:T(8,128)(2,1)S(1)} %bitcast.51), channel_id=1, replica_groups=mesh['far'=4,'near'=4,'tm'=32] {'near'}, dimensions={0} | all-to-all | bytes 262144 | tf_op jit(solution)/shard_map/all_to_all | solution.py:35
  78.5 15.0 %all_to_all.43 = bf16[4,64,256]{2,1,0:T(8,128)(2,1)S(1)} all-to-all(bf16[4,64,256]{2,1,0:T(8,128)(2,1)S(1)} %broadcast_in_dim.50), channel_id=1, replica_groups=mesh['far'=4,'near'=4,'tm'=32] {'far'}, dimensions={0} | all-to-all | bytes 262144 | tf_op jit(solution)/shard_map/all_to_all | solution.py:31
  93.5 0.1 add_convert_fusion
  93.6 0.7 broadcast_in_dim.51
  94.3 3.5 %all-to-all-start.6 = ((bf16[4,64,256]{2,1,0:T(8,128)(2,1)}), bf16[4,64,256]{2,1,0:T(8,128)(2,1)S(1)}, u32[]{:S(2)}, u32[]{:S(2)}) async-start(bf16[4,64,256]{2,1,0:T(8,128)(2,1)} %broadcast_in_dim.51), calls=%async_computation.6 | async-start | bytes 262144 | tf_op jit(solution)/shard_map/all_to_all | solution.py:31
  97.7 2.2 %narrow.1.counts = s8[4096,256]{1,0:T(32,128)(4,1)S(1)} custom-call(s32[4096,256]{1,0:T(8,128)} %counts_far.3, bf16[64,256]{1,0:T(8,128)(2,1)S(1)} %multiply_convert_fusion.6.after), custom_call_target="tpu_custom_call" | custom-call | tf_op jit(solution)/shard_map/narrow/pallas_call | solution.py:95
  100.0 2.5 %all-to-all-done.6 = bf16[4,64,256]{2,1,0:T(8,128)(2,1)S(1)} async-done(((bf16[4,64,256]{2,1,0:T(8,128)(2,1)}), bf16[4,64,256]{2,1,0:T(8,128)(2,1)S(1)}, u32[]{:S(2)}, u32[]{:S(2)}) %all-to-all-start.6) | async-done | bytes 131104 | tf_op jit(solution)/shard_map/all_to_all | solution.py:31
  102.5 1.8 %likelihood.1 = (bf16[32,32,128]{2,1,0:T(8,128)(2,1)S(1)}, bf16[256,256]{1,0:T(8,128)(2,1)}) custom-call(bf16[256,256]{1,0:T(8,128)(2,1)S(1)} %bitcast.48, bf16[4096,256]{1,0:T(8,128)(2,1)S(1)} %copy-done.1, s8[4096,256]{1,0:T(32,128)(4,1)S(1)} %narrow.1.counts), custom_call_target="tpu_custom_call" | custom-call | tf_op jit(solution)/shard_map/likelihood/pallas_call | solution.py:127
  104.3 17.5 %all_to_all.44 = bf16[32,32,128]{2,1,0:T(8,128)(2,1)S(1)} all-to-all(bf16[32,32,128]{2,1,0:T(8,128)(2,1)S(1)} %get-tuple-element.51), channel_id=1, replica_groups=mesh['far'=4,'near'=4,'tm'=32] {'tm'}, dimensions={0} | all-to-all | bytes 524288 | tf_op jit(solution)/shard_map/all_to_all | solution.py:241
  121.8 0.6 multiply_bitcast_fusion
  (35 shorter events, 0.4 us)
Async XLA Ops:
  0.6 69.6 %copy-start = (bf16[128,256]{1,0:T(8,128)(2,1)S(1)}, bf16[128,256]{1,0:T(8,128)(2,1)}, u32[]{:S(2)}) copy-start(bf16[128,256]{1,0:T(8,128)(2,1)} %param.12) | copy-start | bytes 196612
  0.6 10.5 %copy-start.2 = (f32[256]{0:T(256)S(1)}, f32[256]{0:T(256)}, u32[]{:S(2)}) copy-start(f32[256]{0:T(256)} %param.11) | copy-start | bytes 3076
  0.7 28.4 %copy-start.3 = (f32[128]{0:T(128)S(1)}, f32[128]{0:T(128)}, u32[]{:S(2)}) copy-start(f32[128]{0:T(128)} %param.10) | copy-start | bytes 1540
  0.7 49.5 %copy-start.4 = (bf16[256,128]{1,0:T(8,128)(2,1)S(1)}, bf16[256,128]{1,0:T(8,128)(2,1)}, u32[]{:S(2)}) copy-start(bf16[256,128]{1,0:T(8,128)(2,1)} %param.9) | copy-start | bytes 196612
  0.7 70.0 %copy-start.5 = (bf16[128,256]{1,0:T(8,128)(2,1)S(1)}, bf16[128,256]{1,0:T(8,128)(2,1)}, u32[]{:S(2)}) copy-start(bf16[128,256]{1,0:T(8,128)(2,1)} %param.13) | copy-start | bytes 196612
  4.6 11.2 %all-to-all-start = ((bf16[4,64,256]{2,1,0:T(8,128)(2,1)}), bf16[4,64,256]{2,1,0:T(8,128)(2,1)S(1)}, u32[]{:S(2)}, u32[]{:S(2)}) async-start(bf16[4,64,256]{2,1,0:T(8,128)(2,1)} %read_in.1), calls=%async_computation | async-start | bytes 262144 | tf_op jit(solution)/shard_map/all_to_all | solution.py:35
  16.5 24.7 %all-to-all-start.1 = ((bf16[4,64,256]{2,1,0:T(8,128)(2,1)}), bf16[4,64,256]{2,1,0:T(8,128)(2,1)S(1)}, u32[]{:S(2)}, u32[]{:S(2)}) async-start(bf16[4,64,256]{2,1,0:T(8,128)(2,1)} %broadcast_in_dim.40), calls=%async_computation.1 | async-start | bytes 262144 | tf_op jit(solution)/shard_map/all_to_all | solution.py:31
  70.7 31.8 %copy-start.1 = (bf16[4096,256]{1,0:T(8,128)(2,1)S(1)}, bf16[4096,256]{1,0:T(8,128)(2,1)}, u32[]{:S(2)}) copy-start(bf16[4096,256]{1,0:T(8,128)(2,1)} %weights.1) | copy-start | bytes 6291460
  94.3 8.2 %all-to-all-start.6 = ((bf16[4,64,256]{2,1,0:T(8,128)(2,1)}), bf16[4,64,256]{2,1,0:T(8,128)(2,1)S(1)}, u32[]{:S(2)}, u32[]{:S(2)}) async-start(bf16[4,64,256]{2,1,0:T(8,128)(2,1)} %broadcast_in_dim.51), calls=%async_computation.6 | async-start | bytes 262144 | tf_op jit(solution)/shard_map/all_to_all | solution.py:31

commit v10 on v9

--- a/solution.py
+++ b/solution.py
@@ -31,12 +31,9 @@
     return lax.all_to_all(copies, axis, 0, 0)
 
 
-def reduce_near(parts):
-    return jnp.sum(lax.all_to_all(parts, "near", 0, 0).astype(F32), axis=0).astype(BF16)
-
-
-def reduce_rows(parts):
-    return jnp.sum(spread(reduce_near(parts), "far").astype(F32), axis=0)
+def sum_quads(parts):
+    quarter = jnp.sum(parts.astype(F32), axis=0).astype(BF16)
+    return jnp.sum(spread(quarter, "far").astype(F32), axis=0)
 
 
 def read_kernel(counts_far, weights_far, part, counts, weights, arrived):
@@ -144,7 +141,9 @@
     down = jnp.log(gate)[:, None]
     upto = jnp.sum(jnp.where(bin_across <= bin_down, across, 0.0), axis=1, keepdims=True)
     upto_t = jnp.sum(jnp.where(bin_down <= bin_across, down, 0.0), axis=0, keepdims=True)
-    whole = jnp.sum(across, axis=1, keepdims=True)
+    lane = lax.broadcasted_iota(jnp.int32, (1, decay_rate.shape[0]), 1).astype(F32)
+    whole = jnp.sum(jnp.where(bin_across >= -bin_down, across, 0.0), axis=1, keepdims=True)
+    whole_row = jnp.sum(jnp.where(bin_down >= -lane, down, 0.0), axis=0, keepdims=True)
     before = upto - down
     rate = decay_rate[None, :]
     return dict(
@@ -154,7 +153,7 @@
         before_t=upto_t - across,
         after_upto=whole - upto,
         after_before=whole - before,
-        whole=jnp.broadcast_to(whole, rate.shape),
+        whole=whole_row,
         rate=rate,
         scale=jnp.sqrt(-jnp.expm1(-2.0 * rate)),
         bin_down=bin_down,
@@ -182,11 +181,11 @@
     order = jnp.arange(blocks, dtype=jnp.int32).astype(F32)[:, None]
     place = lax.axis_index("tm").astype(F32)
 
-    quarter = reduce_near(read_in(spikes, read_weight, quad))
-    got, tables = lax.optimization_barrier(
-        (spread(quarter, "far"), tables_of(gate, decay_rate, bin_down, bin_across, order, place))
-    )
-    rows = jnp.sum(got.astype(F32), axis=0)
+    parts = read_in(spikes, read_weight, quad)
+    parts, tables = lax.optimization_barrier(
+        (lax.all_to_all(parts, "near", 0, 0), tables_of(gate, decay_rate, bin_down, bin_across, order, place))
+    )
+    rows = sum_quads(parts)
     power = jnp.mean(rows * rows, axis=-1, keepdims=True) + 1e-05
     normed_rows = (rows * lax.rsqrt(power)).astype(BF16)
     normed = spread(normed_rows, "near").reshape(bins, -1)
@@ -232,7 +231,8 @@
     backward = (state_bwd + cum_bwd * enter_bwd[None, :]).astype(BF16)
     mixed = jnp.dot(forward, out_fwd, preferred_element_type=F32)
     mixed = mixed + jnp.dot(backward, out_bwd, preferred_element_type=F32)
-    mixed_rows = reduce_rows(mixed.astype(BF16).reshape(quad, bins // quad, -1))
+    parts = mixed.astype(BF16).reshape(quad, bins // quad, -1)
+    mixed_rows = sum_quads(lax.all_to_all(parts, "near", 0, 0))
     latent_rows = (normed_rows.astype(F32) + mixed_rows).astype(BF16)
     latent = spread(latent_rows, "near").reshape(bins, -1)
 

time: 123 us -> 121 us (0.984)
  blocking collectives: 67.1 us -> 91.5 us
  starting transfers between devices: 22.4 us -> 9.93 us
  waiting for transfers between devices: 17.1 us -> 6.59 us
  other arithmetic: 3.77 us -> 2.12 us
  local copies, waits for them, and re-layouts: 2.08 us -> 0.78 us
    all_to_all x3 -> x4, blocking collectives: 42.3 us -> 66.8 us  [spread(): return lax.all_to_all(copies, axis, 0, 0)]
    all_to_all x2 -> x1, starting transfers between devices: 16 us -> 3.48 us  [spread(): return lax.all_to_all(copies, axis, 0, 0)]
    all_to_all x2 -> x1, waiting for transfers between devices: 14.6 us -> 2.52 us  [spread(): return lax.all_to_all(copies, axis, 0, 0)]
    all_to_all x1, waiting for transfers between devices: 2.53 us -> 4.06 us  [body(): lax.all_to_all(parts, 'near', 0, 0)]
  transfers between devices with their start and end apart: 3 -> 2, of which waited for: 3 -> 2; matrix products, arithmetic and copies ran while one was open for 2% -> 0% of each run, Pallas kernels for 2% -> 2%
where the time goes in v10:
time: 121 us
  blocking collectives  91.5 us (76%)
  starting transfers between devices  9.93 us (8%)
  Pallas kernels  7.94 us (7%)
  waiting for transfers between devices  6.59 us (5%)
  other arithmetic  2.12 us (2%)
    all_to_all x4, blocking collectives, spread(): return lax.all_to_all(copies, axis, 0, 0)  66.8 us
    all_to_all x1, blocking collectives, body(): terms = lax.all_to_all(copies, 'tm', 0, 0)  17.5 us
    all_to_all x1, blocking collectives, body(): mixed_rows = sum_quads(lax.all_to_all(parts, 'near', 0, 0))  7.32 us
    all_to_all x1, starting transfers between devices, body(): lax.all_to_all(parts, 'near', 0, 0)  6.46 us
    all_to_all x1, waiting for transfers between devices, body(): lax.all_to_all(parts, 'near', 0, 0)  4.06 us
    pallas_call x1, Pallas kernels, read_in(): pl.pallas_call(read_kernel, in_specs=[IN_HBM, IN_HBM], out_specs=IN_VMEM,...  3.92 us
    all_to_all x1, starting transfers between devices, spread(): return lax.all_to_all(copies, axis, 0, 0)  3.48 us
    all_to_all x1, waiting for transfers between devices, spread(): return lax.all_to_all(copies, axis, 0, 0)  2.52 us
  transfers between devices with their start and end apart: 2, of which 2 were waited for; matrix products, arithmetic and copies ran while one was open for 0% of the time, Pallas kernels for 2%

profile of v10, /device:TPU:1, one launch (start us, length us, event | category | flops | bytes accessed | tf_op | source)
XLA Modules:
  0.0 120.9 jit_solution(17004490337212824767)
XLA Ops:
  0.6 0.0 copy-start
  0.6 0.0 copy-start.3
  0.7 0.0 copy-start.2
  0.7 3.9 %read_in.1 = bf16[4,64,256]{2,1,0:T(8,128)(2,1)} custom-call(s32[4096,256]{1,0:T(8,128)} %counts_far.3, bf16[4096,256]{1,0:T(8,128)(2,1)} %weights.1), custom_call_target="tpu_custom_call" | custom-call | tf_op jit(solution)/shard_map/read_in/pallas_call | solution.py:62
  4.6 6.5 %all-to-all-start = ((bf16[4,64,256]{2,1,0:T(8,128)(2,1)}), bf16[4,64,256]{2,1,0:T(8,128)(2,1)S(1)}, u32[]{:S(2)}, u32[]{:S(2)}) async-start(bf16[4,64,256]{2,1,0:T(8,128)(2,1)} %read_in.1), calls=%async_computation | async-start | bytes 262144 | tf_op jit(solution)/shard_map/all_to_all | solution.py:186
  11.2 0.3 select_reduce_fusion
  11.6 0.1 select_reduce_fusion.3
  11.7 0.1 compare_convert_fusion
  11.8 4.1 %all-to-all-done = bf16[4,64,256]{2,1,0:T(8,128)(2,1)S(1)} async-done(((bf16[4,64,256]{2,1,0:T(8,128)(2,1)}), bf16[4,64,256]{2,1,0:T(8,128)(2,1)S(1)}, u32[]{:S(2)}, u32[]{:S(2)}) %all-to-all-start) | async-done | bytes 131104 | tf_op jit(solution)/shard_map/all_to_all | solution.py:186
  15.9 24.5 %all_to_all.40 = bf16[4,64,256]{2,1,0:T(8,128)(2,1)S(1)} all-to-all(bf16[4,64,256]{2,1,0:T(8,128)(2,1)S(1)} %broadcast_in_dim.101), channel_id=1, replica_groups=mesh['far'=4,'near'=4,'tm'=32] {'far'}, dimensions={0} | all-to-all | bytes 262144 | tf_op jit(solution)/shard_map/all_to_all | solution.py:31
  40.4 0.1 multiply_reduce_fusion.3
  40.5 0.1 multiply_convert_fusion.6.after
  40.6 8.0 %all_to_all.41 = bf16[4,64,256]{2,1,0:T(8,128)(2,1)S(1)} all-to-all(bf16[4,64,256]{2,1,0:T(8,128)(2,1)S(1)} %broadcast_in_dim.102), channel_id=1, replica_groups=mesh['far'=4,'near'=4,'tm'=32] {'near'}, dimensions={0} | all-to-all | bytes 262144 | tf_op jit(solution)/shard_map/all_to_all | solution.py:31
  48.6 0.2 multiply_reduce_fusion.2
  48.9 19.3 %all_to_all.42 = f32[32,3,128]{2,1,0:T(4,128)S(1)} all-to-all(f32[32,3,128]{2,1,0:T(4,128)S(1)} %broadcast_in_dim.103), channel_id=1, replica_groups=mesh['far'=4,'near'=4,'tm'=32] {'tm'}, dimensions={0} | all-to-all | bytes 98304 | tf_op jit(solution)/shard_map/all_to_all | solution.py:31
  68.2 0.2 multiply_reduce_fusion
  68.5 0.1 multiply_reduce_fusion.5
  68.5 0.1 multiply_reduce_fusion.4
  68.6 0.1 multiply_reduce_fusion.6
  68.8 0.4 fusion.5
  69.2 0.0 copy-start.1
  69.2 0.4 fusion
  69.6 7.3 %all_to_all.43 = bf16[4,64,256]{2,1,0:T(8,128)(2,1)S(1)} all-to-all(bf16[4,64,256]{2,1,0:T(8,128)(2,1)S(1)} %bitcast.53), channel_id=1, replica_groups=mesh['far'=4,'near'=4,'tm'=32] {'near'}, dimensions={0} | all-to-all | bytes 262144 | tf_op jit(solution)/shard_map/all_to_all | solution.py:235
  77.0 15.0 %all_to_all.44 = bf16[4,64,256]{2,1,0:T(8,128)(2,1)S(1)} all-to-all(bf16[4,64,256]{2,1,0:T(8,128)(2,1)S(1)} %broadcast_in_dim.104), channel_id=1, replica_groups=mesh['far'=4,'near'=4,'tm'=32] {'far'}, dimensions={0} | all-to-all | bytes 262144 | tf_op jit(solution)/shard_map/all_to_all | solution.py:31
  92.0 0.1 add_convert_fusion
  92.1 0.7 broadcast_in_dim.105
  92.7 3.5 %all-to-all-start.6 = ((bf16[4,64,256]{2,1,0:T(8,128)(2,1)}), bf16[4,64,256]{2,1,0:T(8,128)(2,1)S(1)}, u32[]{:S(2)}, u32[]{:S(2)}) async-start(bf16[4,64,256]{2,1,0:T(8,128)(2,1)} %broadcast_in_dim.105), calls=%async_computation.6 | async-start | bytes 262144 | tf_op jit(solution)/shard_map/all_to_all | solution.py:31
  96.2 2.2 %narrow.1.counts = s8[4096,256]{1,0:T(32,128)(4,1)S(1)} custom-call(s32[4096,256]{1,0:T(8,128)} %counts_far.3, bf16[64,256]{1,0:T(8,128)(2,1)S(1)} %multiply_convert_fusion.6.after), custom_call_target="tpu_custom_call" | custom-call | tf_op jit(solution)/shard_map/narrow/pallas_call | solution.py:92
  98.5 2.5 %all-to-all-done.6 = bf16[4,64,256]{2,1,0:T(8,128)(2,1)S(1)} async-done(((bf16[4,64,256]{2,1,0:T(8,128)(2,1)}), bf16[4,64,256]{2,1,0:T(8,128)(2,1)S(1)}, u32[]{:S(2)}, u32[]{:S(2)}) %all-to-all-start.6) | async-done | bytes 131104 | tf_op jit(solution)/shard_map/all_to_all | solution.py:31
  101.0 1.8 %likelihood.1 = (bf16[32,32,128]{2,1,0:T(8,128)(2,1)S(1)}, bf16[256,256]{1,0:T(8,128)(2,1)}) custom-call(bf16[256,256]{1,0:T(8,128)(2,1)S(1)} %bitcast.50, bf16[4096,256]{1,0:T(8,128)(2,1)S(1)} %copy-done.1, s8[4096,256]{1,0:T(32,128)(4,1)S(1)} %narrow.1.counts), custom_call_target="tpu_custom_call" | custom-call | tf_op jit(solution)/shard_map/likelihood/pallas_call | solution.py:124
  102.8 17.5 %all_to_all.45 = bf16[32,32,128]{2,1,0:T(8,128)(2,1)S(1)} all-to-all(bf16[32,32,128]{2,1,0:T(8,128)(2,1)S(1)} %get-tuple-element.51), channel_id=1, replica_groups=mesh['far'=4,'near'=4,'tm'=32] {'tm'}, dimensions={0} | all-to-all | bytes 524288 | tf_op jit(solution)/shard_map/all_to_all | solution.py:241
  120.3 0.6 multiply_bitcast_fusion
  (36 shorter events, 0.3 us)
Async XLA Ops:
  0.6 68.1 %copy-start = (bf16[128,256]{1,0:T(8,128)(2,1)S(1)}, bf16[128,256]{1,0:T(8,128)(2,1)}, u32[]{:S(2)}) copy-start(bf16[128,256]{1,0:T(8,128)(2,1)} %param.12) | copy-start | bytes 196612
  0.6 10.5 %copy-start.3 = (f32[128]{0:T(128)S(1)}, f32[128]{0:T(128)}, u32[]{:S(2)}) copy-start(f32[128]{0:T(128)} %param.10) | copy-start | bytes 1540
  0.7 10.6 %copy-start.2 = (f32[256]{0:T(256)S(1)}, f32[256]{0:T(256)}, u32[]{:S(2)}) copy-start(f32[256]{0:T(256)} %param.11) | copy-start | bytes 3076
  0.7 48.0 %copy-start.4 = (bf16[256,128]{1,0:T(8,128)(2,1)S(1)}, bf16[256,128]{1,0:T(8,128)(2,1)}, u32[]{:S(2)}) copy-start(bf16[256,128]{1,0:T(8,128)(2,1)} %param.9) | copy-start | bytes 196612
  0.7 68.5 %copy-start.5 = (bf16[128,256]{1,0:T(8,128)(2,1)S(1)}, bf16[128,256]{1,0:T(8,128)(2,1)}, u32[]{:S(2)}) copy-start(bf16[128,256]{1,0:T(8,128)(2,1)} %param.13) | copy-start | bytes 196612
  4.6 11.2 %all-to-all-start = ((bf16[4,64,256]{2,1,0:T(8,128)(2,1)}), bf16[4,64,256]{2,1,0:T(8,128)(2,1)S(1)}, u32[]{:S(2)}, u32[]{:S(2)}) async-start(bf16[4,64,256]{2,1,0:T(8,128)(2,1)} %read_in.1), calls=%async_computation | async-start | bytes 262144 | tf_op jit(solution)/shard_map/all_to_all | solution.py:186
  69.2 31.8 %copy-start.1 = (bf16[4096,256]{1,0:T(8,128)(2,1)S(1)}, bf16[4096,256]{1,0:T(8,128)(2,1)}, u32[]{:S(2)}) copy-start(bf16[4096,256]{1,0:T(8,128)(2,1)} %weights.1) | copy-start | bytes 6291460
  92.7 8.2 %all-to-all-start.6 = ((bf16[4,64,256]{2,1,0:T(8,128)(2,1)}), bf16[4,64,256]{2,1,0:T(8,128)(2,1)S(1)}, u32[]{:S(2)}, u32[]{:S(2)}) async-start(bf16[4,64,256]{2,1,0:T(8,128)(2,1)} %broadcast_in_dim.105), calls=%async_computation.6 | async-start | bytes 262144 | tf_op jit(solution)/shard_map/all_to_all | solution.py:31

commit v11 on v10

--- a/solution.py
+++ b/solution.py
@@ -103,10 +103,11 @@
     )(far(spikes), after)
 
 
-def likelihood_kernel(latent, weights, counts, copies, out_latent, sums):
+def likelihood_kernel(latent, weights, counts, copies, out_latent, sums, left):
     wide = 4 * LANES
     rows = latent[...]
-    out_latent[...] = rows
+    leaving = pltpu.make_async_copy(latent, out_latent, left)
+    leaving.start()
     for k in range(weights.shape[0] // wide):
         here = slice(k * wide, (k + 1) * wide)
         log_rate = lax.dot_general(weights[here, :], rows, ROWS, preferred_element_type=F32)
@@ -117,6 +118,7 @@
             sums[4 * k + j : 4 * k + j + 1, :] = jnp.sum(turned, axis=0, keepdims=True)
     small = sums[...].astype(BF16)
     copies[...] = jnp.broadcast_to(small[None], copies.shape)
+    leaving.wait()
 
 
 def likelihood(latent, read_weight, spikes, blocks):
@@ -124,12 +126,12 @@
     return pl.pallas_call(
         likelihood_kernel,
         in_specs=[IN_VMEM, IN_VMEM, IN_VMEM],
-        out_specs=[IN_VMEM, IN_VMEM],
+        out_specs=[IN_VMEM, IN_HBM],
         out_shape=[
             jax.ShapeDtypeStruct((blocks, neurons // LANES, LANES), BF16),
-            jax.ShapeDtypeStruct(latent.shape, BF16),
+            pltpu.HBM(latent.shape, BF16),
         ],
-        scratch_shapes=[pltpu.VMEM((neurons // LANES, LANES), F32)],
+        scratch_shapes=[pltpu.VMEM((neurons // LANES, LANES), F32), pltpu.SemaphoreType.DMA],
         compiler_params=pltpu.CompilerParams(vmem_limit_bytes=ROOM),
         name="likelihood",
     )(near(latent), near(read_weight), near(spikes))

time: 121 us -> 121 us (level)
  transfers between devices with their start and end apart: 2 -> 2, of which waited for: 2 -> 2; matrix products, arithmetic and copies ran while one was open for 0% -> 1% of each run, Pallas kernels for 2% -> 2%
where the time goes in v11:
time: 121 us; the launch traced here: 120 us
  blocking collectives  91.5 us (76%)
  starting transfers between devices  9.93 us (8%)
  Pallas kernels  7.42 us (6%)
  waiting for transfers between devices  6.59 us (5%)
  other arithmetic  2.12 us (2%)
    all_to_all x4, blocking collectives, spread(): return lax.all_to_all(copies, axis, 0, 0)  66.8 us
    all_to_all x1, blocking collectives, body(): terms = lax.all_to_all(copies, 'tm', 0, 0)  17.5 us
    all_to_all x1, blocking collectives, body(): mixed_rows = sum_quads(lax.all_to_all(parts, 'near', 0, 0))  7.32 us
    all_to_all x1, starting transfers between devices, body(): lax.all_to_all(parts, 'near', 0, 0)  6.46 us
    all_to_all x1, waiting for transfers between devices, body(): lax.all_to_all(parts, 'near', 0, 0)  4.06 us
    pallas_call x1, Pallas kernels, read_in(): pl.pallas_call(read_kernel, in_specs=[IN_HBM, IN_HBM], out_specs=IN_VMEM,...  3.92 us
    all_to_all x1, starting transfers between devices, spread(): return lax.all_to_all(copies, axis, 0, 0)  3.48 us
    all_to_all x1, waiting for transfers between devices, spread(): return lax.all_to_all(copies, axis, 0, 0)  2.52 us
  transfers between devices with their start and end apart: 2, of which 2 were waited for; matrix products, arithmetic and copies ran while one was open for 1% of the time, Pallas kernels for 2%

profile of v11, /device:TPU:1, one launch (start us, length us, event | category | flops | bytes accessed | tf_op | source)
XLA Modules:
  0.0 120.4 jit_solution(15953065071151459529)
XLA Ops:
  0.6 0.0 copy-start
  0.7 3.9 %read_in.1 = bf16[4,64,256]{2,1,0:T(8,128)(2,1)} custom-call(s32[4096,256]{1,0:T(8,128)} %counts_far.3, bf16[4096,256]{1,0:T(8,128)(2,1)} %weights.1), custom_call_target="tpu_custom_call" | custom-call | tf_op jit(solution)/shard_map/read_in/pallas_call | solution.py:62
  4.6 6.5 %all-to-all-start = ((bf16[4,64,256]{2,1,0:T(8,128)(2,1)}), bf16[4,64,256]{2,1,0:T(8,128)(2,1)S(1)}, u32[]{:S(2)}, u32[]{:S(2)}) async-start(bf16[4,64,256]{2,1,0:T(8,128)(2,1)} %read_in.1), calls=%async_computation | async-start | bytes 262144 | tf_op jit(solution)/shard_map/all_to_all | solution.py:188
  11.2 0.3 select_reduce_fusion
  11.6 0.1 select_reduce_fusion.3
  11.7 0.1 compare_convert_fusion
  11.8 4.1 %all-to-all-done = bf16[4,64,256]{2,1,0:T(8,128)(2,1)S(1)} async-done(((bf16[4,64,256]{2,1,0:T(8,128)(2,1)}), bf16[4,64,256]{2,1,0:T(8,128)(2,1)S(1)}, u32[]{:S(2)}, u32[]{:S(2)}) %all-to-all-start) | async-done | bytes 131104 | tf_op jit(solution)/shard_map/all_to_all | solution.py:188
  15.9 24.5 %all_to_all.40 = bf16[4,64,256]{2,1,0:T(8,128)(2,1)S(1)} all-to-all(bf16[4,64,256]{2,1,0:T(8,128)(2,1)S(1)} %broadcast_in_dim.101), channel_id=1, replica_groups=mesh['far'=4,'near'=4,'tm'=32] {'far'}, dimensions={0} | all-to-all | bytes 262144 | tf_op jit(solution)/shard_map/all_to_all | solution.py:31
  40.4 0.1 multiply_reduce_fusion.3
  40.5 0.1 multiply_convert_fusion.6.after
  40.6 8.0 %all_to_all.41 = bf16[4,64,256]{2,1,0:T(8,128)(2,1)S(1)} all-to-all(bf16[4,64,256]{2,1,0:T(8,128)(2,1)S(1)} %broadcast_in_dim.102), channel_id=1, replica_groups=mesh['far'=4,'near'=4,'tm'=32] {'near'}, dimensions={0} | all-to-all | bytes 262144 | tf_op jit(solution)/shard_map/all_to_all | solution.py:31
  48.6 0.0 copy-done.4
  48.6 0.2 multiply_reduce_fusion.2
  48.9 19.3 %all_to_all.42 = f32[32,3,128]{2,1,0:T(4,128)S(1)} all-to-all(f32[32,3,128]{2,1,0:T(4,128)S(1)} %broadcast_in_dim.103), channel_id=1, replica_groups=mesh['far'=4,'near'=4,'tm'=32] {'tm'}, dimensions={0} | all-to-all | bytes 98304 | tf_op jit(solution)/shard_map/all_to_all | solution.py:31
  68.2 0.2 multiply_reduce_fusion
  68.5 0.1 multiply_reduce_fusion.5
  68.5 0.1 multiply_reduce_fusion.4
  68.6 0.1 multiply_reduce_fusion.6
  68.8 0.4 fusion.5
  69.2 0.0 copy-start.1
  69.2 0.0 copy-done.5
  69.2 0.4 fusion
  69.6 7.3 %all_to_all.43 = bf16[4,64,256]{2,1,0:T(8,128)(2,1)S(1)} all-to-all(bf16[4,64,256]{2,1,0:T(8,128)(2,1)S(1)} %bitcast.53), channel_id=1, replica_groups=mesh['far'=4,'near'=4,'tm'=32] {'near'}, dimensions={0} | all-to-all | bytes 262144 | tf_op jit(solution)/shard_map/all_to_all | solution.py:237
  77.0 15.0 %all_to_all.44 = bf16[4,64,256]{2,1,0:T(8,128)(2,1)S(1)} all-to-all(bf16[4,64,256]{2,1,0:T(8,128)(2,1)S(1)} %broadcast_in_dim.104), channel_id=1, replica_groups=mesh['far'=4,'near'=4,'tm'=32] {'far'}, dimensions={0} | all-to-all | bytes 262144 | tf_op jit(solution)/shard_map/all_to_all | solution.py:31
  92.0 0.1 add_convert_fusion
  92.1 0.7 broadcast_in_dim.105
  92.7 3.5 %all-to-all-start.6 = ((bf16[4,64,256]{2,1,0:T(8,128)(2,1)}), bf16[4,64,256]{2,1,0:T(8,128)(2,1)S(1)}, u32[]{:S(2)}, u32[]{:S(2)}) async-start(bf16[4,64,256]{2,1,0:T(8,128)(2,1)} %broadcast_in_dim.105), calls=%async_computation.6 | async-start | bytes 262144 | tf_op jit(solution)/shard_map/all_to_all | solution.py:31
  96.2 2.2 %narrow.1.counts = s8[4096,256]{1,0:T(32,128)(4,1)S(1)} custom-call(s32[4096,256]{1,0:T(8,128)} %counts_far.3, bf16[64,256]{1,0:T(8,128)(2,1)S(1)} %multiply_convert_fusion.6.after), custom_call_target="tpu_custom_call" | custom-call | tf_op jit(solution)/shard_map/narrow/pallas_call | solution.py:92
  98.5 2.5 %all-to-all-done.6 = bf16[4,64,256]{2,1,0:T(8,128)(2,1)S(1)} async-done(((bf16[4,64,256]{2,1,0:T(8,128)(2,1)}), bf16[4,64,256]{2,1,0:T(8,128)(2,1)S(1)}, u32[]{:S(2)}, u32[]{:S(2)}) %all-to-all-start.6) | async-done | bytes 131104 | tf_op jit(solution)/shard_map/all_to_all | solution.py:31
  101.0 1.3 %likelihood.1 = (bf16[32,32,128]{2,1,0:T(8,128)(2,1)S(1)}, bf16[256,256]{1,0:T(8,128)(2,1)}) custom-call(bf16[256,256]{1,0:T(8,128)(2,1)S(1)} %bitcast.50, bf16[4096,256]{1,0:T(8,128)(2,1)S(1)} %copy-done.1, s8[4096,256]{1,0:T(32,128)(4,1)S(1)} %narrow.1.counts), custom_call_target="tpu_custom_call" | custom-call | tf_op jit(solution)/shard_map/likelihood/pallas_call | solution.py:126
  102.3 17.5 %all_to_all.45 = bf16[32,32,128]{2,1,0:T(8,128)(2,1)S(1)} all-to-all(bf16[32,32,128]{2,1,0:T(8,128)(2,1)S(1)} %get-tuple-element.51), channel_id=1, replica_groups=mesh['far'=4,'near'=4,'tm'=32] {'tm'}, dimensions={0} | all-to-all | bytes 524288 | tf_op jit(solution)/shard_map/all_to_all | solution.py:243
  119.8 0.6 multiply_bitcast_fusion
  (36 shorter events, 0.3 us)
Async XLA Ops:
  0.6 68.1 %copy-start = (bf16[128,256]{1,0:T(8,128)(2,1)S(1)}, bf16[128,256]{1,0:T(8,128)(2,1)}, u32[]{:S(2)}) copy-start(bf16[128,256]{1,0:T(8,128)(2,1)} %param.12) | copy-start | bytes 196612
  0.6 10.5 %copy-start.3 = (f32[128]{0:T(128)S(1)}, f32[128]{0:T(128)}, u32[]{:S(2)}) copy-start(f32[128]{0:T(128)} %param.10) | copy-start | bytes 1540
  0.7 10.6 %copy-start.2 = (f32[256]{0:T(256)S(1)}, f32[256]{0:T(256)}, u32[]{:S(2)}) copy-start(f32[256]{0:T(256)} %param.11) | copy-start | bytes 3076
  0.7 48.0 %copy-start.4 = (bf16[256,128]{1,0:T(8,128)(2,1)S(1)}, bf16[256,128]{1,0:T(8,128)(2,1)}, u32[]{:S(2)}) copy-start(bf16[256,128]{1,0:T(8,128)(2,1)} %param.9) | copy-start | bytes 196612
  0.7 68.5 %copy-start.5 = (bf16[128,256]{1,0:T(8,128)(2,1)S(1)}, bf16[128,256]{1,0:T(8,128)(2,1)}, u32[]{:S(2)}) copy-start(bf16[128,256]{1,0:T(8,128)(2,1)} %param.13) | copy-start | bytes 196612
  4.6 11.2 %all-to-all-start = ((bf16[4,64,256]{2,1,0:T(8,128)(2,1)}), bf16[4,64,256]{2,1,0:T(8,128)(2,1)S(1)}, u32[]{:S(2)}, u32[]{:S(2)}) async-start(bf16[4,64,256]{2,1,0:T(8,128)(2,1)} %read_in.1), calls=%async_computation | async-start | bytes 262144 | tf_op jit(solution)/shard_map/all_to_all | solution.py:188
  69.2 31.8 %copy-start.1 = (bf16[4096,256]{1,0:T(8,128)(2,1)S(1)}, bf16[4096,256]{1,0:T(8,128)(2,1)}, u32[]{:S(2)}) copy-start(bf16[4096,256]{1,0:T(8,128)(2,1)} %weights.1) | copy-start | bytes 6291460
  92.7 8.2 %all-to-all-start.6 = ((bf16[4,64,256]{2,1,0:T(8,128)(2,1)}), bf16[4,64,256]{2,1,0:T(8,128)(2,1)S(1)}, u32[]{:S(2)}, u32[]{:S(2)}) async-start(bf16[4,64,256]{2,1,0:T(8,128)(2,1)} %broadcast_in_dim.105), calls=%async_computation.6 | async-start | bytes 262144 | tf_op jit(solution)/shard_map/all_to_all | solution.py:31

commit v12 on v11

--- a/solution.py
+++ b/solution.py
@@ -67,7 +67,7 @@
         scratch_shapes=[
             pltpu.VMEM((neurons, bins), spikes.dtype),
             pltpu.VMEM((neurons, channels), BF16),
-            pltpu.SemaphoreType.DMA((2, 8)),
+            pltpu.SemaphoreType.DMA((2, 4)),
         ],
         compiler_params=pltpu.CompilerParams(vmem_limit_bytes=ROOM),
         name="read_in",

time: 121 us -> 121 us (level)
  transfers between devices with their start and end apart: 2 -> 2, of which waited for: 2 -> 2; matrix products, arithmetic and copies ran while one was open for 1% -> 0% of each run, Pallas kernels for 2% -> 2%
where the time goes in v12:
time: 121 us
  blocking collectives  91.5 us (76%)
  starting transfers between devices  9.93 us (8%)
  Pallas kernels  7.6 us (6%)
  waiting for transfers between devices  6.59 us (5%)
  other arithmetic  2.12 us (2%)
    all_to_all x4, blocking collectives, spread(): return lax.all_to_all(copies, axis, 0, 0)  66.8 us
    all_to_all x1, blocking collectives, body(): terms = lax.all_to_all(copies, 'tm', 0, 0)  17.4 us
    all_to_all x1, blocking collectives, body(): mixed_rows = sum_quads(lax.all_to_all(parts, 'near', 0, 0))  7.32 us
    all_to_all x1, starting transfers between devices, body(): lax.all_to_all(parts, 'near', 0, 0)  6.46 us
    pallas_call x1, Pallas kernels, read_in(): pl.pallas_call(read_kernel, in_specs=[IN_HBM, IN_HBM], out_specs=IN_VMEM,...  4.09 us
    all_to_all x1, waiting for transfers between devices, body(): lax.all_to_all(parts, 'near', 0, 0)  4.06 us
    all_to_all x1, starting transfers between devices, spread(): return lax.all_to_all(copies, axis, 0, 0)  3.47 us
    all_to_all x1, waiting for transfers between devices, spread(): return lax.all_to_all(copies, axis, 0, 0)  2.52 us
  transfers between devices with their start and end apart: 2, of which 2 were waited for; matrix products, arithmetic and copies ran while one was open for 0% of the time, Pallas kernels for 2%

profile of v12, /device:TPU:1, one launch (start us, length us, event | category | flops | bytes accessed | tf_op | source)
XLA Modules:
  0.0 120.6 jit_solution(11865935343241225547)
XLA Ops:
  0.6 0.0 copy-start
  0.6 0.0 copy-start.3
  0.7 0.0 copy-start.2
  0.7 4.1 %read_in.1 = bf16[4,64,256]{2,1,0:T(8,128)(2,1)} custom-call(s32[4096,256]{1,0:T(8,128)} %counts_far.3, bf16[4096,256]{1,0:T(8,128)(2,1)} %weights.1), custom_call_target="tpu_custom_call" | custom-call | tf_op jit(solution)/shard_map/read_in/pallas_call | solution.py:62
  4.8 6.5 %all-to-all-start = ((bf16[4,64,256]{2,1,0:T(8,128)(2,1)}), bf16[4,64,256]{2,1,0:T(8,128)(2,1)S(1)}, u32[]{:S(2)}, u32[]{:S(2)}) async-start(bf16[4,64,256]{2,1,0:T(8,128)(2,1)} %read_in.1), calls=%async_computation | async-start | bytes 262144 | tf_op jit(solution)/shard_map/all_to_all | solution.py:188
  11.4 0.3 select_reduce_fusion
  11.7 0.1 select_reduce_fusion.3
  11.9 0.1 compare_convert_fusion
  12.0 4.1 %all-to-all-done = bf16[4,64,256]{2,1,0:T(8,128)(2,1)S(1)} async-done(((bf16[4,64,256]{2,1,0:T(8,128)(2,1)}), bf16[4,64,256]{2,1,0:T(8,128)(2,1)S(1)}, u32[]{:S(2)}, u32[]{:S(2)}) %all-to-all-start) | async-done | bytes 131104 | tf_op jit(solution)/shard_map/all_to_all | solution.py:188
  16.1 24.5 %all_to_all.40 = bf16[4,64,256]{2,1,0:T(8,128)(2,1)S(1)} all-to-all(bf16[4,64,256]{2,1,0:T(8,128)(2,1)S(1)} %broadcast_in_dim.101), channel_id=1, replica_groups=mesh['far'=4,'near'=4,'tm'=32] {'far'}, dimensions={0} | all-to-all | bytes 262144 | tf_op jit(solution)/shard_map/all_to_all | solution.py:31
  40.6 0.1 multiply_reduce_fusion.3
  40.7 0.1 multiply_convert_fusion.6.after
  40.8 8.0 %all_to_all.41 = bf16[4,64,256]{2,1,0:T(8,128)(2,1)S(1)} all-to-all(bf16[4,64,256]{2,1,0:T(8,128)(2,1)S(1)} %broadcast_in_dim.102), channel_id=1, replica_groups=mesh['far'=4,'near'=4,'tm'=32] {'near'}, dimensions={0} | all-to-all | bytes 262144 | tf_op jit(solution)/shard_map/all_to_all | solution.py:31
  48.8 0.2 multiply_reduce_fusion.2
  49.1 19.3 %all_to_all.42 = f32[32,3,128]{2,1,0:T(4,128)S(1)} all-to-all(f32[32,3,128]{2,1,0:T(4,128)S(1)} %broadcast_in_dim.103), channel_id=1, replica_groups=mesh['far'=4,'near'=4,'tm'=32] {'tm'}, dimensions={0} | all-to-all | bytes 98304 | tf_op jit(solution)/shard_map/all_to_all | solution.py:31
  68.4 0.2 multiply_reduce_fusion
  68.6 0.1 multiply_reduce_fusion.5
  68.7 0.1 multiply_reduce_fusion.4
  68.8 0.1 multiply_reduce_fusion.6
  68.9 0.4 fusion.5
  69.4 0.0 copy-start.1
  69.4 0.4 fusion
  69.8 7.3 %all_to_all.43 = bf16[4,64,256]{2,1,0:T(8,128)(2,1)S(1)} all-to-all(bf16[4,64,256]{2,1,0:T(8,128)(2,1)S(1)} %bitcast.53), channel_id=1, replica_groups=mesh['far'=4,'near'=4,'tm'=32] {'near'}, dimensions={0} | all-to-all | bytes 262144 | tf_op jit(solution)/shard_map/all_to_all | solution.py:237
  77.2 15.0 %all_to_all.44 = bf16[4,64,256]{2,1,0:T(8,128)(2,1)S(1)} all-to-all(bf16[4,64,256]{2,1,0:T(8,128)(2,1)S(1)} %broadcast_in_dim.104), channel_id=1, replica_groups=mesh['far'=4,'near'=4,'tm'=32] {'far'}, dimensions={0} | all-to-all | bytes 262144 | tf_op jit(solution)/shard_map/all_to_all | solution.py:31
  92.2 0.1 add_convert_fusion
  92.3 0.7 broadcast_in_dim.105
  92.9 3.5 %all-to-all-start.6 = ((bf16[4,64,256]{2,1,0:T(8,128)(2,1)}), bf16[4,64,256]{2,1,0:T(8,128)(2,1)S(1)}, u32[]{:S(2)}, u32[]{:S(2)}) async-start(bf16[4,64,256]{2,1,0:T(8,128)(2,1)} %broadcast_in_dim.105), calls=%async_computation.6 | async-start | bytes 262144 | tf_op jit(solution)/shard_map/all_to_all | solution.py:31
  96.4 2.2 %narrow.1.counts = s8[4096,256]{1,0:T(32,128)(4,1)S(1)} custom-call(s32[4096,256]{1,0:T(8,128)} %counts_far.3, bf16[64,256]{1,0:T(8,128)(2,1)S(1)} %multiply_convert_fusion.6.after), custom_call_target="tpu_custom_call" | custom-call | tf_op jit(solution)/shard_map/narrow/pallas_call | solution.py:92
  98.7 2.5 %all-to-all-done.6 = bf16[4,64,256]{2,1,0:T(8,128)(2,1)S(1)} async-done(((bf16[4,64,256]{2,1,0:T(8,128)(2,1)}), bf16[4,64,256]{2,1,0:T(8,128)(2,1)S(1)}, u32[]{:S(2)}, u32[]{:S(2)}) %all-to-all-start.6) | async-done | bytes 131104 | tf_op jit(solution)/shard_map/all_to_all | solution.py:31
  101.2 1.3 %likelihood.1 = (bf16[32,32,128]{2,1,0:T(8,128)(2,1)S(1)}, bf16[256,256]{1,0:T(8,128)(2,1)}) custom-call(bf16[256,256]{1,0:T(8,128)(2,1)S(1)} %bitcast.50, bf16[4096,256]{1,0:T(8,128)(2,1)S(1)} %copy-done.1, s8[4096,256]{1,0:T(32,128)(4,1)S(1)} %narrow.1.counts), custom_call_target="tpu_custom_call" | custom-call | tf_op jit(solution)/shard_map/likelihood/pallas_call | solution.py:126
  102.4 17.4 %all_to_all.45 = bf16[32,32,128]{2,1,0:T(8,128)(2,1)S(1)} all-to-all(bf16[32,32,128]{2,1,0:T(8,128)(2,1)S(1)} %get-tuple-element.51), channel_id=1, replica_groups=mesh['far'=4,'near'=4,'tm'=32] {'tm'}, dimensions={0} | all-to-all | bytes 524288 | tf_op jit(solution)/shard_map/all_to_all | solution.py:243
  119.9 0.6 multiply_bitcast_fusion
  (36 shorter events, 0.3 us)
Async XLA Ops:
  0.6 68.3 %copy-start = (bf16[128,256]{1,0:T(8,128)(2,1)S(1)}, bf16[128,256]{1,0:T(8,128)(2,1)}, u32[]{:S(2)}) copy-start(bf16[128,256]{1,0:T(8,128)(2,1)} %param.12) | copy-start | bytes 196612
  0.6 10.7 %copy-start.3 = (f32[128]{0:T(128)S(1)}, f32[128]{0:T(128)}, u32[]{:S(2)}) copy-start(f32[128]{0:T(128)} %param.10) | copy-start | bytes 1540
  0.7 10.7 %copy-start.2 = (f32[256]{0:T(256)S(1)}, f32[256]{0:T(256)}, u32[]{:S(2)}) copy-start(f32[256]{0:T(256)} %param.11) | copy-start | bytes 3076
  0.7 48.2 %copy-start.4 = (bf16[256,128]{1,0:T(8,128)(2,1)S(1)}, bf16[256,128]{1,0:T(8,128)(2,1)}, u32[]{:S(2)}) copy-start(bf16[256,128]{1,0:T(8,128)(2,1)} %param.9) | copy-start | bytes 196612
  0.7 68.7 %copy-start.5 = (bf16[128,256]{1,0:T(8,128)(2,1)S(1)}, bf16[128,256]{1,0:T(8,128)(2,1)}, u32[]{:S(2)}) copy-start(bf16[128,256]{1,0:T(8,128)(2,1)} %param.13) | copy-start | bytes 196612
  4.8 11.2 %all-to-all-start = ((bf16[4,64,256]{2,1,0:T(8,128)(2,1)}), bf16[4,64,256]{2,1,0:T(8,128)(2,1)S(1)}, u32[]{:S(2)}, u32[]{:S(2)}) async-start(bf16[4,64,256]{2,1,0:T(8,128)(2,1)} %read_in.1), calls=%async_computation | async-start | bytes 262144 | tf_op jit(solution)/shard_map/all_to_all | solution.py:188
  69.4 31.8 %copy-start.1 = (bf16[4096,256]{1,0:T(8,128)(2,1)S(1)}, bf16[4096,256]{1,0:T(8,128)(2,1)}, u32[]{:S(2)}) copy-start(bf16[4096,256]{1,0:T(8,128)(2,1)} %weights.1) | copy-start | bytes 6291460
  92.9 8.2 %all-to-all-start.6 = ((bf16[4,64,256]{2,1,0:T(8,128)(2,1)}), bf16[4,64,256]{2,1,0:T(8,128)(2,1)S(1)}, u32[]{:S(2)}, u32[]{:S(2)}) async-start(bf16[4,64,256]{2,1,0:T(8,128)(2,1)} %broadcast_in_dim.105), calls=%async_computation.6 | async-start | bytes 262144 | tf_op jit(solution)/shard_map/all_to_all | solution.py:31
